TPU v7x, 32 devices: a whole 2x2x4 slice. The times are simulated.
32 devices in a mesh: gx: 8 (over z, y), gy: 4 (over x, core).
Axes of the slice: x: 2, y: 2, z: 4, core: 2. Of those that a mesh axis runs over, the one named last changes fastest.
Arguments:
- cot_u: float32 [30, 1024, 1024], P(None, 'gy', 'gx'), may hold values from -6 to 6
- cot_v: float32 [30, 1024, 1024], P(None, 'gy', 'gx'), may hold values from -6 to 6
- cot_t: float32 [30, 1024, 1024], P(None, 'gy', 'gx'), may hold values from -6 to 6
- levels: int32 [1024, 1024], P('gy', 'gx'), may hold values from 0 to 30
- mixing: float32 [1024, 1024], P('gy', 'gx'), may hold values from 0.02 to 0.12
- pattern_x: int32 [8, 3], replicated, may hold values from 0 to 7, all different within a row
- blocks_x: float32 [8, 3, 128, 128], replicated, may hold values from -0.3125 to 0.3125
- pattern_y: int32 [8, 3], replicated, may hold values from 0 to 7, all different within a row
- blocks_y: float32 [8, 3, 128, 128], replicated, may hold values from -0.3125 to 0.3125
Outputs:
- grad_u: float32 [30, 1024, 1024], P(None, 'gy', 'gx')
- grad_v: float32 [30, 1024, 1024], P(None, 'gy', 'gx')
- grad_t: float32 [30, 1024, 1024], P(None, 'gy', 'gx')
- forcing_update: float32 [3, 1024, 1024], P(None, 'gy', 'gx')
Inputs may be any that keep to these rules, and one draw needn't show every extreme that they name: `pattern_x`: each block row names 3 different block columns, and every block column is named by some row. `pattern_y`: each block row names 3 different block columns, and every block column is named by some row.
All inputs are finite; a program needn't handle non-finite values.
Results may differ from a plain program's by a relative error of at most 0.00007.
Values sent between devices are 32-bit elements; how exact they have to be, the bound alone decides.
No kernel may reach another device: no remote copies, remote signals or barrier semaphores. Data moves between devices by JAX's collectives and lax.ppermute only.
A program may use at most 384 MiB of HBM per device.

v0:
```python
import functools

import jax
import jax.numpy as jnp
from jax import lax
from jax.experimental import pallas as pl
from jax.experimental.pallas import tpu as pltpu
from jax.sharding import PartitionSpec as P

time_step = 0.5
gravity_scale = 0.05
coriolis_base = 0.4
zonal_slope = 0.3
north_slope = 0.2

LANES = 128
GROUP = 8
F32 = jnp.float32
BF16 = jnp.bfloat16
VMEM_LIMIT = 48 * 1024 * 1024


def whole():
    return pl.BlockSpec(memory_space=pltpu.VMEM)


def anywhere():
    return pl.BlockSpec(memory_space=pl.ANY)


def smem():
    return pl.BlockSpec(memory_space=pltpu.SMEM)


def struct(*shape):
    return jax.ShapeDtypeStruct(shape, F32)


def params(**kwargs):
    return pltpu.CompilerParams(vmem_limit_bytes=VMEM_LIMIT, **kwargs)


def cost(microseconds):
    return pl.CostEstimate(
        flops=int(microseconds * 1e6), bytes_accessed=int(microseconds * 3.0e6), transcendentals=0
    )


def lane_ids(shape):
    return lax.broadcasted_iota(jnp.int32, shape, 1)


def row_ids(shape):
    return lax.broadcasted_iota(jnp.int32, shape, 0)


def edge_kernel(levels_ref, col_ref, row_ref):
    rows, cols = levels_ref.shape
    field = levels_ref[...].astype(F32)
    col_ref[...] = jnp.transpose(field)[cols - GROUP :]
    row_ref[...] = field[rows - GROUP :]


def edges(levels):
    rows, cols = levels.shape
    return pl.pallas_call(
        edge_kernel,
        out_shape=(struct(GROUP, rows), struct(GROUP, cols)),
        in_specs=[whole()],
        out_specs=(whole(), whole()),
        compiler_params=params(),
        cost_estimate=cost(1.0),
        name="edges",
    )(levels)


def surface_kernel(
    levels_ref, col_ref, row_ref, u_ref, v_ref, t_ref, out_ref, wet_c_ref, wet_u_ref, wet_v_ref
):
    rows, cols = levels_ref.shape
    field = levels_ref[...].astype(F32)
    lane = lane_ids(field.shape)
    row = row_ids(field.shape)
    col = jnp.broadcast_to(jnp.transpose(col_ref[...])[:, GROUP - 1 :], field.shape)
    west = jnp.where(lane == 0, col, pltpu.roll(field, 1, 1))
    line = jnp.broadcast_to(row_ref[GROUP - 1 :, :], field.shape)
    south = jnp.where(row == 0, line, pltpu.roll(field, 1, 0))
    wet_u = jnp.minimum(field, west)
    wet_v = jnp.minimum(field, south)
    wet_c_ref[...] = field
    wet_u_ref[...] = wet_u
    wet_v_ref[...] = wet_v
    parts, chunk = (out_ref.shape[0], out_ref.shape[1] // 3)
    for comp, (ref, wet) in enumerate(((u_ref, wet_u), (v_ref, wet_v), (t_ref, field))):
        grad = jnp.where(wet > 0.0, time_step * ref[0], 0.0)
        for part in range(parts):
            out_ref[part, comp * chunk : (comp + 1) * chunk, :] = grad[
                part * chunk : (part + 1) * chunk
            ]


def surface(levels, col, row, cot_u, cot_v, cot_t, parts):
    rows, cols = levels.shape
    top = pl.BlockSpec((1, rows, cols), lambda i: (0, 0, 0))

    def full(*shape):
        return pl.BlockSpec(shape, lambda i: (0,) * len(shape))

    out = (parts, 3 * rows // parts, cols)
    return pl.pallas_call(
        surface_kernel,
        grid=(1,),
        out_shape=(struct(*out),) + (struct(rows, cols),) * 3,
        in_specs=[full(rows, cols), full(GROUP, rows), full(GROUP, cols), top, top, top],
        out_specs=(full(*out),) + (full(rows, cols),) * 3,
        compiler_params=params(),
        cost_estimate=cost(1.5),
        name="surface",
    )(levels, col, row, cot_u, cot_v, cot_t)


def rim_kernel(
    step,
    wet_c_ref,
    wet_u_ref,
    wet_v_ref,
    mix_ref,
    u_ref,
    v_ref,
    t_ref,
    east_ref,
    west_ref,
    north_ref,
    south_ref,
    corner_e_ref,
    corner_w_ref,
):
    at = pl.program_id(0)
    depth = pl.num_programs(0) * step
    rows, cols = mix_ref.shape
    slots = 3 * depth
    first = at * step
    chunk = 2 * GROUP
    lane = lane_ids((chunk, cols))

    @pl.when(at == 0)
    def _():
        mix = mix_ref[...]
        rolled = pltpu.roll(mix, slots + 1, 1)
        ids = lane_ids(mix.shape)
        east_ref[...] = jnp.where(ids == slots, rolled, 0.0)
        west_ref[...] = jnp.where(ids == slots + 1, rolled, 0.0)
        north_ref[slots:, :] = jnp.broadcast_to(
            mix[rows - 1 :], (north_ref.shape[0] - slots, cols)
        )
        south_ref[slots:, :] = jnp.broadcast_to(mix[:1], (south_ref.shape[0] - slots, cols))

    fields = ((u_ref, wet_u_ref), (v_ref, wet_v_ref), (t_ref, wet_c_ref))

    def body(i, carry):
        base = pl.multiple_of(i * chunk, chunk)
        here = pl.ds(base, chunk)
        east = east_ref[here, :]
        west = west_ref[here, :]
        wets = [wet[here, :] for _, wet in fields]
        for k in range(step):
            level = (first + k).astype(F32)
            for f, (ref, _) in enumerate(fields):
                slot = 3 * (first + k) + f
                value = jnp.where(level < wets[f], ref[k, here, :], 0.0)
                rolled = pltpu.roll(value, slot + 1, 1)
                east = jnp.where(lane == slot, rolled, east)
                west = jnp.where(lane == slot + 1, rolled, west)
        east_ref[here, :] = east
        west_ref[here, :] = west
        return carry

    lax.fori_loop(0, rows // chunk, body, 0)
    for k in range(step):
        level = (first + k).astype(F32)
        for f, (ref, wet) in enumerate(fields):
            slot = 3 * (first + k) + f
            for line, out in ((rows - 1, north_ref), (0, south_ref)):
                value = jnp.where(
                    level < wet[line : line + 1, :], ref[k, line : line + 1, :], 0.0
                )
                out[pl.ds(slot, 1), :] = value

    @pl.when(at == pl.num_programs(0) - 1)
    def _():
        corner_e_ref[...] = east_ref[:GROUP, :]
        corner_w_ref[...] = west_ref[rows - GROUP :, :]


def rims(wet_c, wet_u, wet_v, mixing, cot_u, cot_v, cot_t, after):
    depth, rows, cols = cot_u.shape
    step = 3
    lines = -(-(3 * depth + 1) // GROUP) * GROUP

    def full(*shape):
        return pl.BlockSpec(shape, lambda i: (0,) * len(shape))

    plane = full(rows, cols)
    block = pl.BlockSpec((step, rows, cols), lambda i: (i, 0, 0))

    def kernel(*refs):
        rim_kernel(step, *refs[:7], *refs[8:])

    return pl.pallas_call(
        kernel,
        grid=(depth // step,),
        out_shape=(struct(rows, cols),) * 2
        + (struct(lines, cols),) * 2
        + (struct(GROUP, cols),) * 2,
        in_specs=[plane] * 4 + [block] * 3 + [anywhere()],
        out_specs=(plane,) * 2 + (full(lines, cols),) * 2 + (full(GROUP, cols),) * 2,
        compiler_params=params(),
        cost_estimate=cost(5.0),
        name="rims",
    )(wet_c, wet_u, wet_v, mixing, cot_u, cot_v, cot_t, after)


def adjoint_kernel(
    step,
    depth,
    total_rows,
    wet_c_ref,
    wet_u_ref,
    wet_v_ref,
    mix_ref,
    hw_ref,
    he_ref,
    hn_ref,
    hs_ref,
    nw_ref,
    se_ref,
    u_ref,
    v_ref,
    t_ref,
    gu_ref,
    gv_ref,
    gt_ref,
    a_ref,
    b_ref,
    c_ref,
    mix_n_ref,
    mix_s_ref,
    keep_ref,
    cor_ref,
    pe_ref,
    pw_ref,
    sum_a_ref,
    sum_d_ref,
):
    rows, cols = mix_ref.shape
    at = pl.program_id(0)
    slots = 3 * depth
    first = depth - (at + 1) * step
    pad = GROUP
    half = 0.5 * time_step
    cor_step = coriolis_base * half * 0.5 / total_rows
    slope_u = 0.5 * time_step * zonal_slope
    slope_v = 0.5 * time_step * north_slope
    weight = time_step * gravity_scale

    @pl.when(at == 0)
    def _():
        shape = (rows, cols)
        lane = lane_ids(shape)
        row = row_ids(shape)
        start = lax.axis_index("gy") * rows
        lines = (row + start).astype(F32)
        cor = (0.25 * time_step * coriolis_base) * (0.5 + (lines + 0.5) / total_rows)
        cor_n = (0.25 * time_step * coriolis_base) * (0.5 + (lines + 1.5) / total_rows)
        cor_s = (0.25 * time_step * coriolis_base) * (0.5 + (lines - 0.5) / total_rows)
        cor_ref[...] = cor
        mix = mix_ref[...]
        keep_ref[...] = 1.0 - 4.0 * mix
        mix_n_ref[...] = jnp.where(
            row == rows - 1,
            jnp.broadcast_to(hn_ref[slots : slots + 1, :], shape),
            pltpu.roll(mix, rows - 1, 0),
        )
        mix_s_ref[...] = jnp.where(
            row == 0,
            jnp.broadcast_to(hs_ref[slots : slots + 1, :], shape),
            pltpu.roll(mix, 1, 0),
        )
        east = he_ref[...]
        kind = lax.rem(lane + 2, 3)
        mixed = east * jnp.broadcast_to(east[:, slots + 1 : slots + 2], shape)
        below = jnp.where(
            row == 0,
            jnp.broadcast_to(se_ref[GROUP - 1 :, :], shape),
            pltpu.roll(east, 1, 0),
        )
        turned = cor * east + cor_s * below
        total = jnp.where((kind == 0) & (lane <= slots), east, 0.0)
        reach = 3
        while reach < slots:
            moved = pltpu.roll(total, cols - reach, 1)
            total = total + jnp.where(lane + reach < cols, moved, 0.0)
            reach *= 2
        pe_ref[...] = (
            mixed
            + jnp.where(kind == 1, pltpu.roll(turned, 1, 1), 0.0)
            + jnp.where(kind == 2, pltpu.roll(weight * total, 2, 1), 0.0)
        )
        west = hw_ref[...]
        kind = lax.rem(lane, 3)
        mixed = west * jnp.broadcast_to(west[:, slots : slots + 1], shape)
        above = jnp.where(
            row == rows - 1,
            jnp.broadcast_to(nw_ref[:1, :], shape),
            pltpu.roll(west, rows - 1, 0),
        )
        turned = cor * west + cor_n * above
        pw_ref[...] = mixed - jnp.where(
            kind == 0,
            pltpu.roll(turned, cols - 1, 1) + pltpu.roll(slope_u * west, cols - 2, 1),
            0.0,
        )
        sum_a_ref[...] = jnp.zeros(shape, F32)
        sum_d_ref[...] = jnp.zeros(shape, F32)

    fields = (
        (u_ref, wet_u_ref, a_ref),
        (v_ref, wet_v_ref, b_ref),
        (t_ref, wet_c_ref, c_ref),
    )

    def mask(i, carry):
        base = pl.multiple_of(i * 2 * GROUP, 2 * GROUP)
        here = pl.ds(base, 2 * GROUP)
        there = pl.ds(pl.multiple_of(base + pad, GROUP), 2 * GROUP)
        wets = [wet[here, :] for _, wet, _ in fields]
        for k in range(step):
            level = (first + k).astype(F32)
            for f, (ref, _, out) in enumerate(fields):
                out[k, there, :] = jnp.where(level < wets[f], ref[k, here, :], 0.0)
        return carry

    lax.fori_loop(0, rows // (2 * GROUP), mask, 0)
    for k in range(step):
        for f, (_, _, out) in enumerate(fields):
            slot = 3 * (first + k) + f
            out[k, pad - 1 : pad, :] = hs_ref[pl.ds(slot, 1), :]
            out[k, pad + rows : pad + rows + 1, :] = hn_ref[pl.ds(slot, 1), :]

    chunk = 2 * GROUP
    lane = lane_ids((chunk, cols))
    is_east = lane == cols - 1
    is_west = lane == 0

    def body(i, carry):
        base = pl.multiple_of(i * chunk, chunk)
        here = pl.ds(base, chunk)
        center = pl.ds(base + pad, chunk)
        north = pl.ds(base + pad + 1, chunk)
        south = pl.ds(base + pad - 1, chunk)
        mix = mix_ref[here, :]
        mix_n = mix_n_ref[here, :]
        mix_s = mix_s_ref[here, :]
        keep = keep_ref[here, :]
        cor = cor_ref[here, :]
        cor_n = cor + cor_step
        cor_s = cor - cor_step
        pe = pe_ref[here, :]
        pw = pw_ref[here, :]
        sum_a = sum_a_ref[here, :]
        sum_d = sum_d_ref[here, :]
        for k in reversed(range(step)):
            slot = 3 * (first + k)

            def from_east(value, f, slot=slot):
                edge = pltpu.roll(pe, cols - 2 - (slot + f), 1)
                return jnp.where(is_east, edge, pltpu.roll(value, cols - 1, 1))

            def from_west(value, f, slot=slot):
                edge = pltpu.roll(pw, cols - (slot + f), 1)
                return jnp.where(is_west, edge, pltpu.roll(value, 1, 1))

            a = a_ref[k, center, :]
            a_n = a_ref[k, north, :]
            a_s = a_ref[k, south, :]
            b = b_ref[k, center, :]
            b_n = b_ref[k, north, :]
            b_s = b_ref[k, south, :]
            c = c_ref[k, center, :]
            c_n = c_ref[k, north, :]
            c_s = c_ref[k, south, :]
            mix_a = mix * a
            turn_b = cor * b + cor_n * b_n + slope_u * c
            gu_ref[k, here, :] = (
                keep * a
                + (mix_n * a_n + mix_s * a_s)
                - turn_b
                + (from_west(mix_a - turn_b, 0) + from_east(mix_a, 0))
            )
            mix_b = mix * b
            turn_a = cor * a + cor_s * a_s
            gv_ref[k, here, :] = (
                keep * b
                + (mix_n * b_n + mix_s * b_s)
                + (turn_a - slope_v * (c + c_s))
                + (from_west(mix_b, 1) + from_east(mix_b + turn_a, 1))
            )
            mix_c = mix * c
            sum_a = sum_a + weight * a
            sum_d = sum_d + weight * (b - b_n)
            gt_ref[k, here, :] = (
                keep * c
                + (mix_n * c_n + mix_s * c_s)
                - (sum_a + sum_d)
                + (from_west(mix_c, 2) + from_east(mix_c + sum_a, 2))
            )
        sum_a_ref[here, :] = sum_a
        sum_d_ref[here, :] = sum_d
        return carry

    lax.fori_loop(0, rows // chunk, body, 0)


def adjoint(planes, halos, cots, after, total_rows):
    depth, rows, cols = cots[0].shape
    step = 3
    steps = depth // step

    def full(*shape):
        return pl.BlockSpec(shape, lambda i: (0,) * len(shape))

    plane = full(rows, cols)
    block = pl.BlockSpec((step, rows, cols), lambda i: (steps - 1 - i, 0, 0))
    n_in = len(planes) + len(halos) + 3

    def kernel(*refs):
        adjoint_kernel(step, depth, total_rows, *refs[:n_in], *refs[n_in + 1 :])

    padded = pltpu.VMEM((step, rows + 2 * GROUP, cols), F32)
    return pl.pallas_call(
        kernel,
        grid=(steps,),
        out_shape=(struct(depth, rows, cols),) * 3,
        in_specs=[plane] * len(planes)
        + [full(*halo.shape) for halo in halos]
        + [block] * 3
        + [anywhere()],
        out_specs=(block,) * 3,
        scratch_shapes=[padded] * 3 + [pltpu.VMEM((rows, cols), F32)] * 8,
        compiler_params=params(),
        cost_estimate=cost(12.0),
        name="adjoint",
    )(*planes, *halos, *cots, after)


def halves(value):
    high = value.astype(BF16)
    return high, (value - high.astype(F32)).astype(BF16)


def zonal_kernel(
    gy_size, pattern_ref, blocks_ref, field_ref, out_ref, high_ref, low_ref
):
    tiles, height, cols = field_ref.shape
    chunk = height // 3
    width = cols // gy_size
    slots = LANES // width
    groups = chunk // GROUP
    owner = lane_ids((GROUP, cols)) // width
    for tile in range(tiles):
        high_ref[tile], low_ref[tile] = halves(field_ref[tile])
    for r in range(blocks_ref.shape[0]):
        picked = [pattern_ref[r, j] for j in range(blocks_ref.shape[1])]
        high = [high_ref[p] for p in picked]
        low = [low_ref[p] for p in picked]
        block = [halves(blocks_ref[r, j]) for j in range(blocks_ref.shape[1])]
        left = jnp.concatenate(high + high + low, axis=1)
        right = jnp.concatenate(
            [h for h, _ in block] + [l for _, l in block] + [h for h, _ in block], axis=1
        )
        result = lax.dot_general(
            left, right, (((1,), (1,)), ((), ())), preferred_element_type=F32
        )
        for y in range(gy_size):
            for v in range(out_ref.shape[1] // GROUP):
                packed = jnp.zeros((GROUP, cols), F32)
                for s in range(min(slots, 3 * groups - v * slots)):
                    q = v * slots + s
                    piece = result[q * GROUP : (q + 1) * GROUP]
                    if s != y:
                        piece = pltpu.roll(piece, ((s - y) * width) % cols, 1)
                    packed = jnp.where(owner == s, piece, packed)
                out_ref[y * tiles + r, v * GROUP : (v + 1) * GROUP, :] = packed


def zonal(pattern, blocks, field, gy_size, after):
    tiles, height, cols = field.shape
    width = cols // gy_size
    slots = LANES // width
    lines = -(-(height // GROUP) // slots) * GROUP

    def kernel(pattern_ref, blocks_ref, field_ref, after_ref, *refs):
        zonal_kernel(gy_size, pattern_ref, blocks_ref, field_ref, *refs)

    return pl.pallas_call(
        kernel,
        out_shape=struct(gy_size * tiles, lines, cols),
        in_specs=[smem(), whole(), whole(), anywhere()],
        out_specs=whole(),
        scratch_shapes=[pltpu.VMEM((tiles, height, cols), BF16)] * 2,
        compiler_params=params(),
        cost_estimate=cost(2.0),
        name="zonal",
    )(pattern, blocks, field, after)


def meridional_kernel(
    gx_size, gy_size, pattern_ref, blocks_ref, field_ref, out_ref, high_ref, low_ref
):
    devices, lines, cols = field_ref.shape
    tiles, block, _ = high_ref.shape
    rows = tiles * block // gy_size
    chunk = rows // gx_size
    width = cols // gy_size
    slots = LANES // width
    groups = chunk // GROUP
    owner = lane_ids((GROUP, cols)) // width
    for d in range(devices):
        pieces = []
        for g in range(groups):
            packed = jnp.zeros((GROUP, cols), F32)
            for c in range(3):
                q = c * groups + g
                v, s = divmod(q, slots)
                piece = field_ref[d, v * GROUP : (v + 1) * GROUP, :]
                if s != c:
                    piece = pltpu.roll(piece, ((c - s) * width) % cols, 1)
                packed = jnp.where(owner == c, piece, packed)
            pieces.append(packed)
        tile, line = divmod(d * chunk, block)
        high, low = halves(jnp.concatenate(pieces, axis=0))
        high_ref[tile, line : line + chunk, :] = high
        low_ref[tile, line : line + chunk, :] = low
    for r in range(blocks_ref.shape[0]):
        picked = [pattern_ref[r, j] for j in range(blocks_ref.shape[1])]
        high = [high_ref[p] for p in picked]
        low = [low_ref[p] for p in picked]
        parts = [halves(blocks_ref[r, j]) for j in range(blocks_ref.shape[1])]
        left = jnp.concatenate(
            [h for h, _ in parts] + [l for _, l in parts] + [h for h, _ in parts], axis=1
        )
        right = jnp.concatenate(high + high + low, axis=0)
        result = jnp.dot(left, right, preferred_element_type=F32)
        dest, line = divmod(r * block, rows)
        first = line // GROUP
        for c in range(3):
            for v in range(block // GROUP // slots):
                packed = jnp.zeros((GROUP, cols), F32)
                for s in range(slots):
                    g = v * slots + s
                    piece = result[g * GROUP : (g + 1) * GROUP]
                    if s != c:
                        piece = pltpu.roll(piece, ((s - c) * width) % cols, 1)
                    packed = jnp.where(owner == s, piece, packed)
                at = (c * (rows // GROUP) + first) // slots + v
                out_ref[dest, at * GROUP : (at + 1) * GROUP, :] = packed


def meridional(pattern, blocks, field, gx_size, gy_size, after):
    devices, lines, cols = field.shape
    tiles, _, block, _ = blocks.shape
    rows = tiles * block // gy_size
    slots = LANES // (cols // gy_size)

    def kernel(pattern_ref, blocks_ref, field_ref, after_ref, *refs):
        meridional_kernel(gx_size, gy_size, pattern_ref, blocks_ref, field_ref, *refs)

    return pl.pallas_call(
        kernel,
        out_shape=struct(gy_size, 3 * rows // slots, cols),
        in_specs=[smem(), whole(), whole(), anywhere()],
        out_specs=whole(),
        scratch_shapes=[pltpu.VMEM((tiles, block, cols), BF16)] * 2,
        compiler_params=params(),
        cost_estimate=cost(2.0),
        name="meridional",
    )(pattern, blocks, field, after)


def finish_kernel(field_ref, out_ref):
    sources, _, cols = field_ref.shape
    _, rows, _ = out_ref.shape
    width = cols // sources
    slots = LANES // width
    owner = lane_ids((GROUP, cols)) // width
    for c in range(3):
        for g in range(rows // GROUP):
            v, s = divmod(c * (rows // GROUP) + g, slots)
            packed = jnp.zeros((GROUP, cols), F32)
            for y in range(sources):
                piece = field_ref[y, v * GROUP : (v + 1) * GROUP, :]
                if s != y:
                    piece = pltpu.roll(piece, ((y - s) * width) % cols, 1)
                packed = jnp.where(owner == y, piece, packed)
            out_ref[c, g * GROUP : (g + 1) * GROUP, :] = packed


def finish(field, rows):
    sources, _, cols = field.shape
    return pl.pallas_call(
        finish_kernel,
        out_shape=struct(3, rows, cols),
        in_specs=[whole()],
        out_specs=whole(),
        compiler_params=params(),
        cost_estimate=cost(1.0),
        name="finish",
    )(field)


def shards(cot_u, cot_v, cot_t, levels, mixing, pattern_x, blocks_x, pattern_y, blocks_y):
    depth, rows, cols = cot_u.shape
    nx, ny = (lax.axis_size("gx"), lax.axis_size("gy"))
    up_x = [(i, i + 1) for i in range(nx - 1)]
    down_x = [(j, i) for i, j in up_x]
    up_y = [(i, i + 1) for i in range(ny - 1)]
    down_y = [(j, i) for i, j in up_y]
    place = lambda y, x: x * ny + y
    to_se = [(place(j, i), place(j - 1, i + 1)) for j in range(1, ny) for i in range(nx - 1)]
    to_nw = [(j, i) for i, j in to_se]

    level_col, level_row = edges(levels)
    level_col = lax.ppermute(level_col, "gx", up_x)
    level_row = lax.ppermute(level_row, "gy", up_y)
    field, wet_c, wet_u, wet_v = surface(
        levels, level_col, level_row, cot_u, cot_v, cot_t, nx
    )
    cots = (cot_u, cot_v, cot_t)
    lines = lax.all_to_all(field, "gx", 0, 0)

    east, west, north, south, corner_e, corner_w = rims(
        wet_c, wet_u, wet_v, mixing, *cots, field
    )
    halo_w = lax.ppermute(east, "gx", up_x)
    halo_e = lax.ppermute(west, "gx", down_x)
    halo_s = lax.ppermute(north, "gy", up_y)
    halo_n = lax.ppermute(south, "gy", down_y)
    halo_nw = lax.ppermute(corner_e, ("gx", "gy"), to_se)
    halo_se = lax.ppermute(corner_w, ("gx", "gy"), to_nw)

    packed = zonal(pattern_x, blocks_x, lines, ny, corner_e)
    columns = lax.all_to_all(packed, ("gy", "gx"), 0, 0)
    grads = adjoint(
        (wet_c, wet_u, wet_v, mixing),
        (halo_w, halo_e, halo_n, halo_s, halo_nw, halo_se),
        cots,
        packed,
        rows * ny,
    )
    sent = meridional(pattern_y, blocks_y, columns, nx, ny, grads[0])
    mixed = finish(lax.all_to_all(sent, "gy", 0, 0), rows)
    return (*grads, mixed)


def solution(mesh):
    grid = P(None, "gy", "gx")
    flat = P("gy", "gx")
    return jax.shard_map(
        shards,
        mesh=mesh,
        in_specs=(grid, grid, grid, flat, flat, P(), P(), P(), P()),
        out_specs=(grid, grid, grid, grid),
        check_vma=False,
    )
```

profile of v0, /device:TPU:0, one launch (start us, length us, event | category | flops | bytes accessed | tf_op | source)
XLA Modules:
  0.0 112.8 jit_solution(10692579452107520330)
XLA Ops:
  0.6 0.0 copy-start.6
  0.6 0.9 copy-done.6
  1.5 0.1 edges.1
  1.6 4.9 %collective-permute-start = (f32[8,256]{1,0:T(8,128)S(1)}, f32[8,256]{1,0:T(8,128)S(1)}, u32[]{:S(2)}, u32[]{:S(2)}) collective-permute-start(f32[8,256]{1,0:T(8,128)S(1)} %get-tuple-element.19), channel_id=1, source_target_pairs={{0,4},{4,8},{8,12},{12,16},{16,20},{20,24},{24,28},{1,5},{5,9},{9,... | collective-permute-start | bytes 24584 | tf_op jit(solution)/shard_map/ppermute | solution.py:633
  6.5 1.5 %collective-permute-start.1 = (f32[8,128]{1,0:T(8,128)S(1)}, f32[8,128]{1,0:T(8,128)S(1)}, u32[]{:S(2)}, u32[]{:S(2)}) collective-permute-start(f32[8,128]{1,0:T(8,128)S(1)} %get-tuple-element.20), channel_id=1, source_target_pairs={{0,1},{1,2},{2,3},{4,5},{5,6},{6,7},{8,9},{9,10},{10,11},{12,13},{... | collective-permute-start | bytes 12296 | tf_op jit(solution)/shard_map/ppermute | solution.py:634
  8.0 0.8 collective-permute-done.1.row_ref
  8.8 0.0 collective-permute-done.col_ref
  8.8 0.0 copy-start
  8.8 2.1 %copy-done = f32[30,256,128]{2,1,0:T(8,128)S(1)} copy-done((f32[30,256,128]{2,1,0:T(8,128)S(1)}, f32[30,256,128]{2,1,0:T(8,128)}, u32[]{:S(2)}) %copy-start) | copy-done | bytes 3932184
  10.9 0.0 copy-start.7
  10.9 0.0 copy-start.5
  10.9 2.1 %surface.1 = (f32[8,96,128]{2,1,0:T(8,128)}, f32[256,128]{1,0:T(8,128)S(1)}, f32[256,128]{1,0:T(8,128)S(1)}, f32[256,128]{1,0:T(8,128)S(1)}) custom-call(s32[256,128]{1,0:T(8,128)S(1)} %copy-done.6, f32[8,256]{1,0:T(8,128)S(1)} %collective-permute-done.col_ref, f32[8,128]{1,0:T(8,128)S(1)} %collective-permute-done.1.row_ref, f32[30,256,128]{2,1,0:T(8,128)S(1)} %copy-done, ...), custom_call_target="tpu_custom_call" | custom-call | flops 1500000 | bytes 4500000 | tf_op jit(solution)/shard_map/surface/pallas_call | solution.py:110
  13.0 5.7 %all-to-all-start = ((f32[8,96,128]{2,1,0:T(8,128)}), f32[8,96,128]{2,1,0:T(8,128)S(1)}, u32[]{:S(2)}, u32[]{:S(2)}) async-start(f32[8,96,128]{2,1,0:T(8,128)} %get-tuple-element.24.refs_7_), calls=%async_computation | async-start | bytes 786432 | tf_op jit(solution)/shard_map/all_to_all | solution.py:639
  18.6 0.0 copy-done.7
  18.6 0.1 copy.13.pattern_ref
  18.7 0.0 copy-done.5
  18.7 0.0 copy-start.1
  18.7 2.1 %copy-done.1 = f32[30,256,128]{2,1,0:T(8,128)S(1)} copy-done((f32[30,256,128]{2,1,0:T(8,128)S(1)}, f32[30,256,128]{2,1,0:T(8,128)}, u32[]{:S(2)}) %copy-start.1) | copy-done | bytes 3932184
  20.8 0.0 copy-start.3
  20.8 0.0 copy-start.8
  20.8 16.2 %rims.1 = (f32[256,128]{1,0:T(8,128)S(1)}, f32[256,128]{1,0:T(8,128)S(1)}, f32[96,128]{1,0:T(8,128)S(1)}, f32[96,128]{1,0:T(8,128)S(1)}, f32[8,128]{1,0:T(8,128)S(1)}, /*index=5*/f32[8,128]{1,0:T(8,128)S(1)}) custom-call(f32[256,128]{1,0:T(8,128)S(1)} %get-tuple-element.21.refs_0_, f32[256,128]{1,0:T(8,128)S(1)} %get-tuple-element.22.refs_1_, ...), custom_call_target="tpu_custom_call" | custom-call | flops 5000000 | bytes 15000000 | tf_op jit(solution)/shard_map/rims/pallas_call | solution.py:209
  37.0 0.0 all-to-all-done.field_ref
  37.1 0.0 copy-done.3
  37.1 2.3 %zonal.1.refs_13_ = f32[32,24,128]{2,1,0:T(8,128)} custom-call(s32[8,3]{1,0:T(8,128)S(1)} %copy.13.pattern_ref, f32[8,3,128,128]{3,2,1,0:T(8,128)S(1)} %copy-done.3, f32[8,96,128]{2,1,0:T(8,128)S(1)} %all-to-all-done.field_ref, f32[8,128]{1,0:T(8,128)S(1)} %get-tuple-element.29.after_ref), custom_call_target="tpu_custom_call" | custom-call | flops 2000000 | bytes 6000000 | tf_op jit(solution)/shard_map/zonal/pallas_call | solution.py:505
  39.4 7.9 %all-to-all-start.1 = ((f32[32,24,128]{2,1,0:T(8,128)}), f32[32,24,128]{2,1,0:T(8,128)S(1)}, u32[]{:S(2)}, u32[]{:S(2)}) async-start(f32[32,24,128]{2,1,0:T(8,128)} %zonal.1.refs_13_), calls=%async_computation.1 | async-start | bytes 786432 | tf_op jit(solution)/shard_map/all_to_all | solution.py:652
  47.2 3.7 %collective-permute-start.2 = (f32[256,128]{1,0:T(8,128)S(1)}, f32[256,128]{1,0:T(8,128)S(1)}, u32[]{:S(2)}, u32[]{:S(2)}) collective-permute-start(f32[256,128]{1,0:T(8,128)S(1)} %get-tuple-element.25), channel_id=1, source_target_pairs={{0,4},{4,8},{8,12},{12,16},{16,20},{20,24},{24,28},{1,5},{5,9},{9,... | collective-permute-start | bytes 393224 | tf_op jit(solution)/shard_map/ppermute | solution.py:644
  50.9 1.3 %collective-permute-start.3 = (f32[256,128]{1,0:T(8,128)S(1)}, f32[256,128]{1,0:T(8,128)S(1)}, u32[]{:S(2)}, u32[]{:S(2)}) collective-permute-start(f32[256,128]{1,0:T(8,128)S(1)} %get-tuple-element.26), channel_id=1, source_target_pairs={{4,0},{8,4},{12,8},{16,12},{20,16},{24,20},{28,24},{5,1},{9,5},{13... | collective-permute-start | bytes 393224 | tf_op jit(solution)/shard_map/ppermute | solution.py:645
  52.2 1.3 %collective-permute-start.4 = (f32[96,128]{1,0:T(8,128)S(1)}, f32[96,128]{1,0:T(8,128)S(1)}, u32[]{:S(2)}, u32[]{:S(2)}) collective-permute-start(f32[96,128]{1,0:T(8,128)S(1)} %get-tuple-element.27), channel_id=1, source_target_pairs={{1,0},{2,1},{3,2},{5,4},{6,5},{7,6},{9,8},{10,9},{11,10},{13,12},{... | collective-permute-start | bytes 147464 | tf_op jit(solution)/shard_map/ppermute | solution.py:647
  53.5 3.0 %collective-permute-start.5 = (f32[96,128]{1,0:T(8,128)S(1)}, f32[96,128]{1,0:T(8,128)S(1)}, u32[]{:S(2)}, u32[]{:S(2)}) collective-permute-start(f32[96,128]{1,0:T(8,128)S(1)} %get-tuple-element.28), channel_id=1, source_target_pairs={{0,1},{1,2},{2,3},{4,5},{5,6},{6,7},{8,9},{9,10},{10,11},{12,13},{... | collective-permute-start | bytes 147464 | tf_op jit(solution)/shard_map/ppermute | solution.py:646
  56.6 0.7 collective-permute-start.6
  57.2 0.0 collective-permute-done.6.refs_8_
  57.3 0.7 collective-permute-start.7
  57.9 0.0 copy-done.8
  57.9 0.1 copy.14.pattern_ref
  58.0 0.0 collective-permute-done.7.refs_9_
  58.0 0.0 collective-permute-done.4.refs_6_
  58.0 0.0 collective-permute-done.5.refs_7_
  58.0 0.0 collective-permute-done.2.refs_4_
  58.0 0.8 collective-permute-done.3.refs_5_
  58.8 0.0 copy-start.2
  58.8 2.1 %copy-done.2 = f32[30,256,128]{2,1,0:T(8,128)S(1)} copy-done((f32[30,256,128]{2,1,0:T(8,128)S(1)}, f32[30,256,128]{2,1,0:T(8,128)}, u32[]{:S(2)}) %copy-start.2) | copy-done | bytes 3932184
  60.9 0.0 copy-start.4
  60.9 28.7 %adjoint.1 = (f32[30,256,128]{2,1,0:T(8,128)}, f32[30,256,128]{2,1,0:T(8,128)}, f32[30,256,128]{2,1,0:T(8,128)}) custom-call(f32[256,128]{1,0:T(8,128)S(1)} %get-tuple-element.21.refs_0_, f32[256,128]{1,0:T(8,128)S(1)} %get-tuple-element.22.refs_1_, f32[256,128]{1,0:T(8,128)S(1)} %get-tuple-element.23.refs_2_, f32[256,128]{1,0:T(8,128)S(1)} %copy-done.5, ...), custom_call_target="tpu_custom_call" | custom-call | flops 12000000 | bytes 36000000 | tf_op jit(solution)/shard_map/adjoint/pallas_call | solution.py:440
  89.6 0.0 all-to-all-done.1.field_ref
  89.7 0.0 copy-done.4
  89.7 1.8 %meridional.1 = f32[4,192,128]{2,1,0:T(8,128)S(1)} custom-call(s32[8,3]{1,0:T(8,128)S(1)} %copy.14.pattern_ref, f32[8,3,128,128]{3,2,1,0:T(8,128)S(1)} %copy-done.4, f32[32,24,128]{2,1,0:T(8,128)S(1)} %all-to-all-done.1.field_ref, f32[30,256,128]{2,1,0:T(8,128)} %get-tuple-element.15.after_ref), custom_call_target="tpu_custom_call" | custom-call | flops 2000000 | bytes 6000000 | tf_op jit(solution)/shard_map/meridional/pallas_call | solution.py:578
  91.5 20.1 %all_to_all.15.field_ref = f32[4,192,128]{2,1,0:T(8,128)S(1)} all-to-all(f32[4,192,128]{2,1,0:T(8,128)S(1)} %meridional.1), channel_id=1, replica_groups=mesh['gx'=8,'gy'=4] {'gy'}, dimensions={0} | all-to-all | bytes 786432 | tf_op jit(solution)/shard_map/all_to_all | solution.py:661
  111.6 1.1 finish.1
Async XLA Ops:
  0.6 0.9 copy-start.6
  1.6 7.2 %collective-permute-start = (f32[8,256]{1,0:T(8,128)S(1)}, f32[8,256]{1,0:T(8,128)S(1)}, u32[]{:S(2)}, u32[]{:S(2)}) collective-permute-start(f32[8,256]{1,0:T(8,128)S(1)} %get-tuple-element.19), channel_id=1, source_target_pairs={{0,4},{4,8},{8,12},{12,16},{16,20},{20,24},{24,28},{1,5},{5,9},{9,... | collective-permute-start | bytes 24584 | tf_op jit(solution)/shard_map/ppermute | solution.py:633
  6.5 2.3 %collective-permute-start.1 = (f32[8,128]{1,0:T(8,128)S(1)}, f32[8,128]{1,0:T(8,128)S(1)}, u32[]{:S(2)}, u32[]{:S(2)}) collective-permute-start(f32[8,128]{1,0:T(8,128)S(1)} %get-tuple-element.20), channel_id=1, source_target_pairs={{0,1},{1,2},{2,3},{4,5},{5,6},{6,7},{8,9},{9,10},{10,11},{12,13},{... | collective-permute-start | bytes 12296 | tf_op jit(solution)/shard_map/ppermute | solution.py:634
  8.8 2.1 %copy-start = (f32[30,256,128]{2,1,0:T(8,128)S(1)}, f32[30,256,128]{2,1,0:T(8,128)}, u32[]{:S(2)}) copy-start(f32[30,256,128]{2,1,0:T(8,128)} %refs_10_.1) | copy-start | bytes 11796484
  10.9 7.7 %copy-start.7 = (s32[8,3]{0,1:T(4,128)S(1)}, s32[8,3]{0,1:T(4,128)}, u32[]{:S(2)}) copy-start(s32[8,3]{0,1:T(4,128)} %param.14) | copy-start | bytes 292
  10.9 7.8 %copy-start.5 = (f32[256,128]{1,0:T(8,128)S(1)}, f32[256,128]{1,0:T(8,128)}, u32[]{:S(2)}) copy-start(f32[256,128]{1,0:T(8,128)} %refs_3_.3) | copy-start | bytes 393220
  13.0 24.1 %all-to-all-start = ((f32[8,96,128]{2,1,0:T(8,128)}), f32[8,96,128]{2,1,0:T(8,128)S(1)}, u32[]{:S(2)}, u32[]{:S(2)}) async-start(f32[8,96,128]{2,1,0:T(8,128)} %get-tuple-element.24.refs_7_), calls=%async_computation | async-start | bytes 786432 | tf_op jit(solution)/shard_map/all_to_all | solution.py:639
  18.7 2.1 %copy-start.1 = (f32[30,256,128]{2,1,0:T(8,128)S(1)}, f32[30,256,128]{2,1,0:T(8,128)}, u32[]{:S(2)}) copy-start(f32[30,256,128]{2,1,0:T(8,128)} %refs_10_.1) | copy-start | bytes 11796484
  20.8 16.2 %copy-start.3 = (f32[8,3,128,128]{3,2,1,0:T(8,128)S(1)}, f32[8,3,128,128]{3,2,1,0:T(8,128)}, u32[]{:S(2)}) copy-start(f32[8,3,128,128]{3,2,1,0:T(8,128)} %blocks_ref.2) | copy-start | bytes 4718596
  20.8 37.1 %copy-start.8 = (s32[8,3]{0,1:T(4,128)S(1)}, s32[8,3]{0,1:T(4,128)}, u32[]{:S(2)}) copy-start(s32[8,3]{0,1:T(4,128)} %param.16) | copy-start | bytes 292
  39.4 50.3 %all-to-all-start.1 = ((f32[32,24,128]{2,1,0:T(8,128)}), f32[32,24,128]{2,1,0:T(8,128)S(1)}, u32[]{:S(2)}, u32[]{:S(2)}) async-start(f32[32,24,128]{2,1,0:T(8,128)} %zonal.1.refs_13_), calls=%async_computation.1 | async-start | bytes 786432 | tf_op jit(solution)/shard_map/all_to_all | solution.py:652
  47.2 10.8 %collective-permute-start.2 = (f32[256,128]{1,0:T(8,128)S(1)}, f32[256,128]{1,0:T(8,128)S(1)}, u32[]{:S(2)}, u32[]{:S(2)}) collective-permute-start(f32[256,128]{1,0:T(8,128)S(1)} %get-tuple-element.25), channel_id=1, source_target_pairs={{0,4},{4,8},{8,12},{12,16},{16,20},{20,24},{24,28},{1,5},{5,9},{9,... | collective-permute-start | bytes 393224 | tf_op jit(solution)/shard_map/ppermute | solution.py:644
  50.9 7.9 %collective-permute-start.3 = (f32[256,128]{1,0:T(8,128)S(1)}, f32[256,128]{1,0:T(8,128)S(1)}, u32[]{:S(2)}, u32[]{:S(2)}) collective-permute-start(f32[256,128]{1,0:T(8,128)S(1)} %get-tuple-element.26), channel_id=1, source_target_pairs={{4,0},{8,4},{12,8},{16,12},{20,16},{24,20},{28,24},{5,1},{9,5},{13... | collective-permute-start | bytes 393224 | tf_op jit(solution)/shard_map/ppermute | solution.py:645
  52.2 5.8 %collective-permute-start.4 = (f32[96,128]{1,0:T(8,128)S(1)}, f32[96,128]{1,0:T(8,128)S(1)}, u32[]{:S(2)}, u32[]{:S(2)}) collective-permute-start(f32[96,128]{1,0:T(8,128)S(1)} %get-tuple-element.27), channel_id=1, source_target_pairs={{1,0},{2,1},{3,2},{5,4},{6,5},{7,6},{9,8},{10,9},{11,10},{13,12},{... | collective-permute-start | bytes 147464 | tf_op jit(solution)/shard_map/ppermute | solution.py:647
  53.5 4.5 %collective-permute-start.5 = (f32[96,128]{1,0:T(8,128)S(1)}, f32[96,128]{1,0:T(8,128)S(1)}, u32[]{:S(2)}, u32[]{:S(2)}) collective-permute-start(f32[96,128]{1,0:T(8,128)S(1)} %get-tuple-element.28), channel_id=1, source_target_pairs={{0,1},{1,2},{2,3},{4,5},{5,6},{6,7},{8,9},{9,10},{10,11},{12,13},{... | collective-permute-start | bytes 147464 | tf_op jit(solution)/shard_map/ppermute | solution.py:646
  56.6 0.7 collective-permute-start.6
  57.3 0.8 collective-permute-start.7
  58.8 2.1 %copy-start.2 = (f32[30,256,128]{2,1,0:T(8,128)S(1)}, f32[30,256,128]{2,1,0:T(8,128)}, u32[]{:S(2)}) copy-start(f32[30,256,128]{2,1,0:T(8,128)} %refs_10_.1) | copy-start | bytes 11796484
  60.9 28.7 %copy-start.4 = (f32[8,3,128,128]{3,2,1,0:T(8,128)S(1)}, f32[8,3,128,128]{3,2,1,0:T(8,128)}, u32[]{:S(2)}) copy-start(f32[8,3,128,128]{3,2,1,0:T(8,128)} %blocks_ref.3) | copy-start | bytes 4718596
where the time goes:
time: 114 us; the launch traced here: 113 us
  Pallas kernels  52.3 us (46%)
  starting transfers between devices  30.5 us (27%)
  blocking collectives  20.1 us (18%)
  local copies, waits for them, and re-layouts  7.42 us (7%)
  waiting for transfers between devices  1.59 us (1%)
    pallas_call x1, Pallas kernels, adjoint(): pl.pallas_call(kernel, grid=(steps,), out_shape=(struct(depth, rows, cols...  28.7 us
    all_to_all x1, blocking collectives, shards(): mixed = finish(lax.all_to_all(sent, 'gy', 0, 0), rows)  20.1 us
    pallas_call x1, Pallas kernels, rims(): pl.pallas_call(kernel, grid=(depth // step,), out_shape=(struct(rows, col...  16.2 us
    all_to_all x1, starting transfers between devices, shards(): columns = lax.all_to_all(packed, ('gy', 'gx'), 0, 0)  7.88 us
    unnamed x20, local copies, waits for them, and re-layouts  7.42 us
    all_to_all x1, starting transfers between devices, shards(): lines = lax.all_to_all(field, 'gx', 0, 0)  5.67 us
    ppermute x1, starting transfers between devices, shards(): level_col = lax.ppermute(level_col, 'gx', up_x)  4.87 us
    ppermute x1, starting transfers between devices, shards(): halo_w = lax.ppermute(east, 'gx', up_x)  3.68 us
  transfers between devices with their start and end apart: 10, of which 2 were waited for; matrix products, arithmetic and copies ran while one was open for 0% of the time, Pallas kernels for 40%

commit v1 on v0

v1 whole, which is shorter than its diff:
```python
import functools

import jax
import jax.numpy as jnp
from jax import lax
from jax.experimental import pallas as pl
from jax.experimental.pallas import tpu as pltpu
from jax.sharding import PartitionSpec as P

time_step = 0.5
gravity_scale = 0.05
coriolis_base = 0.4
zonal_slope = 0.3
north_slope = 0.2

LANES = 128
GROUP = 8
F32 = jnp.float32
BF16 = jnp.bfloat16
MIB = 1024 * 1024
BAND = 32


def whole():
    return pl.BlockSpec(memory_space=pltpu.VMEM)


def anywhere():
    return pl.BlockSpec(memory_space=pl.ANY)


def full(*shape):
    return pl.BlockSpec(shape, lambda i: (0,) * len(shape))


def smem():
    return pl.BlockSpec(memory_space=pltpu.SMEM)


def struct(*shape):
    return jax.ShapeDtypeStruct(shape, F32)


def params(mib):
    return pltpu.CompilerParams(vmem_limit_bytes=mib * MIB)


def cost(microseconds):
    return pl.CostEstimate(
        flops=int(microseconds * 1e6), bytes_accessed=int(microseconds * 3.0e6), transcendentals=0
    )


def has_before(axis):
    return lax.axis_index(axis) > 0


def has_after(axis):
    return lax.axis_index(axis) < lax.axis_size(axis) - 1


def lane_ids(shape):
    return lax.broadcasted_iota(jnp.int32, shape, 1)


def row_ids(shape):
    return lax.broadcasted_iota(jnp.int32, shape, 0)


def rim_kernel(
    step,
    levels_ref,
    mix_ref,
    u_ref,
    v_ref,
    t_ref,
    first_u_ref,
    first_v_ref,
    first_t_ref,
    last_u_ref,
    last_v_ref,
    last_t_ref,
    col_ref,
    row_ref,
    east_ref,
    west_ref,
    north_ref,
    south_ref,
):
    at = pl.program_id(0)
    rows, cols = mix_ref.shape
    depth = first_u_ref.shape[0]
    first = at * step
    chunk = 2 * GROUP
    lane = lane_ids((chunk, cols))
    edge = (lane == 0) | (lane == cols - 1)

    @pl.when(at == 0)
    def _():
        field = levels_ref[...].astype(F32)
        col_ref[...] = jnp.transpose(field)[cols - GROUP :]
        row_ref[...] = field[rows - GROUP :]
        east_ref[...] = jnp.zeros((rows, cols), F32)
        west_ref[...] = jnp.zeros((rows, cols), F32)
        mix = mix_ref[...]
        rest = north_ref.shape[0] - 3 * BAND
        north_ref[3 * BAND :, :] = jnp.broadcast_to(mix[rows - 1 :], (rest, cols))
        south_ref[3 * BAND :, :] = jnp.broadcast_to(mix[:1], (rest, cols))
        empty = jnp.zeros((BAND - depth, cols), F32)
        for f, ref in enumerate((last_u_ref, last_v_ref, last_t_ref)):
            line = ref[:, GROUP - 1 :, :].reshape(depth, cols)
            north_ref[f * BAND : (f + 1) * BAND, :] = jnp.concatenate([line, empty], axis=0)
        for f, ref in enumerate((first_u_ref, first_v_ref, first_t_ref)):
            line = ref[:, :1, :].reshape(depth, cols)
            south_ref[f * BAND : (f + 1) * BAND, :] = jnp.concatenate([line, empty], axis=0)

    flip = lax.rem(first, 2) == 1

    def body(i, carry):
        base = pl.multiple_of(i * chunk, chunk)
        here = pl.ds(base, chunk)
        sums = [None, None]
        for k in range(step):
            for f, ref in enumerate((u_ref, v_ref, t_ref)):
                value = jnp.where(edge, ref[k, here, :], 0.0)
                rolled = pltpu.roll(value, BAND * f + first + k + 1, 1)
                sums[k % 2] = rolled if sums[k % 2] is None else sums[k % 2] + rolled
        east_ref[here, :] += jnp.where(flip, sums[1], sums[0])
        west_ref[here, :] += jnp.where(flip, sums[0], sums[1])
        return carry

    lax.fori_loop(0, rows // chunk, body, 0, unroll=8)

    @pl.when(at == pl.num_programs(0) - 1)
    def _():
        ids = lane_ids((rows, cols))
        even = lax.rem(ids, 2) == 0
        mix = pltpu.roll(mix_ref[...], 3 * BAND + 1, 1)
        even_levels = east_ref[...]
        odd_levels = west_ref[...]
        east = jnp.where(even, even_levels, odd_levels)
        west = jnp.where(even, odd_levels, even_levels)
        east_ref[...] = jnp.where(ids == 3 * BAND, mix, east)
        west_ref[...] = jnp.where(ids == 3 * BAND + 1, mix, west)


def rims(levels, mixing, cots):
    depth, rows, cols = cots[0].shape
    step = 5
    lines = 3 * BAND + GROUP
    plane = full(rows, cols)
    block = pl.BlockSpec((step, rows, cols), lambda i: (i, 0, 0))
    top = rows // GROUP - 1
    first = pl.BlockSpec((depth, GROUP, cols), lambda i: (0, 0, 0))
    last = pl.BlockSpec((depth, GROUP, cols), lambda i: (0, top, 0))
    return pl.pallas_call(
        functools.partial(rim_kernel, step),
        grid=(depth // step,),
        out_shape=(struct(GROUP, rows), struct(GROUP, cols))
        + (struct(rows, cols),) * 2
        + (struct(lines, cols),) * 2,
        in_specs=[plane] * 2 + [block] * 3 + [first] * 3 + [last] * 3,
        out_specs=(full(GROUP, rows), full(GROUP, cols))
        + (plane,) * 2
        + (full(lines, cols),) * 2,
        compiler_params=params(12),
        cost_estimate=cost(6.0),
        name="rims",
    )(levels, mixing, *cots, *cots, *cots)


def surface_kernel(
    levels_ref,
    col_ref,
    row_ref,
    east_ref,
    west_ref,
    north_ref,
    south_ref,
    u_ref,
    v_ref,
    t_ref,
    out_ref,
    wet_c_ref,
    wet_u_ref,
    wet_v_ref,
    east_out_ref,
    west_out_ref,
    north_out_ref,
    south_out_ref,
):
    rows, cols = levels_ref.shape
    field = levels_ref[...].astype(F32)
    lane = lane_ids(field.shape)
    row = row_ids(field.shape)
    col = jnp.broadcast_to(jnp.transpose(col_ref[...])[:, GROUP - 1 :], field.shape)
    col = jnp.where(has_before("gx"), col, 0.0)
    west = jnp.where(lane == 0, col, pltpu.roll(field, 1, 1))
    line = jnp.broadcast_to(row_ref[GROUP - 1 :, :], field.shape)
    line = jnp.where(has_before("gy"), line, 0.0)
    south = jnp.where(row == 0, line, pltpu.roll(field, 1, 0))
    wet_u = jnp.minimum(field, west)
    wet_v = jnp.minimum(field, south)
    wets = (wet_u, wet_v, field)
    wet_c_ref[...] = field
    wet_u_ref[...] = wet_u
    wet_v_ref[...] = wet_v
    parts, chunk = (out_ref.shape[0], out_ref.shape[1] // 3)
    for comp, ref in enumerate((u_ref, v_ref, t_ref)):
        grad = jnp.where(wets[comp] > 0.0, time_step * ref[0], 0.0)
        for part in range(parts):
            out_ref[part, comp * chunk : (comp + 1) * chunk, :] = grad[
                part * chunk : (part + 1) * chunk
            ]
    for ref, out, place, shift in (
        (east_ref, east_out_ref, cols - 1, 0),
        (west_ref, west_out_ref, 0, 1),
    ):
        at = lax.rem(lane + cols - shift, cols)
        band = at // BAND
        level = lax.rem(at, BAND).astype(F32)
        limit = [jnp.broadcast_to(wet[:, place : place + 1], field.shape) for wet in wets]
        limit = jnp.where(band == 0, limit[0], jnp.where(band == 1, limit[1], limit[2]))
        out[...] = jnp.where((level < limit) | (band == 3), ref[...], 0.0)
    level = row_ids((BAND, cols)).astype(F32)
    for ref, out, place in ((north_ref, north_out_ref, rows - 1), (south_ref, south_out_ref, 0)):
        out[3 * BAND :, :] = ref[3 * BAND :, :]
        for f in range(3):
            band = slice(f * BAND, (f + 1) * BAND)
            out[band, :] = jnp.where(level < wets[f][place : place + 1], ref[band, :], 0.0)


def surface(levels, col, row, packed, cots, parts):
    rows, cols = levels.shape
    top = pl.BlockSpec((1, rows, cols), lambda i: (0, 0, 0))
    out = (parts, 3 * rows // parts, cols)
    rim = tuple(value.shape for value in packed)
    return pl.pallas_call(
        surface_kernel,
        grid=(1,),
        out_shape=(struct(*out),)
        + (struct(rows, cols),) * 3
        + tuple(struct(*shape) for shape in rim),
        in_specs=[full(rows, cols), full(GROUP, rows), full(GROUP, cols)]
        + [full(*shape) for shape in rim]
        + [top] * 3,
        out_specs=(full(*out),)
        + (full(rows, cols),) * 3
        + tuple(full(*shape) for shape in rim),
        compiler_params=params(12),
        cost_estimate=cost(2.0),
        name="surface",
    )(levels, col, row, *packed, *cots)


def corner_kernel(east_ref, west_ref, north_ref, south_ref, east_out_ref, west_out_ref):
    rows, cols = east_ref.shape
    north = jnp.where(has_after("gy"), north_ref[...], 0.0)
    south = jnp.where(has_before("gy"), south_ref[...], 0.0)
    missing = jnp.zeros((cols - north_ref.shape[0], cols), F32)
    corner_n = jnp.transpose(jnp.concatenate([north, missing], axis=0))[cols - 1 :]
    corner_s = jnp.transpose(jnp.concatenate([south, missing], axis=0))[:1]
    east_out_ref[:rows, :] = east_ref[...]
    west_out_ref[:rows, :] = west_ref[...]
    east_out_ref[rows:, :] = jnp.broadcast_to(corner_n, (GROUP, cols))
    west_out_ref[rows:, :] = jnp.broadcast_to(pltpu.roll(corner_s, 1, 1), (GROUP, cols))


def corners(east, west, halo_n, halo_s):
    rows, cols = east.shape
    return pl.pallas_call(
        corner_kernel,
        out_shape=(struct(rows + GROUP, cols),) * 2,
        in_specs=[whole()] * 4,
        out_specs=(whole(),) * 2,
        compiler_params=params(16),
        cost_estimate=cost(0.5),
        name="corners",
    )(east, west, halo_n, halo_s)


def adjoint_kernel(
    step,
    done,
    depth,
    total_rows,
    wet_c_ref,
    wet_u_ref,
    wet_v_ref,
    mix_ref,
    hw_ref,
    he_ref,
    hn_ref,
    hs_ref,
    old_refs,
    u_ref,
    v_ref,
    t_ref,
    gu_ref,
    gv_ref,
    gt_ref,
    state_ref,
    mix_n_ref,
    mix_s_ref,
    keep_ref,
    cor_ref,
    a_ref,
    b_ref,
    c_ref,
):
    rows, cols = mix_ref.shape
    at = pl.program_id(0)
    half = depth // 2
    first = depth - (done + at + 1) * step
    pad = GROUP
    cor_step = 0.25 * time_step * coriolis_base / total_rows
    slope_u = 0.5 * time_step * zonal_slope
    slope_v = 0.5 * time_step * north_slope
    weight = time_step * gravity_scale
    before_y, after_y = (has_before("gy"), has_after("gy"))

    @pl.when(at == 0)
    def _():
        shape = (rows, cols)
        lane = lane_ids(shape)
        row = row_ids(shape)
        start = lax.axis_index("gy") * rows
        lines = (row + start).astype(F32)
        cor = (0.25 * time_step * coriolis_base) * (0.5 + (lines + 0.5) / total_rows)
        cor_n = (0.25 * time_step * coriolis_base) * (0.5 + (lines + 1.5) / total_rows)
        cor_s = (0.25 * time_step * coriolis_base) * (0.5 + (lines - 0.5) / total_rows)
        cor_ref[...] = cor
        mix = mix_ref[...]
        keep_ref[...] = 1.0 - 4.0 * mix
        mix_n_ref[...] = jnp.where(
            row == rows - 1,
            jnp.broadcast_to(jnp.where(after_y, hn_ref[3 * BAND : 3 * BAND + 1, :], 0.0), shape),
            pltpu.roll(mix, rows - 1, 0),
        )
        mix_s_ref[...] = jnp.where(
            row == 0,
            jnp.broadcast_to(jnp.where(before_y, hs_ref[3 * BAND : 3 * BAND + 1, :], 0.0), shape),
            pltpu.roll(mix, 1, 0),
        )
        if old_refs:
            state_ref[...] = old_refs[0][...]
            return
        columns = jnp.where(has_after("gx"), he_ref[...], 0.0)
        east = columns[:rows]
        kind = lax.rem(lane + cols - 1, cols) // BAND
        mixed = east * jnp.broadcast_to(east[:, 3 * BAND + 1 : 3 * BAND + 2], shape)
        below = jnp.where(
            row == 0,
            jnp.broadcast_to(columns[rows : rows + 1], shape),
            pltpu.roll(east, 1, 0),
        )
        turned = cor * east + cor_s * below
        total = jnp.where(kind == 0, east, 0.0)
        reach = 1
        while reach < depth:
            total = total + pltpu.roll(total, cols - reach, 1)
            reach *= 2
        from_e = (
            mixed
            + jnp.where(kind == 1, pltpu.roll(turned, BAND, 1), 0.0)
            + jnp.where(kind == 2, pltpu.roll(weight * total, 2 * BAND, 1), 0.0)
        )
        columns = jnp.where(has_before("gx"), hw_ref[...], 0.0)
        west = columns[:rows]
        kind = lane // BAND
        mixed = west * jnp.broadcast_to(west[:, 3 * BAND : 3 * BAND + 1], shape)
        above = jnp.where(
            row == rows - 1,
            jnp.broadcast_to(columns[rows : rows + 1], shape),
            pltpu.roll(west, rows - 1, 0),
        )
        turned = cor * west + cor_n * above
        from_w = mixed - jnp.where(
            kind == 0,
            pltpu.roll(turned, cols - BAND, 1) + pltpu.roll(slope_u * west, cols - 2 * BAND, 1),
            0.0,
        )
        both = jnp.concatenate([from_e, from_w], axis=1)
        source = row_ids((2 * cols, 2 * cols))
        place = lane_ids((2 * cols, 2 * cols))
        part = place // cols
        spot = lax.rem(place, cols)
        pair = spot // 2
        slot = BAND * (pair // half) + part * half + lax.rem(pair, half)
        wanted = jnp.where(lax.rem(spot, 2) == 0, slot + 1, slot + cols)
        moves = jnp.where((source == wanted) & (pair < 3 * half), 1.0, 0.0).astype(BF16)
        moved = jnp.zeros((rows, 2 * cols), F32)
        for _ in range(3):
            high = both.astype(BF16)
            both = both - high.astype(F32)
            moved = moved + jnp.dot(high, moves, preferred_element_type=F32)
        state_ref[0] = moved[:, :cols]
        state_ref[1] = moved[:, cols:]
        state_ref[2] = jnp.zeros(shape, F32)
        state_ref[3] = jnp.zeros(shape, F32)

    fields = (
        (u_ref, wet_u_ref, a_ref),
        (v_ref, wet_v_ref, b_ref),
        (t_ref, wet_c_ref, c_ref),
    )

    def mask(i, carry):
        base = pl.multiple_of(i * 2 * GROUP, 2 * GROUP)
        here = pl.ds(base, 2 * GROUP)
        there = pl.ds(pl.multiple_of(base + pad, GROUP), 2 * GROUP)
        wets = [wet[here, :] for _, wet, _ in fields]
        for k in range(step):
            level = (first + k).astype(F32)
            for f, (ref, _, out) in enumerate(fields):
                out[k, there, :] = jnp.where(level < wets[f], ref[k, here, :], 0.0)
        return carry

    lax.fori_loop(0, rows // (2 * GROUP), mask, 0, unroll=8)
    for k in range(step):
        for f, (_, _, out) in enumerate(fields):
            slot = BAND * f + first + k
            out[k, pad - 1 : pad, :] = jnp.where(before_y, hs_ref[pl.ds(slot, 1), :], 0.0)
            out[k, pad + rows : pad + rows + 1, :] = jnp.where(
                after_y, hn_ref[pl.ds(slot, 1), :], 0.0
            )

    chunk = 2 * GROUP
    lane = lane_ids((chunk, cols))
    is_east = lane == cols - 1
    is_west = lane == 0
    part = (first >= half).astype(jnp.int32)

    def body(i, carry):
        base = pl.multiple_of(i * chunk, chunk)
        here = pl.ds(base, chunk)
        center = pl.ds(base + pad, chunk)
        north = pl.ds(base + pad + 1, chunk)
        south = pl.ds(base + pad - 1, chunk)
        mix = mix_ref[here, :]
        mix_n = mix_n_ref[here, :]
        mix_s = mix_s_ref[here, :]
        keep = keep_ref[here, :]
        cor = cor_ref[here, :]
        cor_n = cor + cor_step
        cor_s = cor - cor_step
        edges = state_ref[part, here, :]
        sum_a = state_ref[2, here, :]
        sum_d = state_ref[3, here, :]
        for k in reversed(range(step)):
            inner = first + k - part * half

            def both_sides(west, east, f, inner=inner):
                edge = pltpu.roll(edges, 2 * cols - 1 - 2 * (f * half + inner), 1)
                return jnp.where(is_west, edge, pltpu.roll(west, 1, 1)) + jnp.where(
                    is_east, edge, pltpu.roll(east, cols - 1, 1)
                )

            a = a_ref[k, center, :]
            a_n = a_ref[k, north, :]
            a_s = a_ref[k, south, :]
            b = b_ref[k, center, :]
            b_n = b_ref[k, north, :]
            b_s = b_ref[k, south, :]
            c = c_ref[k, center, :]
            c_n = c_ref[k, north, :]
            c_s = c_ref[k, south, :]
            mix_a = mix * a
            turn_b = cor * b + cor_n * b_n + slope_u * c
            gu_ref[k, here, :] = (
                keep * a
                + (mix_n * a_n + mix_s * a_s)
                - turn_b
                + both_sides(mix_a - turn_b, mix_a, 0)
            )
            mix_b = mix * b
            turn_a = cor * a + cor_s * a_s
            gv_ref[k, here, :] = (
                keep * b
                + (mix_n * b_n + mix_s * b_s)
                + (turn_a - slope_v * (c + c_s))
                + both_sides(mix_b, mix_b + turn_a, 1)
            )
            mix_c = mix * c
            sum_a = sum_a + weight * a
            sum_d = sum_d + weight * (b - b_n)
            gt_ref[k, here, :] = (
                keep * c
                + (mix_n * c_n + mix_s * c_s)
                - (sum_a + sum_d)
                + both_sides(mix_c, mix_c + sum_a, 2)
            )
        state_ref[2, here, :] = sum_a
        state_ref[3, here, :] = sum_d
        return carry

    lax.fori_loop(0, rows // chunk, body, 0, unroll=rows // chunk)


def adjoint(planes, halos, cots, after, total_rows, earlier=None):
    depth, rows, cols = cots[0].shape
    step = 5
    first = 2 * depth // (3 * step)
    done, steps = (0, first) if earlier is None else (first, depth // step - first)
    plane = full(rows, cols)
    top = depth // step - 1 - done
    block = pl.BlockSpec((step, rows, cols), lambda i: (top - i, 0, 0))
    grads, state = ((), ()) if earlier is None else earlier
    n_planes = len(planes) + len(halos)
    n_state = len(state)
    kept = (4, rows, cols)

    def kernel(*refs):
        front, refs = refs[:n_planes], refs[n_planes:]
        old, refs = refs[:n_state], refs[n_state:]
        ins, refs = refs[:3], refs[3 + 1 + len(grads) :]
        adjoint_kernel(step, done, depth, total_rows, *front, old, *ins, *refs)

    padded = pltpu.VMEM((step, rows + 2 * GROUP, cols), F32)
    aliases = {n_planes + n_state + 4 + i: i for i in range(len(grads))}
    result = pl.pallas_call(
        kernel,
        grid=(steps,),
        out_shape=(struct(depth, rows, cols),) * 3 + (struct(*kept),),
        in_specs=[plane] * len(planes)
        + [full(*halo.shape) for halo in halos]
        + [full(*kept)] * n_state
        + [block] * 3
        + [anywhere()] * (1 + len(grads)),
        out_specs=(block,) * 3 + (full(*kept),),
        scratch_shapes=[pltpu.VMEM((rows, cols), F32)] * 4 + [padded] * 3,
        input_output_aliases=aliases,
        compiler_params=params(20),
        cost_estimate=cost(3.0 * steps),
        name="adjoint",
    )(*planes, *halos, *state, *cots, after, *grads)
    return result[:3], result[3:]


def halves(value):
    high = value.astype(BF16)
    return high, (value - high.astype(F32)).astype(BF16)


def zonal_kernel(
    gy_size,
    pattern_ref,
    blocks_ref,
    field_ref,
    out_ref,
    high_ref,
    low_ref,
):
    tiles, height, cols = field_ref.shape
    chunk = height // 3
    width = cols // gy_size
    slots = LANES // width
    groups = chunk // GROUP
    owner = lane_ids((GROUP, cols)) // width
    for tile in range(tiles):
        high_ref[tile], low_ref[tile] = halves(field_ref[tile])
    for r in range(blocks_ref.shape[0]):
        picked = [pattern_ref[r, j] for j in range(blocks_ref.shape[1])]
        high = [high_ref[p] for p in picked]
        low = [low_ref[p] for p in picked]
        block = [halves(blocks_ref[r, j]) for j in range(blocks_ref.shape[1])]
        left = jnp.concatenate(high + high + low, axis=1)
        right = jnp.concatenate(
            [h for h, _ in block] + [l for _, l in block] + [h for h, _ in block], axis=1
        )
        result = lax.dot_general(
            left, right, (((1,), (1,)), ((), ())), preferred_element_type=F32
        )
        for y in range(gy_size):
            for v in range(out_ref.shape[1] // GROUP):
                packed = jnp.zeros((GROUP, cols), F32)
                for s in range(min(slots, 3 * groups - v * slots)):
                    q = v * slots + s
                    piece = result[q * GROUP : (q + 1) * GROUP]
                    if s != y:
                        piece = pltpu.roll(piece, ((s - y) * width) % cols, 1)
                    packed = jnp.where(owner == s, piece, packed)
                out_ref[y * tiles + r, v * GROUP : (v + 1) * GROUP, :] = packed


def zonal(pattern, blocks, field, gy_size):
    tiles, height, cols = field.shape
    width = cols // gy_size
    slots = LANES // width
    lines = -(-(height // GROUP) // slots) * GROUP

    return pl.pallas_call(
        functools.partial(zonal_kernel, gy_size),
        out_shape=struct(gy_size * tiles, lines, cols),
        in_specs=[smem()] + [whole()] * 2,
        out_specs=whole(),
        scratch_shapes=[pltpu.VMEM((tiles, height, cols), BF16)] * 2,
        compiler_params=params(16),
        cost_estimate=cost(2.0),
        name="zonal",
    )(pattern, blocks, field)


def meridional_kernel(
    gx_size, gy_size, pattern_ref, blocks_ref, field_ref, out_ref, high_ref, low_ref
):
    devices, lines, cols = field_ref.shape
    tiles, block, _ = high_ref.shape
    rows = tiles * block // gy_size
    chunk = rows // gx_size
    width = cols // gy_size
    slots = LANES // width
    groups = chunk // GROUP
    owner = lane_ids((GROUP, cols)) // width
    for d in range(devices):
        pieces = []
        for g in range(groups):
            packed = jnp.zeros((GROUP, cols), F32)
            for c in range(3):
                q = c * groups + g
                v, s = divmod(q, slots)
                piece = field_ref[d, v * GROUP : (v + 1) * GROUP, :]
                if s != c:
                    piece = pltpu.roll(piece, ((c - s) * width) % cols, 1)
                packed = jnp.where(owner == c, piece, packed)
            pieces.append(packed)
        tile, line = divmod(d * chunk, block)
        high, low = halves(jnp.concatenate(pieces, axis=0))
        high_ref[tile, line : line + chunk, :] = high
        low_ref[tile, line : line + chunk, :] = low
    for r in range(blocks_ref.shape[0]):
        picked = [pattern_ref[r, j] for j in range(blocks_ref.shape[1])]
        high = [high_ref[p] for p in picked]
        low = [low_ref[p] for p in picked]
        parts = [halves(blocks_ref[r, j]) for j in range(blocks_ref.shape[1])]
        left = jnp.concatenate(
            [h for h, _ in parts] + [l for _, l in parts] + [h for h, _ in parts], axis=1
        )
        right = jnp.concatenate(high + high + low, axis=0)
        result = jnp.dot(left, right, preferred_element_type=F32)
        dest, line = divmod(r * block, rows)
        first = line // GROUP
        for c in range(3):
            for v in range(block // GROUP // slots):
                packed = jnp.zeros((GROUP, cols), F32)
                for s in range(slots):
                    g = v * slots + s
                    piece = result[g * GROUP : (g + 1) * GROUP]
                    if s != c:
                        piece = pltpu.roll(piece, ((s - c) * width) % cols, 1)
                    packed = jnp.where(owner == s, piece, packed)
                at = (c * (rows // GROUP) + first) // slots + v
                out_ref[dest, at * GROUP : (at + 1) * GROUP, :] = packed


def meridional(pattern, blocks, field, gx_size, gy_size, after):
    devices, lines, cols = field.shape
    tiles, _, block, _ = blocks.shape
    rows = tiles * block // gy_size
    slots = LANES // (cols // gy_size)

    def kernel(pattern_ref, blocks_ref, field_ref, after_ref, *refs):
        meridional_kernel(gx_size, gy_size, pattern_ref, blocks_ref, field_ref, *refs)

    return pl.pallas_call(
        kernel,
        out_shape=struct(gy_size, 3 * rows // slots, cols),
        in_specs=[smem(), whole(), whole(), anywhere()],
        out_specs=whole(),
        scratch_shapes=[pltpu.VMEM((tiles, block, cols), BF16)] * 2,
        compiler_params=params(16),
        cost_estimate=cost(2.0),
        name="meridional",
    )(pattern, blocks, field, after)


def finish_kernel(field_ref, after_ref, out_ref):
    sources, _, cols = field_ref.shape
    _, rows, _ = out_ref.shape
    width = cols // sources
    slots = LANES // width
    owner = lane_ids((GROUP, cols)) // width
    for c in range(3):
        for g in range(rows // GROUP):
            v, s = divmod(c * (rows // GROUP) + g, slots)
            packed = jnp.zeros((GROUP, cols), F32)
            for y in range(sources):
                piece = field_ref[y, v * GROUP : (v + 1) * GROUP, :]
                if s != y:
                    piece = pltpu.roll(piece, ((y - s) * width) % cols, 1)
                packed = jnp.where(owner == y, piece, packed)
            out_ref[c, g * GROUP : (g + 1) * GROUP, :] = packed


def finish(field, rows, after):
    sources, _, cols = field.shape
    return pl.pallas_call(
        finish_kernel,
        out_shape=struct(3, rows, cols),
        in_specs=[whole(), anywhere()],
        out_specs=whole(),
        compiler_params=params(16),
        cost_estimate=cost(1.0),
        name="finish",
    )(field, after)


def shards(cot_u, cot_v, cot_t, levels, mixing, pattern_x, blocks_x, pattern_y, blocks_y):
    depth, rows, cols = cot_u.shape
    nx, ny = (lax.axis_size("gx"), lax.axis_size("gy"))
    up_x = [(i, (i + 1) % nx) for i in range(nx)]
    down_x = [(j, i) for i, j in up_x]
    up_y = [(i, (i + 1) % ny) for i in range(ny)]
    down_y = [(j, i) for i, j in up_y]

    cots = tuple(pltpu.with_memory_space_constraint(c, pltpu.HBM) for c in (cot_u, cot_v, cot_t))
    level_col, level_row, *packed = rims(levels, mixing, cots)
    level_col = lax.ppermute(level_col, "gx", up_x)
    level_row = lax.ppermute(level_row, "gy", up_y)
    field, wet_c, wet_u, wet_v, east, west, north, south = surface(
        levels, level_col, level_row, packed, cots, nx
    )
    lines = lax.all_to_all(field, "gx", 0, 0)
    halo_s = lax.ppermute(north, "gy", up_y)
    halo_n = lax.ppermute(south, "gy", down_y)
    east, west = corners(east, west, halo_n, halo_s)
    halo_w = lax.ppermute(east, "gx", up_x)
    halo_e = lax.ppermute(west, "gx", down_x)
    packed = zonal(pattern_x, blocks_x, lines, ny)
    packed, halo_w, halo_e = lax.optimization_barrier((packed, halo_w, halo_e))
    columns = lax.all_to_all(packed, ("gy", "gx"), 0, 0)
    planes = (wet_c, wet_u, wet_v, mixing)
    halos = (halo_w, halo_e, halo_n, halo_s)
    grads, state = adjoint(planes, halos, cots, packed, rows * ny)
    sent = meridional(pattern_y, blocks_y, columns, nx, ny, state[-1])
    back = lax.all_to_all(sent, "gy", 0, 0)
    grads = tuple(pltpu.with_memory_space_constraint(g, pltpu.HBM) for g in grads)
    grads, token = adjoint(planes, halos, cots, sent, rows * ny, (grads, state))
    mixed = finish(back, rows, token[0])
    return (*grads, mixed)


def solution(mesh):
    grid = P(None, "gy", "gx")
    flat = P("gy", "gx")
    return jax.shard_map(
        shards,
        mesh=mesh,
        in_specs=(grid, grid, grid, flat, flat, P(), P(), P(), P()),
        out_specs=(grid, grid, grid, grid),
        check_vma=False,
    )
```

time: 114 us -> 71.9 us (0.63)
  blocking collectives: 20.1 us -> 0 us
  Pallas kernels: 52.3 us -> 34.5 us
  waiting for transfers between devices: 1.59 us -> 14.7 us
  starting transfers between devices: 30.5 us -> 19.4 us
  local copies, waits for them, and re-layouts: 7.42 us -> 1.98 us
    all_to_all x1 -> x0, blocking collectives: 20.1 us -> none  [shards(): mixed = finish(lax.all_to_all(sent, 'gy', 0, 0), rows)]
    pallas_call x1 -> x2, Pallas kernels: 28.7 us -> 17.9 us  [adjoint(): pl.pallas_call(kernel, grid=(steps,), out_shape=(struct(depth, rows, cols...]
    pallas_call x3, Pallas kernels: 18.6 us -> 10.5 us  [the longest x1 8.08 us: rims(): pl.pallas_call(functools.partial(rim_kernel, step), grid=(depth // step,)...]
    unnamed x20 -> x16, local copies, waits for them, and re-layouts: 7.42 us -> 1.98 us
    all_to_all x1, starting transfers between devices: 7.88 us -> 3.99 us  [shards(): columns = lax.all_to_all(packed, ('gy', 'gx'), 0, 0)]
    all_to_all x0 -> x1, starting transfers between devices: none -> 3.46 us  [shards(): back = lax.all_to_all(sent, 'gy', 0, 0)]
    ppermute x1, starting transfers between devices: 3.03 us -> 0.45 us  [shards(): halo_s = lax.ppermute(north, 'gy', up_y)]
    all_to_all x1, waiting for transfers between devices: 0.01 us -> 2.41 us  [shards(): lines = lax.all_to_all(field, 'gx', 0, 0)]
  transfers between devices with their start and end apart: 10 -> 9, of which waited for: 2 -> 8; matrix products, arithmetic and copies ran while one was open for 0% -> 0% of each run, Pallas kernels for 40% -> 29%
where the time goes in v1:
time: 71.9 us; the launch traced here: 71.3 us
  Pallas kernels  34.5 us (48%)
  starting transfers between devices  19.4 us (27%)
  waiting for transfers between devices  14.7 us (20%)
  local copies, waits for them, and re-layouts  1.98 us (3%)
    pallas_call x2, Pallas kernels, adjoint(): pl.pallas_call(kernel, grid=(steps,), out_shape=(struct(depth, rows, cols...  17.9 us
    pallas_call x1, Pallas kernels, rims(): pl.pallas_call(functools.partial(rim_kernel, step), grid=(depth // step,)...  8.08 us
    all_to_all x1, starting transfers between devices, shards(): columns = lax.all_to_all(packed, ('gy', 'gx'), 0, 0)  3.99 us
    all_to_all x1, starting transfers between devices, shards(): lines = lax.all_to_all(field, 'gx', 0, 0)  3.58 us
    all_to_all x1, starting transfers between devices, shards(): back = lax.all_to_all(sent, 'gy', 0, 0)  3.46 us
    ppermute x1, waiting for transfers between devices, shards(): level_row = lax.ppermute(level_row, 'gy', up_y)  3.03 us
    ppermute x1, starting transfers between devices, shards(): level_col = lax.ppermute(level_col, 'gx', up_x)  3.02 us
    ppermute x1, starting transfers between devices, shards(): halo_e = lax.ppermute(west, 'gx', down_x)  2.93 us
  transfers between devices with their start and end apart: 9, of which 8 were waited for; matrix products, arithmetic and copies ran while one was open for 0% of the time, Pallas kernels for 29%

profile of v1, /device:TPU:0, one launch (start us, length us, event | category | flops | bytes accessed | tf_op | source)
XLA Modules:
  0.0 71.3 jit_solution(15052922056502056003)
XLA Ops:
  0.6 0.0 copy-start.2
  0.6 0.9 %copy-done.2 = f32[256,128]{1,0:T(8,128)S(1)} copy-done((f32[256,128]{1,0:T(8,128)S(1)}, f32[256,128]{1,0:T(8,128)}, u32[]{:S(2)}) %copy-start.2) | copy-done | bytes 131096
  1.5 0.0 copy-start.4
  1.5 0.9 %copy-done.4 = s32[256,128]{1,0:T(8,128)S(1)} copy-done((s32[256,128]{1,0:T(8,128)S(1)}, s32[256,128]{1,0:T(8,128)}, u32[]{:S(2)}) %copy-start.4) | copy-done | bytes 131096
  2.4 8.1 %rims.1 = (f32[8,256]{1,0:T(8,128)S(1)}, f32[8,128]{1,0:T(8,128)S(1)}, f32[256,128]{1,0:T(8,128)S(1)}, f32[256,128]{1,0:T(8,128)S(1)}, f32[104,128]{1,0:T(8,128)S(1)}, /*index=5*/f32[104,128]{1,0:T(8,128)S(1)}) custom-call(s32[256,128]{1,0:T(8,128)S(1)} %copy-done.4, f32[256,128]{1,0:T(8,128)S(1)} %copy-done.2, f32[30,256,128]{2,1,0:T(8,128)} %refs_9_.3, ...), custom_call_target="tpu_custom_call" | custom-call | flops 6000000 | bytes 18000000 | tf_op jit(solution)/shard_map/rims/pallas_call | solution.py:156
  10.5 3.0 %collective-permute-start = (f32[8,256]{1,0:T(8,128)S(1)}, f32[8,256]{1,0:T(8,128)S(1)}, u32[]{:S(2)}, u32[]{:S(2)}) collective-permute-start(f32[8,256]{1,0:T(8,128)S(1)} %get-tuple-element.31), channel_id=1, source_target_pairs={{0,4},{4,8},{8,12},{12,16},{16,20},{20,24},{24,28},{28,0},{1,5},{5... | collective-permute-start | bytes 24584 | tf_op jit(solution)/shard_map/ppermute | solution.py:718
  13.6 0.0 collective-permute-start.1
  13.6 3.0 %collective-permute-done.1.row_ref = f32[8,128]{1,0:T(8,128)S(1)} collective-permute-done((f32[8,128]{1,0:T(8,128)S(1)}, f32[8,128]{1,0:T(8,128)S(1)}, u32[]{:S(2)}, u32[]{:S(2)}) %collective-permute-start.1) | collective-permute-done | bytes 4128 | tf_op jit(solution)/shard_map/ppermute | solution.py:719
  16.6 1.6 %collective-permute-done.col_ref = f32[8,256]{1,0:T(8,128)S(1)} collective-permute-done((f32[8,256]{1,0:T(8,128)S(1)}, f32[8,256]{1,0:T(8,128)S(1)}, u32[]{:S(2)}, u32[]{:S(2)}) %collective-permute-start) | collective-permute-done | bytes 8224 | tf_op jit(solution)/shard_map/ppermute | solution.py:718
  18.2 0.0 copy-start.5
  18.2 0.0 copy-start
  18.2 2.3 %surface.1 = (f32[8,96,128]{2,1,0:T(8,128)}, f32[256,128]{1,0:T(8,128)S(1)}, f32[256,128]{1,0:T(8,128)S(1)}, f32[256,128]{1,0:T(8,128)S(1)}, f32[256,128]{1,0:T(...) custom-call(s32[256,128]{1,0:T(8,128)S(1)} %copy-done.4, ...), custom_call_target="tpu_custom_call" | custom-call | flops 2000000 | bytes 6000000 | tf_op jit(solution)/shard_map/surface/pallas_call | solution.py:238
  20.6 0.0 copy-start.6
  20.6 0.0 copy-start.3
  20.6 3.6 %all-to-all-start = ((f32[8,96,128]{2,1,0:T(8,128)}), f32[8,96,128]{2,1,0:T(8,128)S(1)}, u32[]{:S(2)}, u32[]{:S(2)}) async-start(f32[8,96,128]{2,1,0:T(8,128)} %get-tuple-element.40), calls=%async_computation | async-start | bytes 786432 | tf_op jit(solution)/shard_map/all_to_all | solution.py:723
  24.2 0.1 collective-permute-start.2
  24.3 0.4 collective-permute-start.3
  24.7 1.3 %collective-permute-done.2.north_ref.refs_6_ = f32[104,128]{1,0:T(8,128)S(1)} collective-permute-done((f32[104,128]{1,0:T(8,128)S(1)}, f32[104,128]{1,0:T(8,128)S(1)}, u32[]{:S(2)}, u32[]{:S(2)}) %collective-permute-start.2) | collective-permute-done | bytes 53280 | tf_op jit(solution)/shard_map/ppermute | solution.py:725
  26.1 2.2 %collective-permute-done.3.south_ref.refs_7_ = f32[104,128]{1,0:T(8,128)S(1)} collective-permute-done((f32[104,128]{1,0:T(8,128)S(1)}, f32[104,128]{1,0:T(8,128)S(1)}, u32[]{:S(2)}, u32[]{:S(2)}) %collective-permute-start.3) | collective-permute-done | bytes 53280 | tf_op jit(solution)/shard_map/ppermute | solution.py:724
  28.3 0.1 corners.1
  28.4 1.8 %collective-permute-start.4 = (f32[264,128]{1,0:T(8,128)S(1)}, f32[264,128]{1,0:T(8,128)S(1)}, u32[]{:S(2)}, u32[]{:S(2)}) collective-permute-start(f32[264,128]{1,0:T(8,128)S(1)} %get-tuple-element.45), channel_id=1, source_target_pairs={{0,4},{4,8},{8,12},{12,16},{16,20},{20,24},{24,28},{28,0},{1,5},{5... | collective-permute-start | bytes 405512 | tf_op jit(solution)/shard_map/ppermute | solution.py:727
  30.2 2.9 %collective-permute-start.5 = (f32[264,128]{1,0:T(8,128)S(1)}, f32[264,128]{1,0:T(8,128)S(1)}, u32[]{:S(2)}, u32[]{:S(2)}) collective-permute-start(f32[264,128]{1,0:T(8,128)S(1)} %get-tuple-element.46), channel_id=1, source_target_pairs={{4,0},{8,4},{12,8},{16,12},{20,16},{24,20},{28,24},{0,28},{5,1},{9... | collective-permute-start | bytes 405512 | tf_op jit(solution)/shard_map/ppermute | solution.py:728
  33.1 0.0 copy-done.5
  33.2 0.1 copy.16.pattern_ref
  33.2 2.4 %all-to-all-done.field_ref = f32[8,96,128]{2,1,0:T(8,128)S(1)} async-done(((f32[8,96,128]{2,1,0:T(8,128)}), f32[8,96,128]{2,1,0:T(8,128)S(1)}, u32[]{:S(2)}, u32[]{:S(2)}) %all-to-all-start) | async-done | bytes 393248 | tf_op jit(solution)/shard_map/all_to_all | solution.py:723
  35.6 0.0 copy-done
  35.6 2.3 %zonal.1.refs_11_ = f32[32,24,128]{2,1,0:T(8,128)} custom-call(s32[8,3]{1,0:T(8,128)S(1)} %copy.16.pattern_ref, f32[8,3,128,128]{3,2,1,0:T(8,128)S(1)} %copy-done, f32[8,96,128]{2,1,0:T(8,128)S(1)} %all-to-all-done.field_ref), custom_call_target="tpu_custom_call" | custom-call | flops 2000000 | bytes 6000000 | tf_op jit(solution)/shard_map/zonal/pallas_call | solution.py:592
  38.0 0.0 collective-permute-done.4.refs_4_
  38.0 1.2 %collective-permute-done.5.refs_5_ = f32[264,128]{1,0:T(8,128)S(1)} collective-permute-done((f32[264,128]{1,0:T(8,128)S(1)}, f32[264,128]{1,0:T(8,128)S(1)}, u32[]{:S(2)}, u32[]{:S(2)}) %collective-permute-start.5) | collective-permute-done | bytes 135200 | tf_op jit(solution)/shard_map/ppermute | solution.py:728
  39.2 4.0 %all-to-all-start.1 = ((f32[32,24,128]{2,1,0:T(8,128)}), f32[32,24,128]{2,1,0:T(8,128)S(1)}, u32[]{:S(2)}, u32[]{:S(2)}) async-start(f32[32,24,128]{2,1,0:T(8,128)} %zonal.1.refs_11_), calls=%async_computation.1 | async-start | bytes 786432 | tf_op jit(solution)/shard_map/all_to_all | solution.py:731
  43.2 0.0 copy-done.6
  43.2 0.1 copy.17.pattern_ref
  43.3 0.0 copy-done.3
  43.3 0.0 copy-start.1
  43.3 11.4 %adjoint.2 = (f32[30,256,128]{2,1,0:T(8,128)}, f32[30,256,128]{2,1,0:T(8,128)}, f32[30,256,128]{2,1,0:T(8,128)}, f32[4,256,128]{2,1,0:T(8,128)S(1)}) custom-call(f32[256,128]{1,0:T(8,128)S(1)} %get-tuple-element.37.refs_0_, f32[256,128]{1,0:T(8,128)S(1)} %get-tuple-element.38.refs_1_, f32[256,128]{1,0:T(8,128)S(1)} %get-tuple-element.39.refs_2_, ...), custom_call_target="tpu_custom_call" | custom-call | flops 12000000 | bytes 36000000 | tf_op jit(solution)/shard_map/adjoint/pallas_call | solution.py:521
  54.6 2.1 %all-to-all-done.1.field_ref = f32[32,24,128]{2,1,0:T(8,128)S(1)} async-done(((f32[32,24,128]{2,1,0:T(8,128)}), f32[32,24,128]{2,1,0:T(8,128)S(1)}, u32[]{:S(2)}, u32[]{:S(2)}) %all-to-all-start.1) | async-done | bytes 393248 | tf_op jit(solution)/shard_map/all_to_all | solution.py:731
  56.7 0.0 copy-done.1
  56.7 2.6 %meridional.1.refs_12_ = f32[4,192,128]{2,1,0:T(8,128)} custom-call(s32[8,3]{1,0:T(8,128)S(1)} %copy.17.pattern_ref, f32[8,3,128,128]{3,2,1,0:T(8,128)S(1)} %copy-done.1, f32[32,24,128]{2,1,0:T(8,128)S(1)} %all-to-all-done.1.field_ref, f32[4,256,128]{2,1,0:T(8,128)S(1)} %get-tuple-element.50.after_ref.refs_8_), custom_call_target="tpu_custom_call" | custom-call | flops 2000000 | bytes 6000000 | tf_op jit(solution)/shard_map/meridional/pallas_call | solution.py:665
  59.3 3.5 %all-to-all-start.2 = ((f32[4,192,128]{2,1,0:T(8,128)}), f32[4,192,128]{2,1,0:T(8,128)S(1)}, u32[]{:S(2)}, u32[]{:S(2)}) async-start(f32[4,192,128]{2,1,0:T(8,128)} %meridional.1.refs_12_), calls=%async_computation.2 | async-start | bytes 786432 | tf_op jit(solution)/shard_map/all_to_all | solution.py:736
  62.8 6.6 %adjoint.3 = (f32[30,256,128]{2,1,0:T(8,128)}, f32[30,256,128]{2,1,0:T(8,128)}, f32[30,256,128]{2,1,0:T(8,128)}, f32[4,256,128]{2,1,0:T(8,128)S(1)}) custom-call(f32[256,128]{1,0:T(8,128)S(1)} %get-tuple-element.37.refs_0_, f32[256,128]{1,0:T(8,128)S(1)} %get-tuple-element.38.refs_1_, ...), custom_call_target="tpu_custom_call", output_to_operand_aliasing={{0}: (13, {}), {1}: (14, {}), {2}: (15, {})} | custom-call | flops 6000000 | bytes 18000000 | tf_op jit(solution)/shard_map/adjoint/pallas_call | solution.py:521
  69.3 0.9 %all-to-all-done.2.field_ref = f32[4,192,128]{2,1,0:T(8,128)S(1)} async-done(((f32[4,192,128]{2,1,0:T(8,128)}), f32[4,192,128]{2,1,0:T(8,128)S(1)}, u32[]{:S(2)}, u32[]{:S(2)}) %all-to-all-start.2) | async-done | bytes 393248 | tf_op jit(solution)/shard_map/all_to_all | solution.py:736
  70.2 1.1 %finish.1 = f32[3,256,128]{2,1,0:T(8,128)} custom-call(f32[4,192,128]{2,1,0:T(8,128)S(1)} %all-to-all-done.2.field_ref, f32[4,256,128]{2,1,0:T(8,128)S(1)} %get-tuple-element.57.after_ref), custom_call_target="tpu_custom_call" | custom-call | flops 1000000 | bytes 3000000 | tf_op jit(solution)/shard_map/finish/pallas_call | solution.py:697
Async XLA Ops:
  0.6 0.9 %copy-start.2 = (f32[256,128]{1,0:T(8,128)S(1)}, f32[256,128]{1,0:T(8,128)}, u32[]{:S(2)}) copy-start(f32[256,128]{1,0:T(8,128)} %refs_3_.3) | copy-start | bytes 393220
  1.5 0.9 %copy-start.4 = (s32[256,128]{1,0:T(8,128)S(1)}, s32[256,128]{1,0:T(8,128)}, u32[]{:S(2)}) copy-start(s32[256,128]{1,0:T(8,128)} %levels_ref.3) | copy-start | bytes 393220
  10.5 7.7 %collective-permute-start = (f32[8,256]{1,0:T(8,128)S(1)}, f32[8,256]{1,0:T(8,128)S(1)}, u32[]{:S(2)}, u32[]{:S(2)}) collective-permute-start(f32[8,256]{1,0:T(8,128)S(1)} %get-tuple-element.31), channel_id=1, source_target_pairs={{0,4},{4,8},{8,12},{12,16},{16,20},{20,24},{24,28},{28,0},{1,5},{5... | collective-permute-start | bytes 24584 | tf_op jit(solution)/shard_map/ppermute | solution.py:718
  13.6 3.0 %collective-permute-start.1 = (f32[8,128]{1,0:T(8,128)S(1)}, f32[8,128]{1,0:T(8,128)S(1)}, u32[]{:S(2)}, u32[]{:S(2)}) collective-permute-start(f32[8,128]{1,0:T(8,128)S(1)} %get-tuple-element.32), channel_id=1, source_target_pairs={{0,1},{1,2},{2,3},{3,0},{4,5},{5,6},{6,7},{7,4},{8,9},{9,10},{10,1... | collective-permute-start | bytes 12296 | tf_op jit(solution)/shard_map/ppermute | solution.py:719
  18.2 14.9 %copy-start.5 = (s32[8,3]{0,1:T(4,128)S(1)}, s32[8,3]{0,1:T(4,128)}, u32[]{:S(2)}) copy-start(s32[8,3]{0,1:T(4,128)} %param.14) | copy-start | bytes 292
  18.2 17.4 %copy-start = (f32[8,3,128,128]{3,2,1,0:T(8,128)S(1)}, f32[8,3,128,128]{3,2,1,0:T(8,128)}, u32[]{:S(2)}) copy-start(f32[8,3,128,128]{3,2,1,0:T(8,128)} %blocks_ref.2) | copy-start | bytes 4718596
  20.6 22.6 %copy-start.6 = (s32[8,3]{0,1:T(4,128)S(1)}, s32[8,3]{0,1:T(4,128)}, u32[]{:S(2)}) copy-start(s32[8,3]{0,1:T(4,128)} %param.16) | copy-start | bytes 292
  20.6 22.7 %copy-start.3 = (f32[256,128]{1,0:T(8,128)S(1)}, f32[256,128]{1,0:T(8,128)}, u32[]{:S(2)}) copy-start(f32[256,128]{1,0:T(8,128)} %refs_3_.3) | copy-start | bytes 393220
  20.6 15.1 %all-to-all-start = ((f32[8,96,128]{2,1,0:T(8,128)}), f32[8,96,128]{2,1,0:T(8,128)S(1)}, u32[]{:S(2)}, u32[]{:S(2)}) async-start(f32[8,96,128]{2,1,0:T(8,128)} %get-tuple-element.40), calls=%async_computation | async-start | bytes 786432 | tf_op jit(solution)/shard_map/all_to_all | solution.py:723
  24.2 1.9 %collective-permute-start.2 = (f32[104,128]{1,0:T(8,128)S(1)}, f32[104,128]{1,0:T(8,128)S(1)}, u32[]{:S(2)}, u32[]{:S(2)}) collective-permute-start(f32[104,128]{1,0:T(8,128)S(1)} %get-tuple-element.43), channel_id=1, source_target_pairs={{1,0},{2,1},{3,2},{0,3},{5,4},{6,5},{7,6},{4,7},{9,8},{10,9},{11,1... | collective-permute-start | bytes 159752 | tf_op jit(solution)/shard_map/ppermute | solution.py:725
  24.3 4.0 %collective-permute-start.3 = (f32[104,128]{1,0:T(8,128)S(1)}, f32[104,128]{1,0:T(8,128)S(1)}, u32[]{:S(2)}, u32[]{:S(2)}) collective-permute-start(f32[104,128]{1,0:T(8,128)S(1)} %get-tuple-element.44), channel_id=1, source_target_pairs={{0,1},{1,2},{2,3},{3,0},{4,5},{5,6},{6,7},{7,4},{8,9},{9,10},{10,1... | collective-permute-start | bytes 159752 | tf_op jit(solution)/shard_map/ppermute | solution.py:724
  28.4 9.6 %collective-permute-start.4 = (f32[264,128]{1,0:T(8,128)S(1)}, f32[264,128]{1,0:T(8,128)S(1)}, u32[]{:S(2)}, u32[]{:S(2)}) collective-permute-start(f32[264,128]{1,0:T(8,128)S(1)} %get-tuple-element.45), channel_id=1, source_target_pairs={{0,4},{4,8},{8,12},{12,16},{16,20},{20,24},{24,28},{28,0},{1,5},{5... | collective-permute-start | bytes 405512 | tf_op jit(solution)/shard_map/ppermute | solution.py:727
  30.2 8.9 %collective-permute-start.5 = (f32[264,128]{1,0:T(8,128)S(1)}, f32[264,128]{1,0:T(8,128)S(1)}, u32[]{:S(2)}, u32[]{:S(2)}) collective-permute-start(f32[264,128]{1,0:T(8,128)S(1)} %get-tuple-element.46), channel_id=1, source_target_pairs={{4,0},{8,4},{12,8},{16,12},{20,16},{24,20},{28,24},{0,28},{5,1},{9... | collective-permute-start | bytes 405512 | tf_op jit(solution)/shard_map/ppermute | solution.py:728
  39.2 17.5 %all-to-all-start.1 = ((f32[32,24,128]{2,1,0:T(8,128)}), f32[32,24,128]{2,1,0:T(8,128)S(1)}, u32[]{:S(2)}, u32[]{:S(2)}) async-start(f32[32,24,128]{2,1,0:T(8,128)} %zonal.1.refs_11_), calls=%async_computation.1 | async-start | bytes 786432 | tf_op jit(solution)/shard_map/all_to_all | solution.py:731
  43.3 13.5 %copy-start.1 = (f32[8,3,128,128]{3,2,1,0:T(8,128)S(1)}, f32[8,3,128,128]{3,2,1,0:T(8,128)}, u32[]{:S(2)}) copy-start(f32[8,3,128,128]{3,2,1,0:T(8,128)} %blocks_ref.3) | copy-start | bytes 4718596
  59.3 10.9 %all-to-all-start.2 = ((f32[4,192,128]{2,1,0:T(8,128)}), f32[4,192,128]{2,1,0:T(8,128)S(1)}, u32[]{:S(2)}, u32[]{:S(2)}) async-start(f32[4,192,128]{2,1,0:T(8,128)} %meridional.1.refs_12_), calls=%async_computation.2 | async-start | bytes 786432 | tf_op jit(solution)/shard_map/all_to_all | solution.py:736

commit v2 on v1

v2 whole, which is shorter than its diff:
```python
import functools

import jax
import jax.numpy as jnp
from jax import lax
from jax.experimental import pallas as pl
from jax.experimental.pallas import tpu as pltpu
from jax.sharding import PartitionSpec as P

time_step = 0.5
gravity_scale = 0.05
coriolis_base = 0.4
zonal_slope = 0.3
north_slope = 0.2

LANES = 128
GROUP = 8
F32 = jnp.float32
BF16 = jnp.bfloat16
MIB = 1024 * 1024
BAND = 32


def whole():
    return pl.BlockSpec(memory_space=pltpu.VMEM)


def anywhere():
    return pl.BlockSpec(memory_space=pl.ANY)


def full(*shape):
    return pl.BlockSpec(shape, lambda i: (0,) * len(shape))


def smem():
    return pl.BlockSpec(memory_space=pltpu.SMEM)


def struct(*shape):
    return jax.ShapeDtypeStruct(shape, F32)


def params(mib):
    return pltpu.CompilerParams(vmem_limit_bytes=mib * MIB)


def cost(microseconds):
    return pl.CostEstimate(
        flops=int(microseconds * 1e6), bytes_accessed=int(microseconds * 3.0e6), transcendentals=0
    )


def has_before(axis):
    return lax.axis_index(axis) > 0


def has_after(axis):
    return lax.axis_index(axis) < lax.axis_size(axis) - 1


def lane_ids(shape):
    return lax.broadcasted_iota(jnp.int32, shape, 1)


def row_ids(shape):
    return lax.broadcasted_iota(jnp.int32, shape, 0)


def edge_kernel(levels_ref, col_ref, row_ref):
    rows, cols = levels_ref.shape
    field = levels_ref[...].astype(F32)
    col_ref[...] = jnp.transpose(field)[cols - GROUP :]
    row_ref[...] = field[rows - GROUP :]


def edges(levels):
    rows, cols = levels.shape
    return pl.pallas_call(
        edge_kernel,
        grid=(1,),
        out_shape=(struct(GROUP, rows), struct(GROUP, cols)),
        in_specs=[full(rows, cols)],
        out_specs=(full(GROUP, rows), full(GROUP, cols)),
        compiler_params=params(4),
        cost_estimate=cost(1.0),
        name="edges",
    )(levels)


def rim_kernel(
    step,
    mix_ref,
    u_ref,
    v_ref,
    t_ref,
    east_ref,
    west_ref,
    north_ref,
    south_ref,
    top_ref,
    u_here,
    v_here,
    t_here,
    arrived,
):
    depth, rows, cols = u_ref.shape
    fields = ((u_ref, u_here), (v_ref, v_here), (t_ref, t_here))
    chunk = 2 * GROUP
    lane = lane_ids((chunk, cols))
    edge = (lane == 0) | (lane == cols - 1)

    def copy(f, at):
        levels = pl.ds(at * step, step)
        source, target = fields[f]
        return pltpu.make_async_copy(source.at[levels], target.at[levels], arrived.at[f, at])

    for at in range(depth // step):
        for f in range(3):
            copy(f, at).start()
    east_ref[...] = jnp.zeros((rows, cols), F32)
    west_ref[...] = jnp.zeros((rows, cols), F32)
    mix = mix_ref[...]
    rest = north_ref.shape[0] - 3 * BAND
    north_ref[3 * BAND :, :] = jnp.broadcast_to(mix[rows - 1 :], (rest, cols))
    south_ref[3 * BAND :, :] = jnp.broadcast_to(mix[:1], (rest, cols))

    def levels(at, carry):
        first = at * step
        flip = lax.rem(first, 2) == 1
        for f in range(3):
            copy(f, at).wait()

        def body(i, inner):
            here = pl.ds(pl.multiple_of(i * chunk, chunk), chunk)
            sums = [None, None]
            for k in range(step):
                for f in range(3):
                    value = jnp.where(edge, fields[f][1][first + k, here, :], 0.0)
                    moved = pltpu.roll(value, BAND * f + first + k + 1, 1)
                    sums[k % 2] = moved if sums[k % 2] is None else sums[k % 2] + moved
            east_ref[here, :] += jnp.where(flip, sums[1], sums[0])
            west_ref[here, :] += jnp.where(flip, sums[0], sums[1])
            return inner

        lax.fori_loop(0, rows // chunk, body, 0, unroll=8)
        return carry

    lax.fori_loop(0, depth // step, levels, 0)
    ids = lane_ids((rows, cols))
    even = lax.rem(ids, 2) == 0
    mix = pltpu.roll(mix, 3 * BAND + 1, 1)
    even_levels = east_ref[...]
    odd_levels = west_ref[...]
    east = jnp.where(even, even_levels, odd_levels)
    west = jnp.where(even, odd_levels, even_levels)
    east_ref[...] = jnp.where(ids == 3 * BAND, mix, east)
    west_ref[...] = jnp.where(ids == 3 * BAND + 1, mix, west)
    empty = jnp.zeros((BAND - depth, cols), F32)
    for f in range(3):
        band = slice(f * BAND, (f + 1) * BAND)
        here = fields[f][1]
        for out, place in ((north_ref, rows - 1), (south_ref, 0)):
            line = here[:, place : place + 1, :].reshape(depth, cols)
            out[band, :] = jnp.concatenate([line, empty], axis=0)
        top_ref[f] = here[0]


def rims(mixing, cots):
    depth, rows, cols = cots[0].shape
    step = 5
    lines = 3 * BAND + GROUP
    return pl.pallas_call(
        functools.partial(rim_kernel, step),
        out_shape=(struct(rows, cols),) * 2
        + (struct(lines, cols),) * 2
        + (struct(3, rows, cols),),
        in_specs=[whole()] + [anywhere()] * 3,
        out_specs=(whole(),) * 5,
        scratch_shapes=[pltpu.VMEM((depth, rows, cols), F32)] * 3
        + [pltpu.SemaphoreType.DMA((3, depth // step))],
        compiler_params=params(14),
        cost_estimate=cost(6.0),
        name="rims",
    )(mixing, *cots)


def surface_kernel(
    levels_ref,
    col_ref,
    row_ref,
    east_ref,
    west_ref,
    north_ref,
    south_ref,
    top_ref,
    out_ref,
    wet_c_ref,
    wet_u_ref,
    wet_v_ref,
    east_out_ref,
    west_out_ref,
    north_out_ref,
    south_out_ref,
):
    rows, cols = levels_ref.shape
    field = levels_ref[...].astype(F32)
    lane = lane_ids(field.shape)
    row = row_ids(field.shape)
    col = jnp.broadcast_to(jnp.transpose(col_ref[...])[:, GROUP - 1 :], field.shape)
    col = jnp.where(has_before("gx"), col, 0.0)
    west = jnp.where(lane == 0, col, pltpu.roll(field, 1, 1))
    line = jnp.broadcast_to(row_ref[GROUP - 1 :, :], field.shape)
    line = jnp.where(has_before("gy"), line, 0.0)
    south = jnp.where(row == 0, line, pltpu.roll(field, 1, 0))
    wet_u = jnp.minimum(field, west)
    wet_v = jnp.minimum(field, south)
    wets = (wet_u, wet_v, field)
    wet_c_ref[...] = field
    wet_u_ref[...] = wet_u
    wet_v_ref[...] = wet_v
    for comp in range(3):
        out_ref[comp] = jnp.where(wets[comp] > 0.0, time_step * top_ref[comp], 0.0)
    for ref, out, place, shift in (
        (east_ref, east_out_ref, cols - 1, 0),
        (west_ref, west_out_ref, 0, 1),
    ):
        at = lax.rem(lane + cols - shift, cols)
        band = at // BAND
        level = lax.rem(at, BAND).astype(F32)
        limit = [jnp.broadcast_to(wet[:, place : place + 1], field.shape) for wet in wets]
        limit = jnp.where(band == 0, limit[0], jnp.where(band == 1, limit[1], limit[2]))
        out[...] = jnp.where((level < limit) | (band == 3), ref[...], 0.0)
    level = row_ids((BAND, cols)).astype(F32)
    for ref, out, place in ((north_ref, north_out_ref, rows - 1), (south_ref, south_out_ref, 0)):
        out[3 * BAND :, :] = ref[3 * BAND :, :]
        for f in range(3):
            band = slice(f * BAND, (f + 1) * BAND)
            out[band, :] = jnp.where(level < wets[f][place : place + 1], ref[band, :], 0.0)


def surface(levels, col, row, packed):
    rows, cols = levels.shape
    rim = tuple(struct(*value.shape) for value in packed[:4])
    return pl.pallas_call(
        surface_kernel,
        out_shape=(struct(3, rows, cols),) + (struct(rows, cols),) * 3 + rim,
        in_specs=[whole()] * 8,
        out_specs=(whole(),) * 8,
        compiler_params=params(4),
        cost_estimate=cost(1.5),
        name="surface",
    )(levels, col, row, *packed)


def corner_kernel(north_ref, south_ref, east_ref, west_ref, north_out_ref, south_out_ref):
    spot = row_ids(north_ref.shape) == 3 * BAND + 1
    last = east_ref.shape[0] - 1
    corner = jnp.broadcast_to(east_ref[last:, :], north_ref.shape)
    north_out_ref[...] = jnp.where(spot, corner, north_ref[...])
    corner = jnp.broadcast_to(west_ref[:1, :], south_ref.shape)
    south_out_ref[...] = jnp.where(spot, corner, south_ref[...])


def corners(north, south, halo_e, halo_w):
    return pl.pallas_call(
        corner_kernel,
        out_shape=(struct(*north.shape),) * 2,
        in_specs=[whole()] * 4,
        out_specs=(whole(),) * 2,
        compiler_params=params(4),
        cost_estimate=cost(0.3),
        name="corners",
    )(north, south, halo_e, halo_w)


def adjoint_kernel(
    step,
    done,
    depth,
    total_rows,
    wet_c_ref,
    wet_u_ref,
    wet_v_ref,
    mix_ref,
    hw_ref,
    he_ref,
    hn_ref,
    hs_ref,
    old_refs,
    u_ref,
    v_ref,
    t_ref,
    gu_ref,
    gv_ref,
    gt_ref,
    state_ref,
    mix_n_ref,
    mix_s_ref,
    keep_ref,
    cor_ref,
    a_ref,
    b_ref,
    c_ref,
):
    rows, cols = mix_ref.shape
    at = pl.program_id(0)
    half = depth // 2
    first = depth - (done + at + 1) * step
    pad = GROUP
    cor_step = 0.25 * time_step * coriolis_base / total_rows
    slope_u = 0.5 * time_step * zonal_slope
    slope_v = 0.5 * time_step * north_slope
    weight = time_step * gravity_scale
    before_y, after_y = (has_before("gy"), has_after("gy"))

    @pl.when(at == 0)
    def _():
        shape = (rows, cols)
        lane = lane_ids(shape)
        row = row_ids(shape)
        start = lax.axis_index("gy") * rows
        lines = (row + start).astype(F32)
        cor = (0.25 * time_step * coriolis_base) * (0.5 + (lines + 0.5) / total_rows)
        cor_n = (0.25 * time_step * coriolis_base) * (0.5 + (lines + 1.5) / total_rows)
        cor_s = (0.25 * time_step * coriolis_base) * (0.5 + (lines - 0.5) / total_rows)
        cor_ref[...] = cor
        mix = mix_ref[...]
        keep_ref[...] = 1.0 - 4.0 * mix
        mix_n_ref[...] = jnp.where(
            row == rows - 1,
            jnp.broadcast_to(jnp.where(after_y, hn_ref[3 * BAND : 3 * BAND + 1, :], 0.0), shape),
            pltpu.roll(mix, rows - 1, 0),
        )
        mix_s_ref[...] = jnp.where(
            row == 0,
            jnp.broadcast_to(jnp.where(before_y, hs_ref[3 * BAND : 3 * BAND + 1, :], 0.0), shape),
            pltpu.roll(mix, 1, 0),
        )
        if old_refs:
            state_ref[...] = old_refs[0][...]
            return
        east = jnp.where(has_after("gx"), he_ref[...], 0.0)
        corner = hs_ref[3 * BAND + 1 : 3 * BAND + 2, :]
        corner = jnp.where(has_after("gx") & before_y, corner, 0.0)
        kind = lax.rem(lane + cols - 1, cols) // BAND
        mixed = east * jnp.broadcast_to(east[:, 3 * BAND + 1 : 3 * BAND + 2], shape)
        below = jnp.where(
            row == 0,
            jnp.broadcast_to(corner, shape),
            pltpu.roll(east, 1, 0),
        )
        turned = cor * east + cor_s * below
        total = jnp.where(kind == 0, east, 0.0)
        reach = 1
        while reach < depth:
            total = total + pltpu.roll(total, cols - reach, 1)
            reach *= 2
        from_e = (
            mixed
            + jnp.where(kind == 1, pltpu.roll(turned, BAND, 1), 0.0)
            + jnp.where(kind == 2, pltpu.roll(weight * total, 2 * BAND, 1), 0.0)
        )
        west = jnp.where(has_before("gx"), hw_ref[...], 0.0)
        corner = hn_ref[3 * BAND + 1 : 3 * BAND + 2, :]
        corner = jnp.where(has_before("gx") & after_y, corner, 0.0)
        kind = lane // BAND
        mixed = west * jnp.broadcast_to(west[:, 3 * BAND : 3 * BAND + 1], shape)
        above = jnp.where(
            row == rows - 1,
            jnp.broadcast_to(corner, shape),
            pltpu.roll(west, rows - 1, 0),
        )
        turned = cor * west + cor_n * above
        from_w = mixed - jnp.where(
            kind == 0,
            pltpu.roll(turned, cols - BAND, 1) + pltpu.roll(slope_u * west, cols - 2 * BAND, 1),
            0.0,
        )
        both = jnp.concatenate([from_e, from_w], axis=1)
        source = row_ids((2 * cols, 2 * cols))
        place = lane_ids((2 * cols, 2 * cols))
        part = place // cols
        spot = lax.rem(place, cols)
        pair = spot // 2
        slot = BAND * (pair // half) + part * half + lax.rem(pair, half)
        wanted = jnp.where(lax.rem(spot, 2) == 0, slot + 1, slot + cols)
        moves = jnp.where((source == wanted) & (pair < 3 * half), 1.0, 0.0).astype(BF16)
        moved = jnp.zeros((rows, 2 * cols), F32)
        for _ in range(3):
            high = both.astype(BF16)
            both = both - high.astype(F32)
            moved = moved + jnp.dot(high, moves, preferred_element_type=F32)
        state_ref[0] = moved[:, :cols]
        state_ref[1] = moved[:, cols:]
        state_ref[2] = jnp.zeros(shape, F32)
        state_ref[3] = jnp.zeros(shape, F32)

    fields = (
        (u_ref, wet_u_ref, a_ref),
        (v_ref, wet_v_ref, b_ref),
        (t_ref, wet_c_ref, c_ref),
    )

    def mask(i, carry):
        base = pl.multiple_of(i * 2 * GROUP, 2 * GROUP)
        here = pl.ds(base, 2 * GROUP)
        there = pl.ds(pl.multiple_of(base + pad, GROUP), 2 * GROUP)
        wets = [wet[here, :] for _, wet, _ in fields]
        for k in range(step):
            level = (first + k).astype(F32)
            for f, (ref, _, out) in enumerate(fields):
                out[k, there, :] = jnp.where(level < wets[f], ref[k, here, :], 0.0)
        return carry

    lax.fori_loop(0, rows // (2 * GROUP), mask, 0, unroll=8)
    for k in range(step):
        for f, (_, _, out) in enumerate(fields):
            slot = BAND * f + first + k
            out[k, pad - 1 : pad, :] = jnp.where(before_y, hs_ref[pl.ds(slot, 1), :], 0.0)
            out[k, pad + rows : pad + rows + 1, :] = jnp.where(
                after_y, hn_ref[pl.ds(slot, 1), :], 0.0
            )

    chunk = 2 * GROUP
    lane = lane_ids((chunk, cols))
    is_east = lane == cols - 1
    is_west = lane == 0
    part = (first >= half).astype(jnp.int32)

    def body(i, carry):
        base = pl.multiple_of(i * chunk, chunk)
        here = pl.ds(base, chunk)
        center = pl.ds(base + pad, chunk)
        north = pl.ds(base + pad + 1, chunk)
        south = pl.ds(base + pad - 1, chunk)
        mix = mix_ref[here, :]
        mix_n = mix_n_ref[here, :]
        mix_s = mix_s_ref[here, :]
        keep = keep_ref[here, :]
        cor = cor_ref[here, :]
        cor_n = cor + cor_step
        cor_s = cor - cor_step
        edges = state_ref[part, here, :]
        sum_a = state_ref[2, here, :]
        sum_d = state_ref[3, here, :]
        for k in reversed(range(step)):
            inner = first + k - part * half

            def both_sides(west, east, f, inner=inner):
                edge = pltpu.roll(edges, 2 * cols - 1 - 2 * (f * half + inner), 1)
                return jnp.where(is_west, edge, pltpu.roll(west, 1, 1)) + jnp.where(
                    is_east, edge, pltpu.roll(east, cols - 1, 1)
                )

            a = a_ref[k, center, :]
            a_n = a_ref[k, north, :]
            a_s = a_ref[k, south, :]
            b = b_ref[k, center, :]
            b_n = b_ref[k, north, :]
            b_s = b_ref[k, south, :]
            c = c_ref[k, center, :]
            c_n = c_ref[k, north, :]
            c_s = c_ref[k, south, :]
            mix_a = mix * a
            turn_b = cor * b + cor_n * b_n + slope_u * c
            gu_ref[k, here, :] = (
                keep * a
                + (mix_n * a_n + mix_s * a_s)
                - turn_b
                + both_sides(mix_a - turn_b, mix_a, 0)
            )
            mix_b = mix * b
            turn_a = cor * a + cor_s * a_s
            gv_ref[k, here, :] = (
                keep * b
                + (mix_n * b_n + mix_s * b_s)
                + (turn_a - slope_v * (c + c_s))
                + both_sides(mix_b, mix_b + turn_a, 1)
            )
            mix_c = mix * c
            sum_a = sum_a + weight * a
            sum_d = sum_d + weight * (b - b_n)
            gt_ref[k, here, :] = (
                keep * c
                + (mix_n * c_n + mix_s * c_s)
                - (sum_a + sum_d)
                + both_sides(mix_c, mix_c + sum_a, 2)
            )
        state_ref[2, here, :] = sum_a
        state_ref[3, here, :] = sum_d
        return carry

    lax.fori_loop(0, rows // chunk, body, 0, unroll=rows // chunk)


def adjoint(planes, halos, cots, after, total_rows, earlier=None):
    depth, rows, cols = cots[0].shape
    step = 5
    first = depth // (3 * step)
    done, steps = (0, first) if earlier is None else (first, depth // step - first)
    plane = full(rows, cols)
    top = depth // step - 1 - done
    block = pl.BlockSpec((step, rows, cols), lambda i: (top - i, 0, 0))
    grads, state = ((), ()) if earlier is None else earlier
    n_planes = len(planes) + len(halos)
    n_state = len(state)
    kept = (4, rows, cols)

    def kernel(*refs):
        front, refs = refs[:n_planes], refs[n_planes:]
        old, refs = refs[:n_state], refs[n_state:]
        ins, refs = refs[:3], refs[3 + 1 + len(grads) :]
        adjoint_kernel(step, done, depth, total_rows, *front, old, *ins, *refs)

    padded = pltpu.VMEM((step, rows + 2 * GROUP, cols), F32)
    aliases = {n_planes + n_state + 4 + i: i for i in range(len(grads))}
    result = pl.pallas_call(
        kernel,
        grid=(steps,),
        out_shape=(struct(depth, rows, cols),) * 3 + (struct(*kept),),
        in_specs=[plane] * len(planes)
        + [full(*halo.shape) for halo in halos]
        + [full(*kept)] * n_state
        + [block] * 3
        + [anywhere()] * (1 + len(grads)),
        out_specs=(block,) * 3 + (full(*kept),),
        scratch_shapes=[pltpu.VMEM((rows, cols), F32)] * 4 + [padded] * 3,
        input_output_aliases=aliases,
        compiler_params=params(16),
        cost_estimate=cost(3.0 * steps),
        name="adjoint",
    )(*planes, *halos, *state, *cots, after, *grads)
    return result[:3], result[3:]


def halves(value):
    high = value.astype(BF16)
    return high, (value - high.astype(F32)).astype(BF16)


def product(blocks, fields, field_first):
    high = [h for h, _ in blocks], [h for h, _ in fields]
    low = [l for _, l in blocks], [l for _, l in fields]
    left = jnp.concatenate(high[0] + low[0] + high[0], axis=1)
    if field_first:
        right = jnp.concatenate(high[1] + high[1] + low[1], axis=1)
        return lax.dot_general(
            right, left, (((1,), (1,)), ((), ())), preferred_element_type=F32
        )
    right = jnp.concatenate(high[1] + high[1] + low[1], axis=0)
    return jnp.dot(left, right, preferred_element_type=F32)


def zonal_kernel(pattern_ref, blocks_ref, field_ref, after_ref, out_ref, high_ref, low_ref):
    for tile in range(field_ref.shape[0]):
        high_ref[tile], low_ref[tile] = halves(field_ref[tile])
    for r in range(blocks_ref.shape[0]):
        entries = range(blocks_ref.shape[1])
        picked = [pattern_ref[r, j] for j in entries]
        out_ref[r] = product(
            [halves(blocks_ref[r, j]) for j in entries],
            [(high_ref[p], low_ref[p]) for p in picked],
            True,
        )


def zonal(pattern, blocks, field, after):
    return pl.pallas_call(
        zonal_kernel,
        out_shape=struct(*field.shape),
        in_specs=[smem()] + [whole()] * 2 + [anywhere()],
        out_specs=whole(),
        scratch_shapes=[pltpu.VMEM(field.shape, BF16)] * 2,
        compiler_params=params(6),
        cost_estimate=cost(2.0),
        name="zonal",
    )(pattern, blocks, field, after)


def meridional_kernel(pattern_ref, blocks_ref, field_refs, out_ref, high_ref, low_ref):
    _, block, _ = high_ref.shape
    _, rows, cols = field_refs[0].shape
    chunk = out_ref.shape[1] // 3
    mine = rows // block
    me = lax.axis_index("gy")
    for m, ref in enumerate(field_refs):
        first = (me ^ m) * mine
        for h in range(mine):
            here = slice(h * block, (h + 1) * block)
            value = jnp.concatenate([ref[c, here, :] for c in range(3)], axis=1)
            high_ref[first + h], low_ref[first + h] = halves(value)
    entries = range(blocks_ref.shape[1])
    for h in range(mine):
        r = me * mine + h
        picked = [pattern_ref[r, j] for j in entries]
        result = product(
            [halves(blocks_ref[r, j]) for j in entries],
            [(high_ref[p], low_ref[p]) for p in picked],
            False,
        )
        for line in range(0, block, chunk):
            part = (h * block + line) // chunk
            for c in range(3):
                out_ref[part, c * chunk : (c + 1) * chunk, :] = result[
                    line : line + chunk, c * cols : (c + 1) * cols
                ]


def meridional(pattern, blocks, fields, parts):
    n = len(fields)
    _, rows, cols = fields[0].shape
    tiles, _, block, _ = blocks.shape

    def kernel(pattern_ref, blocks_ref, *refs):
        meridional_kernel(pattern_ref, blocks_ref, refs[:n], *refs[n:])

    return pl.pallas_call(
        kernel,
        out_shape=struct(parts, 3 * rows // parts, cols),
        in_specs=[smem()] + [whole()] * (1 + n),
        out_specs=whole(),
        scratch_shapes=[pltpu.VMEM((tiles, block, 3 * cols), BF16)] * 2,
        compiler_params=params(4 + n),
        cost_estimate=cost(2.0),
        name="meridional",
    )(pattern, blocks, *fields)


def finish_kernel(field_ref, after_ref, out_ref):
    parts, height, cols = field_ref.shape
    chunk = height // 3
    for part in range(parts):
        for c in range(3):
            out_ref[c, part * chunk : (part + 1) * chunk, :] = field_ref[
                part, c * chunk : (c + 1) * chunk, :
            ]


def finish(field, after):
    parts, height, cols = field.shape
    return pl.pallas_call(
        finish_kernel,
        out_shape=struct(3, parts * height // 3, cols),
        in_specs=[whole(), anywhere()],
        out_specs=whole(),
        compiler_params=params(4),
        cost_estimate=cost(0.7),
        name="finish",
    )(field, after)


def shards(cot_u, cot_v, cot_t, levels, mixing, pattern_x, blocks_x, pattern_y, blocks_y):
    depth, rows, cols = cot_u.shape
    nx, ny = (lax.axis_size("gx"), lax.axis_size("gy"))
    up_x = [(i, (i + 1) % nx) for i in range(nx)]
    down_x = [(j, i) for i, j in up_x]
    up_y = [(i, (i + 1) % ny) for i in range(ny)]
    down_y = [(j, i) for i, j in up_y]

    mixing = pltpu.with_memory_space_constraint(mixing, pltpu.HBM)
    cots = tuple(pltpu.with_memory_space_constraint(c, pltpu.HBM) for c in (cot_u, cot_v, cot_t))
    level_col, level_row = edges(levels)
    level_col = lax.ppermute(level_col, "gx", up_x)
    level_row = lax.ppermute(level_row, "gy", up_y)
    packed = rims(mixing, cots)
    field, wet_c, wet_u, wet_v, east, west, north, south = surface(
        levels, level_col, level_row, packed
    )
    halo_w = lax.ppermute(east, "gx", up_x)
    halo_e = lax.ppermute(west, "gx", down_x)
    tiles = {0: field}
    bit = ny // 2
    while bit:
        tiles[bit] = lax.ppermute(field, "gy", [(i, i ^ bit) for i in range(ny)])
        bit //= 2
    own = [m for m in tiles if m]
    *received, halo_w, halo_e = lax.optimization_barrier(
        (*(tiles[m] for m in own), halo_w, halo_e)
    )
    tiles.update(zip(own, received))
    bit = ny // 4
    while bit:
        for m in sorted(m for m in tiles if m and m % (2 * bit) == 0):
            tiles[m ^ bit] = lax.ppermute(tiles[m], "gy", [(i, i ^ bit) for i in range(ny)])
        bit //= 2
    north, south = corners(north, south, halo_e, halo_w)
    halo_s = lax.ppermute(north, "gy", up_y)
    halo_n = lax.ppermute(south, "gy", down_y)
    mixed = meridional(pattern_y, blocks_y, [tiles[m] for m in range(ny)], nx)
    mixed, halo_s, halo_n = lax.optimization_barrier((mixed, halo_s, halo_n))
    lines = lax.all_to_all(mixed, "gx", 0, 0)
    planes = (wet_c, wet_u, wet_v, mixing)
    halos = (halo_w, halo_e, halo_n, halo_s)
    grads, state = adjoint(planes, halos, cots, mixed, rows * ny)
    turned = zonal(pattern_x, blocks_x, lines, state[0])
    back = lax.all_to_all(turned, "gx", 0, 0)
    grads = tuple(pltpu.with_memory_space_constraint(g, pltpu.HBM) for g in grads)
    grads, token = adjoint(planes, halos, cots, turned, rows * ny, (grads, state))
    return (*grads, finish(back, token[0]))


def solution(mesh):
    grid = P(None, "gy", "gx")
    flat = P("gy", "gx")
    return jax.shard_map(
        shards,
        mesh=mesh,
        in_specs=(grid, grid, grid, flat, flat, P(), P(), P(), P()),
        out_specs=(grid, grid, grid, grid),
        check_vma=False,
    )
```

time: 71.9 us -> 65.5 us (0.911)
  waiting for transfers between devices: 14.7 us -> 8.97 us
  Pallas kernels: 34.5 us -> 32.4 us
  local copies, waits for them, and re-layouts: 1.98 us -> 2.72 us
    ppermute x1, waiting for transfers between devices: 0.04 us -> 3.28 us  [shards(): halo_w = lax.ppermute(east, 'gx', up_x)]
    ppermute x1, waiting for transfers between devices: 3.03 us -> 0.01 us  [shards(): level_row = lax.ppermute(level_row, 'gy', up_y)]
    pallas_call x6 -> x7, Pallas kernels: 16.5 us -> 13.6 us  [the longest x1 6.7 us: rims(): pl.pallas_call(functools.partial(rim_kernel, step), out_shape=(struct(row...]
    all_to_all x3 -> x2, starting transfers between devices: 11 us -> 8.53 us  [the longest x1 4.89 us: shards(): lines = lax.all_to_all(mixed, 'gx', 0, 0)]
    all_to_all x3 -> x2, waiting for transfers between devices: 5.33 us -> 3.12 us  [the longest x1 2.43 us: shards(): lines = lax.all_to_all(mixed, 'gx', 0, 0)]
    ppermute x1, waiting for transfers between devices: 2.2 us -> 0.01 us  [shards(): halo_s = lax.ppermute(north, 'gy', up_y)]
    ppermute x0 -> x3, starting transfers between devices: none -> 2.07 us  [the longest x2 2.07 us: shards(): tiles[bit] = lax.ppermute(field, 'gy', [(i, i ^ bit) for i in range(ny)])]
    ppermute x1, waiting for transfers between devices: 1.64 us -> 0.01 us  [shards(): level_col = lax.ppermute(level_col, 'gx', up_x)]
  transfers between devices with their start and end apart: 9 -> 11, of which waited for: 8 -> 5; matrix products, arithmetic and copies ran while one was open for 0% -> 0% of each run, Pallas kernels for 29% -> 44%
where the time goes in v2:
time: 65.5 us; the launch traced here: 64.9 us
  Pallas kernels  32.4 us (49%)
  starting transfers between devices  20.1 us (31%)
  waiting for transfers between devices  8.97 us (14%)
  local copies, waits for them, and re-layouts  2.72 us (4%)
  between operations  0.75 us (1%)
    pallas_call x2, Pallas kernels, adjoint(): pl.pallas_call(kernel, grid=(steps,), out_shape=(struct(depth, rows, cols...  18.8 us
    pallas_call x1, Pallas kernels, rims(): pl.pallas_call(functools.partial(rim_kernel, step), out_shape=(struct(row...  6.7 us
    all_to_all x1, starting transfers between devices, shards(): lines = lax.all_to_all(mixed, 'gx', 0, 0)  4.89 us
    all_to_all x1, starting transfers between devices, shards(): back = lax.all_to_all(turned, 'gx', 0, 0)  3.64 us
    ppermute x1, waiting for transfers between devices, shards(): halo_w = lax.ppermute(east, 'gx', up_x)  3.28 us
    ppermute x1, starting transfers between devices, shards(): halo_e = lax.ppermute(west, 'gx', down_x)  3.2 us
    ppermute x1, starting transfers between devices, shards(): level_col = lax.ppermute(level_col, 'gx', up_x)  3.02 us
    unnamed x26, local copies, waits for them, and re-layouts  2.72 us
  transfers between devices with their start and end apart: 11, of which 5 were waited for; matrix products, arithmetic and copies ran while one was open for 0% of the time, Pallas kernels for 44%

profile of v2, /device:TPU:0, one launch (start us, length us, event | category | flops | bytes accessed | tf_op | source)
XLA Modules:
  0.0 64.9 jit_solution(10283702323634319202)
XLA Ops:
  0.6 0.0 copy-start.2
  0.6 0.9 %copy-done.2 = s32[256,128]{1,0:T(8,128)S(1)} copy-done((s32[256,128]{1,0:T(8,128)S(1)}, s32[256,128]{1,0:T(8,128)}, u32[]{:S(2)}) %copy-start.2) | copy-done | bytes 131096
  1.5 0.1 edges.1
  1.6 3.0 %collective-permute-start = (f32[8,256]{1,0:T(8,128)S(1)}, f32[8,256]{1,0:T(8,128)S(1)}, u32[]{:S(2)}, u32[]{:S(2)}) collective-permute-start(f32[8,256]{1,0:T(8,128)S(1)} %get-tuple-element.36), channel_id=1, source_target_pairs={{0,4},{4,8},{8,12},{12,16},{16,20},{20,24},{24,28},{28,0},{1,5},{5... | collective-permute-start | bytes 24584 | tf_op jit(solution)/shard_map/ppermute | solution.py:664
  4.7 0.0 collective-permute-start.1
  4.7 6.7 %rims.1 = (f32[256,128]{1,0:T(8,128)S(1)}, f32[256,128]{1,0:T(8,128)S(1)}, f32[104,128]{1,0:T(8,128)S(1)}, f32[104,128]{1,0:T(8,128)S(1)}, f32[3,256,128]{2,1,0:T(8,128)S(1)}) custom-call(f32[256,128]{1,0:T(8,128)} %refs_3_.3, f32[30,256,128]{2,1,0:T(8,128)} %refs_9_.3, f32[30,256,128]{2,1,0:T(8,128)} %refs_10_.3, f32[30,256,128]{2,1,0:T(8,128)} %refs_11_.1), custom_call_target="tpu_custom_call" | custom-call | flops 6000000 | bytes 18000000 | tf_op jit(solution)/shard_map/rims/pallas_call | solution.py:173
  11.4 0.0 copy-start.11
  11.4 0.0 collective-permute-done.1.row_ref
  11.4 0.0 collective-permute-done.col_ref
  11.4 0.0 copy-done.3
  11.4 0.6 surface.1
  12.0 1.5 %collective-permute-start.3 = (f32[3,256,128]{2,1,0:T(8,128)S(1)}, f32[3,256,128]{2,1,0:T(8,128)S(1)}, u32[]{:S(2)}, u32[]{:S(2)}) collective-permute-start(f32[3,256,128]{2,1,0:T(8,128)S(1)} %get-tuple-element.46.refs_0_), channel_id=1, source_target_pairs={{0,1},{1,0},{2,3},{3,2},{4,5},{5,4},{6,7},{7,6},{8,9},{9,8},{10,11... | collective-permute-start | bytes 1179656 | tf_op jit(solution)/shard_map/ppermute | solution.py:675
  13.5 0.5 collective-permute-start.2
  14.1 1.5 %collective-permute-start.4 = (f32[256,128]{1,0:T(8,128)S(1)}, f32[256,128]{1,0:T(8,128)S(1)}, u32[]{:S(2)}, u32[]{:S(2)}) collective-permute-start(f32[256,128]{1,0:T(8,128)S(1)} %get-tuple-element.47), channel_id=1, source_target_pairs={{0,4},{4,8},{8,12},{12,16},{16,20},{20,24},{24,28},{28,0},{1,5},{5... | collective-permute-start | bytes 393224 | tf_op jit(solution)/shard_map/ppermute | solution.py:670
  15.6 3.2 %collective-permute-start.5 = (f32[256,128]{1,0:T(8,128)S(1)}, f32[256,128]{1,0:T(8,128)S(1)}, u32[]{:S(2)}, u32[]{:S(2)}) collective-permute-start(f32[256,128]{1,0:T(8,128)S(1)} %get-tuple-element.48), channel_id=1, source_target_pairs={{4,0},{8,4},{12,8},{16,12},{20,16},{24,20},{28,24},{0,28},{5,1},{9... | collective-permute-start | bytes 393224 | tf_op jit(solution)/shard_map/ppermute | solution.py:671
  18.8 3.3 %collective-permute-done.4.west_ref.refs_4_ = f32[256,128]{1,0:T(8,128)S(1)} collective-permute-done((f32[256,128]{1,0:T(8,128)S(1)}, f32[256,128]{1,0:T(8,128)S(1)}, u32[]{:S(2)}, u32[]{:S(2)}) %collective-permute-start.4) | collective-permute-done | bytes 131104 | tf_op jit(solution)/shard_map/ppermute | solution.py:670
  22.1 1.3 %collective-permute-done.5.east_ref.refs_5_ = f32[256,128]{1,0:T(8,128)S(1)} collective-permute-done((f32[256,128]{1,0:T(8,128)S(1)}, f32[256,128]{1,0:T(8,128)S(1)}, u32[]{:S(2)}, u32[]{:S(2)}) %collective-permute-start.5) | collective-permute-done | bytes 131104 | tf_op jit(solution)/shard_map/ppermute | solution.py:671
  23.3 0.0 collective-permute-done.3.refs_1_
  23.4 1.3 %collective-permute-done.2.refs_2_ = f32[3,256,128]{2,1,0:T(8,128)S(1)} collective-permute-done((f32[3,256,128]{2,1,0:T(8,128)S(1)}, f32[3,256,128]{2,1,0:T(8,128)S(1)}, u32[]{:S(2)}, u32[]{:S(2)}) %collective-permute-start.2) | collective-permute-done | bytes 393248 | tf_op jit(solution)/shard_map/ppermute | solution.py:675
  24.6 0.0 collective-permute-start.6
  24.6 0.6 corners.1
  25.3 0.5 collective-permute-start.7
  25.8 1.2 %collective-permute-start.8 = (f32[104,128]{1,0:T(8,128)}, f32[104,128]{1,0:T(8,128)S(1)}, u32[]{:S(2)}, u32[]{:S(2)}) collective-permute-start(f32[104,128]{1,0:T(8,128)} %get-tuple-element.56), channel_id=1, source_target_pairs={{1,0},{2,1},{3,2},{0,3},{5,4},{6,5},{7,6},{4,7},{9,8},{10,9},{11,1... | collective-permute-start | bytes 159752 | tf_op jit(solution)/shard_map/ppermute | solution.py:689
  27.0 0.0 copy-done.10
  27.0 0.1 copy.16.pattern_ref
  27.1 0.0 collective-permute-done.6.refs_3_
  27.1 0.0 copy-done
  27.1 2.5 %meridional.1.refs_11_ = f32[8,96,128]{2,1,0:T(8,128)} custom-call(s32[8,3]{1,0:T(8,128)S(1)} %copy.16.pattern_ref, f32[8,3,128,128]{3,2,1,0:T(8,128)S(1)} %copy-done, f32[3,256,128]{2,1,0:T(8,128)S(1)} %get-tuple-element.46.refs_0_, f32[3,256,128]{2,1,0:T(8,128)S(1)} %collective-permute-done.3.refs_1_, f32[3,256,128]{2,1,0:T(8,128)S(1)} %collective-permute-done.2.refs_2_, ...), custom_call_target="tpu_custom_call" | custom-call | flops 2000000 | bytes 6000000 | tf_op jit(solution)/shard_map/meridional/pallas_call | solution.py:618
  29.6 0.0 collective-permute-done.7.refs_7_
  29.6 0.0 collective-permute-done.8.refs_6_
  29.7 0.0 copy-start.7
  29.7 4.9 %all-to-all-start = ((f32[8,96,128]{2,1,0:T(8,128)}), f32[8,96,128]{2,1,0:T(8,128)S(1)}, u32[]{:S(2)}, u32[]{:S(2)}) async-start(f32[8,96,128]{2,1,0:T(8,128)} %meridional.1.refs_11_), calls=%async_computation | async-start | bytes 786432 | tf_op jit(solution)/shard_map/all_to_all | solution.py:692
  34.6 0.0 copy-done.11
  34.6 0.1 copy.17.pattern_ref
  34.6 0.0 copy-done.4
  34.6 0.0 copy-done.7
  34.7 0.8 %copy-done.5 = f32[104,128]{1,0:T(8,128)S(1)} copy-done((f32[104,128]{1,0:T(8,128)S(1)}, f32[104,128]{1,0:T(8,128)}, u32[]{:S(2)}) %copy-start.5) | copy-done | bytes 53272
  35.5 0.8 %copy-done.8 = f32[104,128]{1,0:T(8,128)S(1)} copy-done((f32[104,128]{1,0:T(8,128)S(1)}, f32[104,128]{1,0:T(8,128)}, u32[]{:S(2)}) %copy-start.8) | copy-done | bytes 53272
  36.3 7.7 %adjoint.2 = (f32[30,256,128]{2,1,0:T(8,128)}, f32[30,256,128]{2,1,0:T(8,128)}, f32[30,256,128]{2,1,0:T(8,128)}, f32[4,256,128]{2,1,0:T(8,128)S(1)}) custom-call(f32[256,128]{1,0:T(8,128)S(1)} %get-tuple-element.43.refs_0_, f32[256,128]{1,0:T(8,128)S(1)} %get-tuple-element.44.refs_1_, f32[256,128]{1,0:T(8,128)S(1)} %get-tuple-element.45.refs_2_, ...), custom_call_target="tpu_custom_call" | custom-call | flops 6000000 | bytes 18000000 | tf_op jit(solution)/shard_map/adjoint/pallas_call | solution.py:518
  44.0 2.4 %all-to-all-done.field_ref = f32[8,96,128]{2,1,0:T(8,128)S(1)} async-done(((f32[8,96,128]{2,1,0:T(8,128)}), f32[8,96,128]{2,1,0:T(8,128)S(1)}, u32[]{:S(2)}, u32[]{:S(2)}) %all-to-all-start) | async-done | bytes 393248 | tf_op jit(solution)/shard_map/all_to_all | solution.py:692
  46.4 0.0 copy-done.1
  46.4 2.3 %zonal.1.refs_12_ = f32[8,96,128]{2,1,0:T(8,128)} custom-call(s32[8,3]{1,0:T(8,128)S(1)} %copy.17.pattern_ref, f32[8,3,128,128]{3,2,1,0:T(8,128)S(1)} %copy-done.1, f32[8,96,128]{2,1,0:T(8,128)S(1)} %all-to-all-done.field_ref, f32[4,256,128]{2,1,0:T(8,128)S(1)} %get-tuple-element.60.after_ref.refs_8_), custom_call_target="tpu_custom_call" | custom-call | flops 2000000 | bytes 6000000 | tf_op jit(solution)/shard_map/zonal/pallas_call | solution.py:569
  48.7 3.6 %all-to-all-start.1 = ((f32[8,96,128]{2,1,0:T(8,128)}), f32[8,96,128]{2,1,0:T(8,128)S(1)}, u32[]{:S(2)}, u32[]{:S(2)}) async-start(f32[8,96,128]{2,1,0:T(8,128)} %zonal.1.refs_12_), calls=%async_computation.1 | async-start | bytes 786432 | tf_op jit(solution)/shard_map/all_to_all | solution.py:697
  52.4 0.0 copy-done.6
  52.4 0.0 copy-done.9
  52.4 11.1 %adjoint.3 = (f32[30,256,128]{2,1,0:T(8,128)}, f32[30,256,128]{2,1,0:T(8,128)}, f32[30,256,128]{2,1,0:T(8,128)}, f32[4,256,128]{2,1,0:T(8,128)S(1)}) custom-call(f32[256,128]{1,0:T(8,128)S(1)} %get-tuple-element.43.refs_0_, f32[256,128]{1,0:T(8,128)S(1)} %get-tuple-element.44.refs_1_, ...), custom_call_target="tpu_custom_call", output_to_operand_aliasing={{0}: (13, {}), {1}: (14, {}), {2}: (15, {})} | custom-call | flops 12000000 | bytes 36000000 | tf_op jit(solution)/shard_map/adjoint/pallas_call | solution.py:518
  63.4 0.7 %all-to-all-done.1.field_ref = f32[8,96,128]{2,1,0:T(8,128)S(1)} async-done(((f32[8,96,128]{2,1,0:T(8,128)}), f32[8,96,128]{2,1,0:T(8,128)S(1)}, u32[]{:S(2)}, u32[]{:S(2)}) %all-to-all-start.1) | async-done | bytes 393248 | tf_op jit(solution)/shard_map/all_to_all | solution.py:697
  64.1 0.8 %finish.1 = f32[3,256,128]{2,1,0:T(8,128)} custom-call(f32[8,96,128]{2,1,0:T(8,128)S(1)} %all-to-all-done.1.field_ref, f32[4,256,128]{2,1,0:T(8,128)S(1)} %get-tuple-element.67.after_ref), custom_call_target="tpu_custom_call" | custom-call | flops 700000 | bytes 2100000 | tf_op jit(solution)/shard_map/finish/pallas_call | solution.py:642
  (9 shorter events, 0.0 us)
Async XLA Ops:
  0.6 0.9 %copy-start.2 = (s32[256,128]{1,0:T(8,128)S(1)}, s32[256,128]{1,0:T(8,128)}, u32[]{:S(2)}) copy-start(s32[256,128]{1,0:T(8,128)} %levels_ref.3) | copy-start | bytes 393220
  1.6 9.8 %collective-permute-start = (f32[8,256]{1,0:T(8,128)S(1)}, f32[8,256]{1,0:T(8,128)S(1)}, u32[]{:S(2)}, u32[]{:S(2)}) collective-permute-start(f32[8,256]{1,0:T(8,128)S(1)} %get-tuple-element.36), channel_id=1, source_target_pairs={{0,4},{4,8},{8,12},{12,16},{16,20},{20,24},{24,28},{28,0},{1,5},{5... | collective-permute-start | bytes 24584 | tf_op jit(solution)/shard_map/ppermute | solution.py:664
  4.7 6.8 %copy-start.3 = (s32[256,128]{1,0:T(8,128)S(1)}, s32[256,128]{1,0:T(8,128)}, u32[]{:S(2)}) copy-start(s32[256,128]{1,0:T(8,128)} %levels_ref.3) | copy-start | bytes 393220
  4.7 22.4 %copy-start.10 = (s32[8,3]{0,1:T(4,128)S(1)}, s32[8,3]{0,1:T(4,128)}, u32[]{:S(2)}) copy-start(s32[8,3]{0,1:T(4,128)} %param.16) | copy-start | bytes 292
  4.7 22.4 %copy-start = (f32[8,3,128,128]{3,2,1,0:T(8,128)S(1)}, f32[8,3,128,128]{3,2,1,0:T(8,128)}, u32[]{:S(2)}) copy-start(f32[8,3,128,128]{3,2,1,0:T(8,128)} %blocks_ref.2) | copy-start | bytes 4718596
  4.7 6.7 %collective-permute-start.1 = (f32[8,128]{1,0:T(8,128)S(1)}, f32[8,128]{1,0:T(8,128)S(1)}, u32[]{:S(2)}, u32[]{:S(2)}) collective-permute-start(f32[8,128]{1,0:T(8,128)S(1)} %get-tuple-element.37), channel_id=1, source_target_pairs={{0,1},{1,2},{2,3},{3,0},{4,5},{5,6},{6,7},{7,4},{8,9},{9,10},{10,1... | collective-permute-start | bytes 12296 | tf_op jit(solution)/shard_map/ppermute | solution.py:665
  11.4 23.2 %copy-start.11 = (s32[8,3]{0,1:T(4,128)S(1)}, s32[8,3]{0,1:T(4,128)}, u32[]{:S(2)}) copy-start(s32[8,3]{0,1:T(4,128)} %param.14) | copy-start | bytes 292
  12.0 11.4 %collective-permute-start.3 = (f32[3,256,128]{2,1,0:T(8,128)S(1)}, f32[3,256,128]{2,1,0:T(8,128)S(1)}, u32[]{:S(2)}, u32[]{:S(2)}) collective-permute-start(f32[3,256,128]{2,1,0:T(8,128)S(1)} %get-tuple-element.46.refs_0_), channel_id=1, source_target_pairs={{0,1},{1,0},{2,3},{3,2},{4,5},{5,4},{6,7},{7,6},{8,9},{9,8},{10,11... | collective-permute-start | bytes 1179656 | tf_op jit(solution)/shard_map/ppermute | solution.py:675
  13.5 11.1 %collective-permute-start.2 = (f32[3,256,128]{2,1,0:T(8,128)S(1)}, f32[3,256,128]{2,1,0:T(8,128)S(1)}, u32[]{:S(2)}, u32[]{:S(2)}) collective-permute-start(f32[3,256,128]{2,1,0:T(8,128)S(1)} %get-tuple-element.46.refs_0_), channel_id=1, source_target_pairs={{0,2},{1,3},{2,0},{3,1},{4,6},{5,7},{6,4},{7,5},{8,10},{9,11},{10,... | collective-permute-start | bytes 1179656 | tf_op jit(solution)/shard_map/ppermute | solution.py:675
  14.1 8.0 %collective-permute-start.4 = (f32[256,128]{1,0:T(8,128)S(1)}, f32[256,128]{1,0:T(8,128)S(1)}, u32[]{:S(2)}, u32[]{:S(2)}) collective-permute-start(f32[256,128]{1,0:T(8,128)S(1)} %get-tuple-element.47), channel_id=1, source_target_pairs={{0,4},{4,8},{8,12},{12,16},{16,20},{20,24},{24,28},{28,0},{1,5},{5... | collective-permute-start | bytes 393224 | tf_op jit(solution)/shard_map/ppermute | solution.py:670
  15.6 7.8 %collective-permute-start.5 = (f32[256,128]{1,0:T(8,128)S(1)}, f32[256,128]{1,0:T(8,128)S(1)}, u32[]{:S(2)}, u32[]{:S(2)}) collective-permute-start(f32[256,128]{1,0:T(8,128)S(1)} %get-tuple-element.48), channel_id=1, source_target_pairs={{4,0},{8,4},{12,8},{16,12},{20,16},{24,20},{28,24},{0,28},{5,1},{9... | collective-permute-start | bytes 393224 | tf_op jit(solution)/shard_map/ppermute | solution.py:671
  24.6 2.5 %collective-permute-start.6 = (f32[3,256,128]{2,1,0:T(8,128)S(1)}, f32[3,256,128]{2,1,0:T(8,128)}, u32[]{:S(2)}, u32[]{:S(2)}) collective-permute-start(f32[3,256,128]{2,1,0:T(8,128)S(1)} %collective-permute-done.2.refs_2_), channel_id=1, source_target_pairs={{0,1},{1,0},{2,3},{3,2},{4,5},{5,4},{6,7},{7,6},{8,9},{9,8},{10,11... | collective-permute-start | bytes 1179656 | tf_op jit(solution)/shard_map/ppermute | solution.py:685
  25.3 4.4 %collective-permute-start.7 = (f32[104,128]{1,0:T(8,128)}, f32[104,128]{1,0:T(8,128)S(1)}, u32[]{:S(2)}, u32[]{:S(2)}) collective-permute-start(f32[104,128]{1,0:T(8,128)} %get-tuple-element.55), channel_id=1, source_target_pairs={{0,1},{1,2},{2,3},{3,0},{4,5},{5,6},{6,7},{7,4},{8,9},{9,10},{10,1... | collective-permute-start | bytes 159752 | tf_op jit(solution)/shard_map/ppermute | solution.py:688
  25.8 3.9 %collective-permute-start.8 = (f32[104,128]{1,0:T(8,128)}, f32[104,128]{1,0:T(8,128)S(1)}, u32[]{:S(2)}, u32[]{:S(2)}) collective-permute-start(f32[104,128]{1,0:T(8,128)} %get-tuple-element.56), channel_id=1, source_target_pairs={{1,0},{2,1},{3,2},{0,3},{5,4},{6,5},{7,6},{4,7},{9,8},{10,9},{11,1... | collective-permute-start | bytes 159752 | tf_op jit(solution)/shard_map/ppermute | solution.py:689
  29.6 5.0 %copy-start.4 = (f32[104,128]{1,0:T(8,128)}, f32[104,128]{1,0:T(8,128)S(1)}, u32[]{:S(2)}) copy-start(f32[104,128]{1,0:T(8,128)S(1)} %collective-permute-done.7.refs_7_) | copy-start | bytes 159748
  29.7 5.0 %copy-start.7 = (f32[104,128]{1,0:T(8,128)}, f32[104,128]{1,0:T(8,128)S(1)}, u32[]{:S(2)}) copy-start(f32[104,128]{1,0:T(8,128)S(1)} %collective-permute-done.8.refs_6_) | copy-start | bytes 159748
  29.7 16.7 %all-to-all-start = ((f32[8,96,128]{2,1,0:T(8,128)}), f32[8,96,128]{2,1,0:T(8,128)S(1)}, u32[]{:S(2)}, u32[]{:S(2)}) async-start(f32[8,96,128]{2,1,0:T(8,128)} %meridional.1.refs_11_), calls=%async_computation | async-start | bytes 786432 | tf_op jit(solution)/shard_map/all_to_all | solution.py:692
  34.6 0.8 %copy-start.5 = (f32[104,128]{1,0:T(8,128)S(1)}, f32[104,128]{1,0:T(8,128)}, u32[]{:S(2)}) copy-start(f32[104,128]{1,0:T(8,128)} %copy-done.4) | copy-start | bytes 159748
  35.5 0.8 %copy-start.8 = (f32[104,128]{1,0:T(8,128)S(1)}, f32[104,128]{1,0:T(8,128)}, u32[]{:S(2)}) copy-start(f32[104,128]{1,0:T(8,128)} %copy-done.7) | copy-start | bytes 159748
  36.3 10.1 %copy-start.1 = (f32[8,3,128,128]{3,2,1,0:T(8,128)S(1)}, f32[8,3,128,128]{3,2,1,0:T(8,128)}, u32[]{:S(2)}) copy-start(f32[8,3,128,128]{3,2,1,0:T(8,128)} %blocks_ref.3) | copy-start | bytes 4718596
  36.3 16.1 %copy-start.6 = (f32[104,128]{1,0:T(8,128)S(1)}, f32[104,128]{1,0:T(8,128)}, u32[]{:S(2)}) copy-start(f32[104,128]{1,0:T(8,128)} %copy-done.4) | copy-start | bytes 159748
  36.3 16.1 %copy-start.9 = (f32[104,128]{1,0:T(8,128)S(1)}, f32[104,128]{1,0:T(8,128)}, u32[]{:S(2)}) copy-start(f32[104,128]{1,0:T(8,128)} %copy-done.7) | copy-start | bytes 159748
  48.7 15.4 %all-to-all-start.1 = ((f32[8,96,128]{2,1,0:T(8,128)}), f32[8,96,128]{2,1,0:T(8,128)S(1)}, u32[]{:S(2)}, u32[]{:S(2)}) async-start(f32[8,96,128]{2,1,0:T(8,128)} %zonal.1.refs_12_), calls=%async_computation.1 | async-start | bytes 786432 | tf_op jit(solution)/shard_map/all_to_all | solution.py:697

commit v3 on v2

--- a/solution.py
+++ b/solution.py
@@ -540,16 +540,20 @@
 
 
 def product(blocks, fields, field_first):
-    high = [h for h, _ in blocks], [h for h, _ in fields]
-    low = [l for _, l in blocks], [l for _, l in fields]
-    left = jnp.concatenate(high[0] + low[0] + high[0], axis=1)
+    axis = 1 if field_first else 0
+    block_high, block_low = (jnp.concatenate([b[i] for b in blocks], axis=1) for i in range(2))
+    field_high, field_low = (jnp.concatenate([f[i] for f in fields], axis=axis) for i in range(2))
     if field_first:
-        right = jnp.concatenate(high[1] + high[1] + low[1], axis=1)
-        return lax.dot_general(
-            right, left, (((1,), (1,)), ((), ())), preferred_element_type=F32
-        )
-    right = jnp.concatenate(high[1] + high[1] + low[1], axis=0)
-    return jnp.dot(left, right, preferred_element_type=F32)
+        first, second = (field_high, field_low), (block_high, block_low)
+    else:
+        first, second = (block_high, block_low), (field_high, field_low)
+    dims = (((1,), (axis,)), ((), ()))
+    both = lax.dot_general(
+        jnp.concatenate(first, axis=0), second[0], dims, preferred_element_type=F32
+    )
+    last = lax.dot_general(first[0], second[1], dims, preferred_element_type=F32)
+    size = first[0].shape[0]
+    return both[:size] + (both[size:] + last)
 
 
 def zonal_kernel(pattern_ref, blocks_ref, field_ref, after_ref, out_ref, high_ref, low_ref):
@@ -671,9 +675,10 @@
     halo_e = lax.ppermute(west, "gx", down_x)
     tiles = {0: field}
     bit = ny // 2
-    while bit:
+    bit = 1
+    while bit < ny:
         tiles[bit] = lax.ppermute(field, "gy", [(i, i ^ bit) for i in range(ny)])
-        bit //= 2
+        bit *= 2
     own = [m for m in tiles if m]
     *received, halo_w, halo_e = lax.optimization_barrier(
         (*(tiles[m] for m in own), halo_w, halo_e)

time: 65.5 us -> 65.5 us (level)
    ppermute x2, waiting for transfers between devices: 1.27 us -> 0.11 us  [shards(): tiles[bit] = lax.ppermute(field, 'gy', [(i, i ^ bit) for i in range(ny)])]
    all_to_all x1, waiting for transfers between devices: 2.43 us -> 3.15 us  [shards(): lines = lax.all_to_all(mixed, 'gx', 0, 0)]
where the time goes in v3:
time: 65.5 us; the launch traced here: 64.9 us
  Pallas kernels  32.2 us (49%)
  starting transfers between devices  20.1 us (31%)
  waiting for transfers between devices  9.11 us (14%)
  local copies, waits for them, and re-layouts  2.72 us (4%)
  between operations  0.75 us (1%)
    pallas_call x2, Pallas kernels, adjoint(): pl.pallas_call(kernel, grid=(steps,), out_shape=(struct(depth, rows, cols...  18.8 us
    pallas_call x1, Pallas kernels, rims(): pl.pallas_call(functools.partial(rim_kernel, step), out_shape=(struct(row...  6.7 us
    all_to_all x1, starting transfers between devices, shards(): lines = lax.all_to_all(mixed, 'gx', 0, 0)  4.89 us
    ppermute x1, waiting for transfers between devices, shards(): halo_w = lax.ppermute(east, 'gx', up_x)  3.76 us
    all_to_all x1, starting transfers between devices, shards(): back = lax.all_to_all(turned, 'gx', 0, 0)  3.64 us
    ppermute x1, starting transfers between devices, shards(): halo_e = lax.ppermute(west, 'gx', down_x)  3.2 us
    all_to_all x1, waiting for transfers between devices, shards(): lines = lax.all_to_all(mixed, 'gx', 0, 0)  3.15 us
    ppermute x1, starting transfers between devices, shards(): level_col = lax.ppermute(level_col, 'gx', up_x)  3.02 us
  transfers between devices with their start and end apart: 11, of which 5 were waited for; matrix products, arithmetic and copies ran while one was open for 0% of the time, Pallas kernels for 44%

profile of v3, /device:TPU:0, one launch (start us, length us, event | category | flops | bytes accessed | tf_op | source)
XLA Modules:
  0.0 64.9 jit_solution(6358611898318183847)
XLA Ops:
  0.6 0.0 copy-start.2
  0.6 0.9 %copy-done.2 = s32[256,128]{1,0:T(8,128)S(1)} copy-done((s32[256,128]{1,0:T(8,128)S(1)}, s32[256,128]{1,0:T(8,128)}, u32[]{:S(2)}) %copy-start.2) | copy-done | bytes 131096
  1.5 0.1 edges.1
  1.6 3.0 %collective-permute-start = (f32[8,256]{1,0:T(8,128)S(1)}, f32[8,256]{1,0:T(8,128)S(1)}, u32[]{:S(2)}, u32[]{:S(2)}) collective-permute-start(f32[8,256]{1,0:T(8,128)S(1)} %get-tuple-element.36), channel_id=1, source_target_pairs={{0,4},{4,8},{8,12},{12,16},{16,20},{20,24},{24,28},{28,0},{1,5},{5... | collective-permute-start | bytes 24584 | tf_op jit(solution)/shard_map/ppermute | solution.py:668
  4.7 0.0 collective-permute-start.1
  4.7 6.7 %rims.1 = (f32[256,128]{1,0:T(8,128)S(1)}, f32[256,128]{1,0:T(8,128)S(1)}, f32[104,128]{1,0:T(8,128)S(1)}, f32[104,128]{1,0:T(8,128)S(1)}, f32[3,256,128]{2,1,0:T(8,128)S(1)}) custom-call(f32[256,128]{1,0:T(8,128)} %refs_3_.3, f32[30,256,128]{2,1,0:T(8,128)} %refs_9_.3, f32[30,256,128]{2,1,0:T(8,128)} %refs_10_.3, f32[30,256,128]{2,1,0:T(8,128)} %refs_11_.1), custom_call_target="tpu_custom_call" | custom-call | flops 6000000 | bytes 18000000 | tf_op jit(solution)/shard_map/rims/pallas_call | solution.py:173
  11.4 0.0 copy-start.11
  11.4 0.0 collective-permute-done.1.row_ref
  11.4 0.0 collective-permute-done.col_ref
  11.4 0.0 copy-done.3
  11.4 0.6 surface.1
  12.0 1.6 %collective-permute-start.3 = (f32[3,256,128]{2,1,0:T(8,128)S(1)}, f32[3,256,128]{2,1,0:T(8,128)S(1)}, u32[]{:S(2)}, u32[]{:S(2)}) collective-permute-start(f32[3,256,128]{2,1,0:T(8,128)S(1)} %get-tuple-element.46.refs_0_), channel_id=1, source_target_pairs={{0,2},{1,3},{2,0},{3,1},{4,6},{5,7},{6,4},{7,5},{8,10},{9,11},{10,... | collective-permute-start | bytes 1179656 | tf_op jit(solution)/shard_map/ppermute | solution.py:680
  13.5 0.2 collective-permute-start.2
  13.8 1.5 %collective-permute-start.4 = (f32[256,128]{1,0:T(8,128)S(1)}, f32[256,128]{1,0:T(8,128)S(1)}, u32[]{:S(2)}, u32[]{:S(2)}) collective-permute-start(f32[256,128]{1,0:T(8,128)S(1)} %get-tuple-element.47), channel_id=1, source_target_pairs={{0,4},{4,8},{8,12},{12,16},{16,20},{20,24},{24,28},{28,0},{1,5},{5... | collective-permute-start | bytes 393224 | tf_op jit(solution)/shard_map/ppermute | solution.py:674
  15.3 3.2 %collective-permute-start.5 = (f32[256,128]{1,0:T(8,128)S(1)}, f32[256,128]{1,0:T(8,128)S(1)}, u32[]{:S(2)}, u32[]{:S(2)}) collective-permute-start(f32[256,128]{1,0:T(8,128)S(1)} %get-tuple-element.48), channel_id=1, source_target_pairs={{4,0},{8,4},{12,8},{16,12},{20,16},{24,20},{28,24},{0,28},{5,1},{9... | collective-permute-start | bytes 393224 | tf_op jit(solution)/shard_map/ppermute | solution.py:675
  18.5 3.8 %collective-permute-done.4.west_ref.refs_4_ = f32[256,128]{1,0:T(8,128)S(1)} collective-permute-done((f32[256,128]{1,0:T(8,128)S(1)}, f32[256,128]{1,0:T(8,128)S(1)}, u32[]{:S(2)}, u32[]{:S(2)}) %collective-permute-start.4) | collective-permute-done | bytes 131104 | tf_op jit(solution)/shard_map/ppermute | solution.py:674
  22.3 1.2 %collective-permute-done.5.east_ref.refs_5_ = f32[256,128]{1,0:T(8,128)S(1)} collective-permute-done((f32[256,128]{1,0:T(8,128)S(1)}, f32[256,128]{1,0:T(8,128)S(1)}, u32[]{:S(2)}, u32[]{:S(2)}) %collective-permute-start.5) | collective-permute-done | bytes 131104 | tf_op jit(solution)/shard_map/ppermute | solution.py:675
  23.5 0.1 collective-permute-done.3.refs_2_
  23.6 0.0 collective-permute-done.2.refs_1_
  23.6 0.2 collective-permute-start.6
  23.9 0.6 corners.1
  24.5 0.3 collective-permute-start.7
  24.8 1.5 %collective-permute-start.8 = (f32[104,128]{1,0:T(8,128)}, f32[104,128]{1,0:T(8,128)S(1)}, u32[]{:S(2)}, u32[]{:S(2)}) collective-permute-start(f32[104,128]{1,0:T(8,128)} %get-tuple-element.56), channel_id=1, source_target_pairs={{1,0},{2,1},{3,2},{0,3},{5,4},{6,5},{7,6},{4,7},{9,8},{10,9},{11,1... | collective-permute-start | bytes 159752 | tf_op jit(solution)/shard_map/ppermute | solution.py:694
  26.3 0.0 copy-done.10
  26.3 0.1 copy.16.pattern_ref
  26.3 0.0 collective-permute-done.6.refs_3_
  26.3 0.0 copy-done
  26.3 2.5 %meridional.1.refs_11_ = f32[8,96,128]{2,1,0:T(8,128)} custom-call(s32[8,3]{1,0:T(8,128)S(1)} %copy.16.pattern_ref, f32[8,3,128,128]{3,2,1,0:T(8,128)S(1)} %copy-done, f32[3,256,128]{2,1,0:T(8,128)S(1)} %get-tuple-element.46.refs_0_, f32[3,256,128]{2,1,0:T(8,128)S(1)} %collective-permute-done.2.refs_1_, f32[3,256,128]{2,1,0:T(8,128)S(1)} %collective-permute-done.3.refs_2_, ...), custom_call_target="tpu_custom_call" | custom-call | flops 2000000 | bytes 6000000 | tf_op jit(solution)/shard_map/meridional/pallas_call | solution.py:622
  28.8 0.0 collective-permute-done.7.refs_7_
  28.8 0.0 collective-permute-done.8.refs_6_
  28.9 0.0 copy-start.7
  28.9 4.9 %all-to-all-start = ((f32[8,96,128]{2,1,0:T(8,128)}), f32[8,96,128]{2,1,0:T(8,128)S(1)}, u32[]{:S(2)}, u32[]{:S(2)}) async-start(f32[8,96,128]{2,1,0:T(8,128)} %meridional.1.refs_11_), calls=%async_computation | async-start | bytes 786432 | tf_op jit(solution)/shard_map/all_to_all | solution.py:697
  33.8 0.0 copy-done.11
  33.8 0.1 copy.17.pattern_ref
  33.8 0.0 copy-done.4
  33.8 0.0 copy-done.7
  33.8 0.8 %copy-done.5 = f32[104,128]{1,0:T(8,128)S(1)} copy-done((f32[104,128]{1,0:T(8,128)S(1)}, f32[104,128]{1,0:T(8,128)}, u32[]{:S(2)}) %copy-start.5) | copy-done | bytes 53272
  34.7 0.8 %copy-done.8 = f32[104,128]{1,0:T(8,128)S(1)} copy-done((f32[104,128]{1,0:T(8,128)S(1)}, f32[104,128]{1,0:T(8,128)}, u32[]{:S(2)}) %copy-start.8) | copy-done | bytes 53272
  35.5 7.7 %adjoint.2 = (f32[30,256,128]{2,1,0:T(8,128)}, f32[30,256,128]{2,1,0:T(8,128)}, f32[30,256,128]{2,1,0:T(8,128)}, f32[4,256,128]{2,1,0:T(8,128)S(1)}) custom-call(f32[256,128]{1,0:T(8,128)S(1)} %get-tuple-element.43.refs_0_, f32[256,128]{1,0:T(8,128)S(1)} %get-tuple-element.44.refs_1_, f32[256,128]{1,0:T(8,128)S(1)} %get-tuple-element.45.refs_2_, ...), custom_call_target="tpu_custom_call" | custom-call | flops 6000000 | bytes 18000000 | tf_op jit(solution)/shard_map/adjoint/pallas_call | solution.py:518
  43.2 3.2 %all-to-all-done.field_ref = f32[8,96,128]{2,1,0:T(8,128)S(1)} async-done(((f32[8,96,128]{2,1,0:T(8,128)}), f32[8,96,128]{2,1,0:T(8,128)S(1)}, u32[]{:S(2)}, u32[]{:S(2)}) %all-to-all-start) | async-done | bytes 393248 | tf_op jit(solution)/shard_map/all_to_all | solution.py:697
  46.3 0.0 copy-done.1
  46.3 2.2 %zonal.1.refs_12_ = f32[8,96,128]{2,1,0:T(8,128)} custom-call(s32[8,3]{1,0:T(8,128)S(1)} %copy.17.pattern_ref, f32[8,3,128,128]{3,2,1,0:T(8,128)S(1)} %copy-done.1, f32[8,96,128]{2,1,0:T(8,128)S(1)} %all-to-all-done.field_ref, f32[4,256,128]{2,1,0:T(8,128)S(1)} %get-tuple-element.60.after_ref.refs_8_), custom_call_target="tpu_custom_call" | custom-call | flops 2000000 | bytes 6000000 | tf_op jit(solution)/shard_map/zonal/pallas_call | solution.py:573
  48.5 3.6 %all-to-all-start.1 = ((f32[8,96,128]{2,1,0:T(8,128)}), f32[8,96,128]{2,1,0:T(8,128)S(1)}, u32[]{:S(2)}, u32[]{:S(2)}) async-start(f32[8,96,128]{2,1,0:T(8,128)} %zonal.1.refs_12_), calls=%async_computation.1 | async-start | bytes 786432 | tf_op jit(solution)/shard_map/all_to_all | solution.py:702
  52.2 0.0 copy-done.6
  52.2 0.0 copy-done.9
  52.2 11.1 %adjoint.3 = (f32[30,256,128]{2,1,0:T(8,128)}, f32[30,256,128]{2,1,0:T(8,128)}, f32[30,256,128]{2,1,0:T(8,128)}, f32[4,256,128]{2,1,0:T(8,128)S(1)}) custom-call(f32[256,128]{1,0:T(8,128)S(1)} %get-tuple-element.43.refs_0_, f32[256,128]{1,0:T(8,128)S(1)} %get-tuple-element.44.refs_1_, ...), custom_call_target="tpu_custom_call", output_to_operand_aliasing={{0}: (13, {}), {1}: (14, {}), {2}: (15, {})} | custom-call | flops 12000000 | bytes 36000000 | tf_op jit(solution)/shard_map/adjoint/pallas_call | solution.py:518
  63.3 0.8 %all-to-all-done.1.field_ref = f32[8,96,128]{2,1,0:T(8,128)S(1)} async-done(((f32[8,96,128]{2,1,0:T(8,128)}), f32[8,96,128]{2,1,0:T(8,128)S(1)}, u32[]{:S(2)}, u32[]{:S(2)}) %all-to-all-start.1) | async-done | bytes 393248 | tf_op jit(solution)/shard_map/all_to_all | solution.py:702
  64.1 0.8 %finish.1 = f32[3,256,128]{2,1,0:T(8,128)} custom-call(f32[8,96,128]{2,1,0:T(8,128)S(1)} %all-to-all-done.1.field_ref, f32[4,256,128]{2,1,0:T(8,128)S(1)} %get-tuple-element.67.after_ref), custom_call_target="tpu_custom_call" | custom-call | flops 700000 | bytes 2100000 | tf_op jit(solution)/shard_map/finish/pallas_call | solution.py:646
  (9 shorter events, 0.0 us)
Async XLA Ops:
  0.6 0.9 %copy-start.2 = (s32[256,128]{1,0:T(8,128)S(1)}, s32[256,128]{1,0:T(8,128)}, u32[]{:S(2)}) copy-start(s32[256,128]{1,0:T(8,128)} %levels_ref.3) | copy-start | bytes 393220
  1.6 9.8 %collective-permute-start = (f32[8,256]{1,0:T(8,128)S(1)}, f32[8,256]{1,0:T(8,128)S(1)}, u32[]{:S(2)}, u32[]{:S(2)}) collective-permute-start(f32[8,256]{1,0:T(8,128)S(1)} %get-tuple-element.36), channel_id=1, source_target_pairs={{0,4},{4,8},{8,12},{12,16},{16,20},{20,24},{24,28},{28,0},{1,5},{5... | collective-permute-start | bytes 24584 | tf_op jit(solution)/shard_map/ppermute | solution.py:668
  4.7 6.8 %copy-start.3 = (s32[256,128]{1,0:T(8,128)S(1)}, s32[256,128]{1,0:T(8,128)}, u32[]{:S(2)}) copy-start(s32[256,128]{1,0:T(8,128)} %levels_ref.3) | copy-start | bytes 393220
  4.7 21.6 %copy-start.10 = (s32[8,3]{0,1:T(4,128)S(1)}, s32[8,3]{0,1:T(4,128)}, u32[]{:S(2)}) copy-start(s32[8,3]{0,1:T(4,128)} %param.16) | copy-start | bytes 292
  4.7 21.7 %copy-start = (f32[8,3,128,128]{3,2,1,0:T(8,128)S(1)}, f32[8,3,128,128]{3,2,1,0:T(8,128)}, u32[]{:S(2)}) copy-start(f32[8,3,128,128]{3,2,1,0:T(8,128)} %blocks_ref.2) | copy-start | bytes 4718596
  4.7 6.7 %collective-permute-start.1 = (f32[8,128]{1,0:T(8,128)S(1)}, f32[8,128]{1,0:T(8,128)S(1)}, u32[]{:S(2)}, u32[]{:S(2)}) collective-permute-start(f32[8,128]{1,0:T(8,128)S(1)} %get-tuple-element.37), channel_id=1, source_target_pairs={{0,1},{1,2},{2,3},{3,0},{4,5},{5,6},{6,7},{7,4},{8,9},{9,10},{10,1... | collective-permute-start | bytes 12296 | tf_op jit(solution)/shard_map/ppermute | solution.py:669
  11.4 22.4 %copy-start.11 = (s32[8,3]{0,1:T(4,128)S(1)}, s32[8,3]{0,1:T(4,128)}, u32[]{:S(2)}) copy-start(s32[8,3]{0,1:T(4,128)} %param.14) | copy-start | bytes 292
  12.0 11.6 %collective-permute-start.3 = (f32[3,256,128]{2,1,0:T(8,128)S(1)}, f32[3,256,128]{2,1,0:T(8,128)S(1)}, u32[]{:S(2)}, u32[]{:S(2)}) collective-permute-start(f32[3,256,128]{2,1,0:T(8,128)S(1)} %get-tuple-element.46.refs_0_), channel_id=1, source_target_pairs={{0,2},{1,3},{2,0},{3,1},{4,6},{5,7},{6,4},{7,5},{8,10},{9,11},{10,... | collective-permute-start | bytes 1179656 | tf_op jit(solution)/shard_map/ppermute | solution.py:680
  13.5 10.1 %collective-permute-start.2 = (f32[3,256,128]{2,1,0:T(8,128)S(1)}, f32[3,256,128]{2,1,0:T(8,128)S(1)}, u32[]{:S(2)}, u32[]{:S(2)}) collective-permute-start(f32[3,256,128]{2,1,0:T(8,128)S(1)} %get-tuple-element.46.refs_0_), channel_id=1, source_target_pairs={{0,1},{1,0},{2,3},{3,2},{4,5},{5,4},{6,7},{7,6},{8,9},{9,8},{10,11... | collective-permute-start | bytes 1179656 | tf_op jit(solution)/shard_map/ppermute | solution.py:680
  13.8 8.5 %collective-permute-start.4 = (f32[256,128]{1,0:T(8,128)S(1)}, f32[256,128]{1,0:T(8,128)S(1)}, u32[]{:S(2)}, u32[]{:S(2)}) collective-permute-start(f32[256,128]{1,0:T(8,128)S(1)} %get-tuple-element.47), channel_id=1, source_target_pairs={{0,4},{4,8},{8,12},{12,16},{16,20},{20,24},{24,28},{28,0},{1,5},{5... | collective-permute-start | bytes 393224 | tf_op jit(solution)/shard_map/ppermute | solution.py:674
  15.3 8.2 %collective-permute-start.5 = (f32[256,128]{1,0:T(8,128)S(1)}, f32[256,128]{1,0:T(8,128)S(1)}, u32[]{:S(2)}, u32[]{:S(2)}) collective-permute-start(f32[256,128]{1,0:T(8,128)S(1)} %get-tuple-element.48), channel_id=1, source_target_pairs={{4,0},{8,4},{12,8},{16,12},{20,16},{24,20},{28,24},{0,28},{5,1},{9... | collective-permute-start | bytes 393224 | tf_op jit(solution)/shard_map/ppermute | solution.py:675
  23.6 2.7 %collective-permute-start.6 = (f32[3,256,128]{2,1,0:T(8,128)S(1)}, f32[3,256,128]{2,1,0:T(8,128)}, u32[]{:S(2)}, u32[]{:S(2)}) collective-permute-start(f32[3,256,128]{2,1,0:T(8,128)S(1)} %collective-permute-done.3.refs_2_), channel_id=1, source_target_pairs={{0,1},{1,0},{2,3},{3,2},{4,5},{5,4},{6,7},{7,6},{8,9},{9,8},{10,11... | collective-permute-start | bytes 1179656 | tf_op jit(solution)/shard_map/ppermute | solution.py:690
  24.5 4.3 %collective-permute-start.7 = (f32[104,128]{1,0:T(8,128)}, f32[104,128]{1,0:T(8,128)S(1)}, u32[]{:S(2)}, u32[]{:S(2)}) collective-permute-start(f32[104,128]{1,0:T(8,128)} %get-tuple-element.55), channel_id=1, source_target_pairs={{0,1},{1,2},{2,3},{3,0},{4,5},{5,6},{6,7},{7,4},{8,9},{9,10},{10,1... | collective-permute-start | bytes 159752 | tf_op jit(solution)/shard_map/ppermute | solution.py:693
  24.8 4.1 %collective-permute-start.8 = (f32[104,128]{1,0:T(8,128)}, f32[104,128]{1,0:T(8,128)S(1)}, u32[]{:S(2)}, u32[]{:S(2)}) collective-permute-start(f32[104,128]{1,0:T(8,128)} %get-tuple-element.56), channel_id=1, source_target_pairs={{1,0},{2,1},{3,2},{0,3},{5,4},{6,5},{7,6},{4,7},{9,8},{10,9},{11,1... | collective-permute-start | bytes 159752 | tf_op jit(solution)/shard_map/ppermute | solution.py:694
  28.8 5.0 %copy-start.4 = (f32[104,128]{1,0:T(8,128)}, f32[104,128]{1,0:T(8,128)S(1)}, u32[]{:S(2)}) copy-start(f32[104,128]{1,0:T(8,128)S(1)} %collective-permute-done.7.refs_7_) | copy-start | bytes 159748
  28.9 5.0 %copy-start.7 = (f32[104,128]{1,0:T(8,128)}, f32[104,128]{1,0:T(8,128)S(1)}, u32[]{:S(2)}) copy-start(f32[104,128]{1,0:T(8,128)S(1)} %collective-permute-done.8.refs_6_) | copy-start | bytes 159748
  28.9 17.5 %all-to-all-start = ((f32[8,96,128]{2,1,0:T(8,128)}), f32[8,96,128]{2,1,0:T(8,128)S(1)}, u32[]{:S(2)}, u32[]{:S(2)}) async-start(f32[8,96,128]{2,1,0:T(8,128)} %meridional.1.refs_11_), calls=%async_computation | async-start | bytes 786432 | tf_op jit(solution)/shard_map/all_to_all | solution.py:697
  33.8 0.8 %copy-start.5 = (f32[104,128]{1,0:T(8,128)S(1)}, f32[104,128]{1,0:T(8,128)}, u32[]{:S(2)}) copy-start(f32[104,128]{1,0:T(8,128)} %copy-done.4) | copy-start | bytes 159748
  34.7 0.8 %copy-start.8 = (f32[104,128]{1,0:T(8,128)S(1)}, f32[104,128]{1,0:T(8,128)}, u32[]{:S(2)}) copy-start(f32[104,128]{1,0:T(8,128)} %copy-done.7) | copy-start | bytes 159748
  35.5 10.9 %copy-start.1 = (f32[8,3,128,128]{3,2,1,0:T(8,128)S(1)}, f32[8,3,128,128]{3,2,1,0:T(8,128)}, u32[]{:S(2)}) copy-start(f32[8,3,128,128]{3,2,1,0:T(8,128)} %blocks_ref.3) | copy-start | bytes 4718596
  35.5 16.7 %copy-start.6 = (f32[104,128]{1,0:T(8,128)S(1)}, f32[104,128]{1,0:T(8,128)}, u32[]{:S(2)}) copy-start(f32[104,128]{1,0:T(8,128)} %copy-done.4) | copy-start | bytes 159748
  35.5 16.7 %copy-start.9 = (f32[104,128]{1,0:T(8,128)S(1)}, f32[104,128]{1,0:T(8,128)}, u32[]{:S(2)}) copy-start(f32[104,128]{1,0:T(8,128)} %copy-done.7) | copy-start | bytes 159748
  48.5 15.5 %all-to-all-start.1 = ((f32[8,96,128]{2,1,0:T(8,128)}), f32[8,96,128]{2,1,0:T(8,128)S(1)}, u32[]{:S(2)}, u32[]{:S(2)}) async-start(f32[8,96,128]{2,1,0:T(8,128)} %zonal.1.refs_12_), calls=%async_computation.1 | async-start | bytes 786432 | tf_op jit(solution)/shard_map/all_to_all | solution.py:702

commit v4 on v3

--- a/solution.py
+++ b/solution.py
@@ -57,6 +57,10 @@
 
 def has_after(axis):
     return lax.axis_index(axis) < lax.axis_size(axis) - 1
+
+
+def opposite(part, parts):
+    return (part + parts // 2) % parts
 
 
 def lane_ids(shape):
@@ -497,7 +501,7 @@
 def adjoint(planes, halos, cots, after, total_rows, earlier=None):
     depth, rows, cols = cots[0].shape
     step = 5
-    first = depth // (3 * step)
+    first = depth // (2 * step)
     done, steps = (0, first) if earlier is None else (first, depth // step - first)
     plane = full(rows, cols)
     top = depth // step - 1 - done
@@ -557,12 +561,13 @@
 
 
 def zonal_kernel(pattern_ref, blocks_ref, field_ref, after_ref, out_ref, high_ref, low_ref):
-    for tile in range(field_ref.shape[0]):
-        high_ref[tile], low_ref[tile] = halves(field_ref[tile])
+    for slot in range(field_ref.shape[0]):
+        tile = opposite(slot, field_ref.shape[0])
+        high_ref[tile], low_ref[tile] = halves(field_ref[slot])
     for r in range(blocks_ref.shape[0]):
         entries = range(blocks_ref.shape[1])
         picked = [pattern_ref[r, j] for j in entries]
-        out_ref[r] = product(
+        out_ref[opposite(r, out_ref.shape[0])] = product(
             [halves(blocks_ref[r, j]) for j in entries],
             [(high_ref[p], low_ref[p]) for p in picked],
             True,
@@ -606,7 +611,7 @@
         for line in range(0, block, chunk):
             part = (h * block + line) // chunk
             for c in range(3):
-                out_ref[part, c * chunk : (c + 1) * chunk, :] = result[
+                out_ref[opposite(part, out_ref.shape[0]), c * chunk : (c + 1) * chunk, :] = result[
                     line : line + chunk, c * cols : (c + 1) * cols
                 ]
 
@@ -637,7 +642,7 @@
     for part in range(parts):
         for c in range(3):
             out_ref[c, part * chunk : (part + 1) * chunk, :] = field_ref[
-                part, c * chunk : (c + 1) * chunk, :
+                opposite(part, parts), c * chunk : (c + 1) * chunk, :
             ]
 
 
@@ -661,6 +666,7 @@
     down_x = [(j, i) for i, j in up_x]
     up_y = [(i, (i + 1) % ny) for i in range(ny)]
     down_y = [(j, i) for i, j in up_y]
+    halfway = [[(i + nx // 2) % nx for i in range(nx)]]
 
     mixing = pltpu.with_memory_space_constraint(mixing, pltpu.HBM)
     cots = tuple(pltpu.with_memory_space_constraint(c, pltpu.HBM) for c in (cot_u, cot_v, cot_t))
@@ -694,12 +700,15 @@
     halo_n = lax.ppermute(south, "gy", down_y)
     mixed = meridional(pattern_y, blocks_y, [tiles[m] for m in range(ny)], nx)
     mixed, halo_s, halo_n = lax.optimization_barrier((mixed, halo_s, halo_n))
-    lines = lax.all_to_all(mixed, "gx", 0, 0)
+    lines = lax.all_to_all(mixed, "gx", 0, 0, axis_index_groups=halfway)
     planes = (wet_c, wet_u, wet_v, mixing)
+    halo_n, halo_s = (
+        pltpu.with_memory_space_constraint(halo, pltpu.HBM) for halo in (halo_n, halo_s)
+    )
     halos = (halo_w, halo_e, halo_n, halo_s)
     grads, state = adjoint(planes, halos, cots, mixed, rows * ny)
     turned = zonal(pattern_x, blocks_x, lines, state[0])
-    back = lax.all_to_all(turned, "gx", 0, 0)
+    back = lax.all_to_all(turned, "gx", 0, 0, axis_index_groups=halfway)
     grads = tuple(pltpu.with_memory_space_constraint(g, pltpu.HBM) for g in grads)
     grads, token = adjoint(planes, halos, cots, turned, rows * ny, (grads, state))
     return (*grads, finish(back, token[0]))

time: 65.5 us -> 62.2 us (0.950)
  waiting for transfers between devices: 9.11 us -> 5.68 us
  starting transfers between devices: 20.1 us -> 22.9 us
  local copies, waits for them, and re-layouts: 2.72 us -> 1.08 us
  Pallas kernels: 32.2 us -> 31.4 us
    all_to_all x2, waiting for transfers between devices: 3.98 us -> 0.55 us  [the longest x1 0.45 us: shards(): lines = lax.all_to_all(mixed, 'gx', 0, 0, axis_index_groups=halfway)]
    all_to_all x2, starting transfers between devices: 8.53 us -> 11.3 us  [the longest x1 5.97 us: shards(): lines = lax.all_to_all(mixed, 'gx', 0, 0, axis_index_groups=halfway)]
    unnamed x26 -> x14, local copies, waits for them, and re-layouts: 2.72 us -> 1.08 us
  transfers between devices with their start and end apart: 11 -> 11, of which waited for: 5 -> 5; matrix products, arithmetic and copies ran while one was open for 0% -> 0% of each run, Pallas kernels for 44% -> 45%
where the time goes in v4:
time: 62.2 us; the launch traced here: 61.8 us
  Pallas kernels  31.4 us (50%)
  starting transfers between devices  22.9 us (37%)
  waiting for transfers between devices  5.68 us (9%)
  local copies, waits for them, and re-layouts  1.08 us (2%)
  between operations  0.72 us (1%)
    pallas_call x2, Pallas kernels, adjoint(): pl.pallas_call(kernel, grid=(steps,), out_shape=(struct(depth, rows, cols...  18.6 us
    pallas_call x1, Pallas kernels, rims(): pl.pallas_call(functools.partial(rim_kernel, step), out_shape=(struct(row...  6.7 us
    all_to_all x1, starting transfers between devices, shards(): lines = lax.all_to_all(mixed, 'gx', 0, 0, axis_index_groups=halfway)  5.97 us
    all_to_all x1, starting transfers between devices, shards(): back = lax.all_to_all(turned, 'gx', 0, 0, axis_index_groups=halfway)  5.35 us
    ppermute x1, waiting for transfers between devices, shards(): halo_w = lax.ppermute(east, 'gx', up_x)  3.76 us
    ppermute x1, starting transfers between devices, shards(): halo_e = lax.ppermute(west, 'gx', down_x)  3.2 us
    ppermute x1, starting transfers between devices, shards(): level_col = lax.ppermute(level_col, 'gx', up_x)  3.02 us
    pallas_call x1, Pallas kernels, meridional(): pl.pallas_call(kernel, out_shape=struct(parts, 3 * rows // parts, cols),...  2.5 us
  transfers between devices with their start and end apart: 11, of which 5 were waited for; matrix products, arithmetic and copies ran while one was open for 0% of the time, Pallas kernels for 45%

profile of v4, /device:TPU:0, one launch (start us, length us, event | category | flops | bytes accessed | tf_op | source)
XLA Modules:
  0.0 61.8 jit_solution(9606424903139440992)
XLA Ops:
  0.6 0.0 copy-start.2
  0.6 0.9 %copy-done.2 = s32[256,128]{1,0:T(8,128)S(1)} copy-done((s32[256,128]{1,0:T(8,128)S(1)}, s32[256,128]{1,0:T(8,128)}, u32[]{:S(2)}) %copy-start.2) | copy-done | bytes 131096
  1.5 0.1 edges.1
  1.6 3.0 %collective-permute-start = (f32[8,256]{1,0:T(8,128)S(1)}, f32[8,256]{1,0:T(8,128)S(1)}, u32[]{:S(2)}, u32[]{:S(2)}) collective-permute-start(f32[8,256]{1,0:T(8,128)S(1)} %get-tuple-element.36), channel_id=1, source_target_pairs={{0,4},{4,8},{8,12},{12,16},{16,20},{20,24},{24,28},{28,0},{1,5},{5... | collective-permute-start | bytes 24584 | tf_op jit(solution)/shard_map/ppermute | solution.py:674
  4.7 0.0 copy-start.3
  4.7 0.0 copy-start.4
  4.7 0.0 copy-start
  4.7 0.0 collective-permute-start.1
  4.7 6.7 %rims.1 = (f32[256,128]{1,0:T(8,128)S(1)}, f32[256,128]{1,0:T(8,128)S(1)}, f32[104,128]{1,0:T(8,128)S(1)}, f32[104,128]{1,0:T(8,128)S(1)}, f32[3,256,128]{2,1,0:T(8,128)S(1)}) custom-call(f32[256,128]{1,0:T(8,128)} %refs_3_.3, f32[30,256,128]{2,1,0:T(8,128)} %refs_9_.3, f32[30,256,128]{2,1,0:T(8,128)} %refs_10_.3, f32[30,256,128]{2,1,0:T(8,128)} %refs_11_.1), custom_call_target="tpu_custom_call" | custom-call | flops 6000000 | bytes 18000000 | tf_op jit(solution)/shard_map/rims/pallas_call | solution.py:177
  11.4 0.0 copy-start.5
  11.4 0.0 collective-permute-done.1.row_ref
  11.4 0.0 collective-permute-done.col_ref
  11.4 0.0 copy-done.3
  11.4 0.6 surface.1
  12.0 1.6 %collective-permute-start.3 = (f32[3,256,128]{2,1,0:T(8,128)S(1)}, f32[3,256,128]{2,1,0:T(8,128)S(1)}, u32[]{:S(2)}, u32[]{:S(2)}) collective-permute-start(f32[3,256,128]{2,1,0:T(8,128)S(1)} %get-tuple-element.46.refs_0_), channel_id=1, source_target_pairs={{0,2},{1,3},{2,0},{3,1},{4,6},{5,7},{6,4},{7,5},{8,10},{9,11},{10,... | collective-permute-start | bytes 1179656 | tf_op jit(solution)/shard_map/ppermute | solution.py:686
  13.5 0.2 collective-permute-start.2
  13.8 1.5 %collective-permute-start.4 = (f32[256,128]{1,0:T(8,128)S(1)}, f32[256,128]{1,0:T(8,128)S(1)}, u32[]{:S(2)}, u32[]{:S(2)}) collective-permute-start(f32[256,128]{1,0:T(8,128)S(1)} %get-tuple-element.47), channel_id=1, source_target_pairs={{0,4},{4,8},{8,12},{12,16},{16,20},{20,24},{24,28},{28,0},{1,5},{5... | collective-permute-start | bytes 393224 | tf_op jit(solution)/shard_map/ppermute | solution.py:680
  15.3 3.2 %collective-permute-start.5 = (f32[256,128]{1,0:T(8,128)S(1)}, f32[256,128]{1,0:T(8,128)S(1)}, u32[]{:S(2)}, u32[]{:S(2)}) collective-permute-start(f32[256,128]{1,0:T(8,128)S(1)} %get-tuple-element.48), channel_id=1, source_target_pairs={{4,0},{8,4},{12,8},{16,12},{20,16},{24,20},{28,24},{0,28},{5,1},{9... | collective-permute-start | bytes 393224 | tf_op jit(solution)/shard_map/ppermute | solution.py:681
  18.5 3.8 %collective-permute-done.4.west_ref.refs_4_ = f32[256,128]{1,0:T(8,128)S(1)} collective-permute-done((f32[256,128]{1,0:T(8,128)S(1)}, f32[256,128]{1,0:T(8,128)S(1)}, u32[]{:S(2)}, u32[]{:S(2)}) %collective-permute-start.4) | collective-permute-done | bytes 131104 | tf_op jit(solution)/shard_map/ppermute | solution.py:680
  22.3 1.2 %collective-permute-done.5.east_ref.refs_5_ = f32[256,128]{1,0:T(8,128)S(1)} collective-permute-done((f32[256,128]{1,0:T(8,128)S(1)}, f32[256,128]{1,0:T(8,128)S(1)}, u32[]{:S(2)}, u32[]{:S(2)}) %collective-permute-start.5) | collective-permute-done | bytes 131104 | tf_op jit(solution)/shard_map/ppermute | solution.py:681
  23.5 0.1 collective-permute-done.3.refs_2_
  23.6 0.0 collective-permute-done.2.refs_1_
  23.6 0.2 collective-permute-start.6
  23.9 0.3 collective-permute-start.7
  24.2 1.5 %collective-permute-start.8 = (f32[104,128]{1,0:T(8,128)S(1)}, f32[104,128]{1,0:T(8,128)}, u32[]{:S(2)}, u32[]{:S(2)}) collective-permute-start(f32[104,128]{1,0:T(8,128)S(1)} %get-tuple-element.56), channel_id=1, source_target_pairs={{1,0},{2,1},{3,2},{0,3},{5,4},{6,5},{7,6},{4,7},{9,8},{10,9},{11,1... | collective-permute-start | bytes 159752 | tf_op jit(solution)/shard_map/ppermute | solution.py:700
  25.7 0.0 copy-done.4
  25.7 0.1 copy.16.pattern_ref
  25.8 0.0 collective-permute-done.6.refs_3_
  25.8 0.0 copy-done
  25.8 2.5 %meridional.1.refs_11_ = f32[8,96,128]{2,1,0:T(8,128)} custom-call(s32[8,3]{1,0:T(8,128)S(1)} %copy.16.pattern_ref, f32[8,3,128,128]{3,2,1,0:T(8,128)S(1)} %copy-done, f32[3,256,128]{2,1,0:T(8,128)S(1)} %get-tuple-element.46.refs_0_, f32[3,256,128]{2,1,0:T(8,128)S(1)} %collective-permute-done.2.refs_1_, f32[3,256,128]{2,1,0:T(8,128)S(1)} %collective-permute-done.3.refs_2_, ...), custom_call_target="tpu_custom_call" | custom-call | flops 2000000 | bytes 6000000 | tf_op jit(solution)/shard_map/meridional/pallas_call | solution.py:627
  28.3 0.0 collective-permute-done.7.refs_7_
  28.3 0.0 collective-permute-done.8.refs_6_
  28.3 6.0 %all-to-all-start = ((f32[8,96,128]{2,1,0:T(8,128)}), f32[8,96,128]{2,1,0:T(8,128)S(1)}, u32[]{:S(2)}, u32[]{:S(2)}) async-start(f32[8,96,128]{2,1,0:T(8,128)} %meridional.1.refs_11_), calls=%async_computation | async-start | bytes 786432 | tf_op jit(solution)/shard_map/all_to_all | solution.py:703
  34.2 0.0 copy-done.5
  34.2 0.1 copy.17.pattern_ref
  34.3 0.0 copy-start.1
  34.3 9.6 %adjoint.2 = (f32[30,256,128]{2,1,0:T(8,128)}, f32[30,256,128]{2,1,0:T(8,128)}, f32[30,256,128]{2,1,0:T(8,128)}, f32[4,256,128]{2,1,0:T(8,128)S(1)}) custom-call(f32[256,128]{1,0:T(8,128)S(1)} %get-tuple-element.43.refs_0_, f32[256,128]{1,0:T(8,128)S(1)} %get-tuple-element.44.refs_1_, f32[256,128]{1,0:T(8,128)S(1)} %get-tuple-element.45.refs_2_, ...), custom_call_target="tpu_custom_call" | custom-call | flops 9000000 | bytes 27000000 | tf_op jit(solution)/shard_map/adjoint/pallas_call | solution.py:522
  44.0 0.5 all-to-all-done.field_ref
  44.4 0.0 copy-done.1
  44.4 2.2 %zonal.1.refs_12_ = f32[8,96,128]{2,1,0:T(8,128)} custom-call(s32[8,3]{1,0:T(8,128)S(1)} %copy.17.pattern_ref, f32[8,3,128,128]{3,2,1,0:T(8,128)S(1)} %copy-done.1, f32[8,96,128]{2,1,0:T(8,128)S(1)} %all-to-all-done.field_ref, f32[4,256,128]{2,1,0:T(8,128)S(1)} %get-tuple-element.60.after_ref.refs_8_), custom_call_target="tpu_custom_call" | custom-call | flops 2000000 | bytes 6000000 | tf_op jit(solution)/shard_map/zonal/pallas_call | solution.py:578
  46.6 5.4 %all-to-all-start.1 = ((f32[8,96,128]{2,1,0:T(8,128)}), f32[8,96,128]{2,1,0:T(8,128)S(1)}, u32[]{:S(2)}, u32[]{:S(2)}) async-start(f32[8,96,128]{2,1,0:T(8,128)} %zonal.1.refs_12_), calls=%async_computation.1 | async-start | bytes 786432 | tf_op jit(solution)/shard_map/all_to_all | solution.py:711
  52.0 8.9 %adjoint.3 = (f32[30,256,128]{2,1,0:T(8,128)}, f32[30,256,128]{2,1,0:T(8,128)}, f32[30,256,128]{2,1,0:T(8,128)}, f32[4,256,128]{2,1,0:T(8,128)S(1)}) custom-call(f32[256,128]{1,0:T(8,128)S(1)} %get-tuple-element.43.refs_0_, f32[256,128]{1,0:T(8,128)S(1)} %get-tuple-element.44.refs_1_, ...), custom_call_target="tpu_custom_call", output_to_operand_aliasing={{0}: (13, {}), {1}: (14, {}), {2}: (15, {})} | custom-call | flops 9000000 | bytes 27000000 | tf_op jit(solution)/shard_map/adjoint/pallas_call | solution.py:522
  60.9 0.1 all-to-all-done.1.field_ref
  61.0 0.8 %finish.1 = f32[3,256,128]{2,1,0:T(8,128)} custom-call(f32[8,96,128]{2,1,0:T(8,128)S(1)} %all-to-all-done.1.field_ref, f32[4,256,128]{2,1,0:T(8,128)S(1)} %get-tuple-element.67.after_ref), custom_call_target="tpu_custom_call" | custom-call | flops 700000 | bytes 2100000 | tf_op jit(solution)/shard_map/finish/pallas_call | solution.py:651
  (1 shorter events, 0.0 us)
Async XLA Ops:
  0.6 0.9 %copy-start.2 = (s32[256,128]{1,0:T(8,128)S(1)}, s32[256,128]{1,0:T(8,128)}, u32[]{:S(2)}) copy-start(s32[256,128]{1,0:T(8,128)} %levels_ref.3) | copy-start | bytes 393220
  1.6 9.8 %collective-permute-start = (f32[8,256]{1,0:T(8,128)S(1)}, f32[8,256]{1,0:T(8,128)S(1)}, u32[]{:S(2)}, u32[]{:S(2)}) collective-permute-start(f32[8,256]{1,0:T(8,128)S(1)} %get-tuple-element.36), channel_id=1, source_target_pairs={{0,4},{4,8},{8,12},{12,16},{16,20},{20,24},{24,28},{28,0},{1,5},{5... | collective-permute-start | bytes 24584 | tf_op jit(solution)/shard_map/ppermute | solution.py:674
  4.7 6.8 %copy-start.3 = (s32[256,128]{1,0:T(8,128)S(1)}, s32[256,128]{1,0:T(8,128)}, u32[]{:S(2)}) copy-start(s32[256,128]{1,0:T(8,128)} %levels_ref.3) | copy-start | bytes 393220
  4.7 21.0 %copy-start.4 = (s32[8,3]{0,1:T(4,128)S(1)}, s32[8,3]{0,1:T(4,128)}, u32[]{:S(2)}) copy-start(s32[8,3]{0,1:T(4,128)} %param.16) | copy-start | bytes 292
  4.7 21.1 %copy-start = (f32[8,3,128,128]{3,2,1,0:T(8,128)S(1)}, f32[8,3,128,128]{3,2,1,0:T(8,128)}, u32[]{:S(2)}) copy-start(f32[8,3,128,128]{3,2,1,0:T(8,128)} %blocks_ref.2) | copy-start | bytes 4718596
  4.7 6.7 %collective-permute-start.1 = (f32[8,128]{1,0:T(8,128)S(1)}, f32[8,128]{1,0:T(8,128)S(1)}, u32[]{:S(2)}, u32[]{:S(2)}) collective-permute-start(f32[8,128]{1,0:T(8,128)S(1)} %get-tuple-element.37), channel_id=1, source_target_pairs={{0,1},{1,2},{2,3},{3,0},{4,5},{5,6},{6,7},{7,4},{8,9},{9,10},{10,1... | collective-permute-start | bytes 12296 | tf_op jit(solution)/shard_map/ppermute | solution.py:675
  11.4 22.9 %copy-start.5 = (s32[8,3]{0,1:T(4,128)S(1)}, s32[8,3]{0,1:T(4,128)}, u32[]{:S(2)}) copy-start(s32[8,3]{0,1:T(4,128)} %param.14) | copy-start | bytes 292
  12.0 11.6 %collective-permute-start.3 = (f32[3,256,128]{2,1,0:T(8,128)S(1)}, f32[3,256,128]{2,1,0:T(8,128)S(1)}, u32[]{:S(2)}, u32[]{:S(2)}) collective-permute-start(f32[3,256,128]{2,1,0:T(8,128)S(1)} %get-tuple-element.46.refs_0_), channel_id=1, source_target_pairs={{0,2},{1,3},{2,0},{3,1},{4,6},{5,7},{6,4},{7,5},{8,10},{9,11},{10,... | collective-permute-start | bytes 1179656 | tf_op jit(solution)/shard_map/ppermute | solution.py:686
  13.5 10.1 %collective-permute-start.2 = (f32[3,256,128]{2,1,0:T(8,128)S(1)}, f32[3,256,128]{2,1,0:T(8,128)S(1)}, u32[]{:S(2)}, u32[]{:S(2)}) collective-permute-start(f32[3,256,128]{2,1,0:T(8,128)S(1)} %get-tuple-element.46.refs_0_), channel_id=1, source_target_pairs={{0,1},{1,0},{2,3},{3,2},{4,5},{5,4},{6,7},{7,6},{8,9},{9,8},{10,11... | collective-permute-start | bytes 1179656 | tf_op jit(solution)/shard_map/ppermute | solution.py:686
  13.8 8.5 %collective-permute-start.4 = (f32[256,128]{1,0:T(8,128)S(1)}, f32[256,128]{1,0:T(8,128)S(1)}, u32[]{:S(2)}, u32[]{:S(2)}) collective-permute-start(f32[256,128]{1,0:T(8,128)S(1)} %get-tuple-element.47), channel_id=1, source_target_pairs={{0,4},{4,8},{8,12},{12,16},{16,20},{20,24},{24,28},{28,0},{1,5},{5... | collective-permute-start | bytes 393224 | tf_op jit(solution)/shard_map/ppermute | solution.py:680
  15.3 8.2 %collective-permute-start.5 = (f32[256,128]{1,0:T(8,128)S(1)}, f32[256,128]{1,0:T(8,128)S(1)}, u32[]{:S(2)}, u32[]{:S(2)}) collective-permute-start(f32[256,128]{1,0:T(8,128)S(1)} %get-tuple-element.48), channel_id=1, source_target_pairs={{4,0},{8,4},{12,8},{16,12},{20,16},{24,20},{28,24},{0,28},{5,1},{9... | collective-permute-start | bytes 393224 | tf_op jit(solution)/shard_map/ppermute | solution.py:681
  23.6 2.1 %collective-permute-start.6 = (f32[3,256,128]{2,1,0:T(8,128)S(1)}, f32[3,256,128]{2,1,0:T(8,128)}, u32[]{:S(2)}, u32[]{:S(2)}) collective-permute-start(f32[3,256,128]{2,1,0:T(8,128)S(1)} %collective-permute-done.3.refs_2_), channel_id=1, source_target_pairs={{0,1},{1,0},{2,3},{3,2},{4,5},{5,4},{6,7},{7,6},{8,9},{9,8},{10,11... | collective-permute-start | bytes 1179656 | tf_op jit(solution)/shard_map/ppermute | solution.py:696
  23.9 4.4 %collective-permute-start.7 = (f32[104,128]{1,0:T(8,128)S(1)}, f32[104,128]{1,0:T(8,128)}, u32[]{:S(2)}, u32[]{:S(2)}) collective-permute-start(f32[104,128]{1,0:T(8,128)S(1)} %get-tuple-element.55), channel_id=1, source_target_pairs={{0,1},{1,2},{2,3},{3,0},{4,5},{5,6},{6,7},{7,4},{8,9},{9,10},{10,1... | collective-permute-start | bytes 159752 | tf_op jit(solution)/shard_map/ppermute | solution.py:699
  24.2 4.1 %collective-permute-start.8 = (f32[104,128]{1,0:T(8,128)S(1)}, f32[104,128]{1,0:T(8,128)}, u32[]{:S(2)}, u32[]{:S(2)}) collective-permute-start(f32[104,128]{1,0:T(8,128)S(1)} %get-tuple-element.56), channel_id=1, source_target_pairs={{1,0},{2,1},{3,2},{0,3},{5,4},{6,5},{7,6},{4,7},{9,8},{10,9},{11,1... | collective-permute-start | bytes 159752 | tf_op jit(solution)/shard_map/ppermute | solution.py:700
  28.3 16.1 %all-to-all-start = ((f32[8,96,128]{2,1,0:T(8,128)}), f32[8,96,128]{2,1,0:T(8,128)S(1)}, u32[]{:S(2)}, u32[]{:S(2)}) async-start(f32[8,96,128]{2,1,0:T(8,128)} %meridional.1.refs_11_), calls=%async_computation | async-start | bytes 786432 | tf_op jit(solution)/shard_map/all_to_all | solution.py:703
  34.3 10.1 %copy-start.1 = (f32[8,3,128,128]{3,2,1,0:T(8,128)S(1)}, f32[8,3,128,128]{3,2,1,0:T(8,128)}, u32[]{:S(2)}) copy-start(f32[8,3,128,128]{3,2,1,0:T(8,128)} %blocks_ref.3) | copy-start | bytes 4718596
  46.6 14.4 %all-to-all-start.1 = ((f32[8,96,128]{2,1,0:T(8,128)}), f32[8,96,128]{2,1,0:T(8,128)S(1)}, u32[]{:S(2)}, u32[]{:S(2)}) async-start(f32[8,96,128]{2,1,0:T(8,128)} %zonal.1.refs_12_), calls=%async_computation.1 | async-start | bytes 786432 | tf_op jit(solution)/shard_map/all_to_all | solution.py:711

commit v5 on v4

--- a/solution.py
+++ b/solution.py
@@ -60,7 +60,7 @@
 
 
 def opposite(part, parts):
-    return (part + parts // 2) % parts
+    return (part + parts - parts // 2 + 1) % parts
 
 
 def lane_ids(shape):
@@ -562,7 +562,7 @@
 
 def zonal_kernel(pattern_ref, blocks_ref, field_ref, after_ref, out_ref, high_ref, low_ref):
     for slot in range(field_ref.shape[0]):
-        tile = opposite(slot, field_ref.shape[0])
+        tile = (slot + field_ref.shape[0] // 2 - 1) % field_ref.shape[0]
         high_ref[tile], low_ref[tile] = halves(field_ref[slot])
     for r in range(blocks_ref.shape[0]):
         entries = range(blocks_ref.shape[1])
@@ -666,7 +666,7 @@
     down_x = [(j, i) for i, j in up_x]
     up_y = [(i, (i + 1) % ny) for i in range(ny)]
     down_y = [(j, i) for i, j in up_y]
-    halfway = [[(i + nx // 2) % nx for i in range(nx)]]
+    halfway = [[(i + nx // 2 - 1) % nx for i in range(nx)]]
 
     mixing = pltpu.with_memory_space_constraint(mixing, pltpu.HBM)
     cots = tuple(pltpu.with_memory_space_constraint(c, pltpu.HBM) for c in (cot_u, cot_v, cot_t))

time: 62.2 us -> 63.4 us (1.019)
  waiting for transfers between devices: 5.68 us -> 7.62 us
  starting transfers between devices: 22.9 us -> 22.1 us
    all_to_all x1, starting transfers between devices: 5.35 us -> 4.2 us  [shards(): back = lax.all_to_all(turned, 'gx', 0, 0, axis_index_groups=halfway)]
    all_to_all x1, waiting for transfers between devices: 0.09 us -> 1.2 us  [shards(): back = lax.all_to_all(turned, 'gx', 0, 0, axis_index_groups=halfway)]
    all_to_all x1, waiting for transfers between devices: 0.45 us -> 1.3 us  [shards(): lines = lax.all_to_all(mixed, 'gx', 0, 0, axis_index_groups=halfway)]
  transfers between devices with their start and end apart: 11 -> 11, of which waited for: 5 -> 5; matrix products, arithmetic and copies ran while one was open for 0% -> 0% of each run, Pallas kernels for 45% -> 44%
where the time goes in v5:
time: 63.4 us; the launch traced here: 62.9 us
  Pallas kernels  31.4 us (50%)
  starting transfers between devices  22.1 us (35%)
  waiting for transfers between devices  7.62 us (12%)
  local copies, waits for them, and re-layouts  1.08 us (2%)
  between operations  0.72 us (1%)
    pallas_call x2, Pallas kernels, adjoint(): pl.pallas_call(kernel, grid=(steps,), out_shape=(struct(depth, rows, cols...  18.6 us
    pallas_call x1, Pallas kernels, rims(): pl.pallas_call(functools.partial(rim_kernel, step), out_shape=(struct(row...  6.7 us
    all_to_all x1, starting transfers between devices, shards(): lines = lax.all_to_all(mixed, 'gx', 0, 0, axis_index_groups=halfway)  6.36 us
    all_to_all x1, starting transfers between devices, shards(): back = lax.all_to_all(turned, 'gx', 0, 0, axis_index_groups=halfway)  4.2 us
    ppermute x1, waiting for transfers between devices, shards(): halo_w = lax.ppermute(east, 'gx', up_x)  3.76 us
    ppermute x1, starting transfers between devices, shards(): halo_e = lax.ppermute(west, 'gx', down_x)  3.2 us
    ppermute x1, starting transfers between devices, shards(): level_col = lax.ppermute(level_col, 'gx', up_x)  3.02 us
    pallas_call x1, Pallas kernels, meridional(): pl.pallas_call(kernel, out_shape=struct(parts, 3 * rows // parts, cols),...  2.5 us
  transfers between devices with their start and end apart: 11, of which 5 were waited for; matrix products, arithmetic and copies ran while one was open for 0% of the time, Pallas kernels for 44%

profile of v5, /device:TPU:0, one launch (start us, length us, event | category | flops | bytes accessed | tf_op | source)
XLA Modules:
  0.0 62.9 jit_solution(3716627224056800853)
XLA Ops:
  0.6 0.0 copy-start.2
  0.6 0.9 %copy-done.2 = s32[256,128]{1,0:T(8,128)S(1)} copy-done((s32[256,128]{1,0:T(8,128)S(1)}, s32[256,128]{1,0:T(8,128)}, u32[]{:S(2)}) %copy-start.2) | copy-done | bytes 131096
  1.5 0.1 edges.1
  1.6 3.0 %collective-permute-start = (f32[8,256]{1,0:T(8,128)S(1)}, f32[8,256]{1,0:T(8,128)S(1)}, u32[]{:S(2)}, u32[]{:S(2)}) collective-permute-start(f32[8,256]{1,0:T(8,128)S(1)} %get-tuple-element.36), channel_id=1, source_target_pairs={{0,4},{4,8},{8,12},{12,16},{16,20},{20,24},{24,28},{28,0},{1,5},{5... | collective-permute-start | bytes 24584 | tf_op jit(solution)/shard_map/ppermute | solution.py:674
  4.7 0.0 copy-start.3
  4.7 0.0 copy-start.4
  4.7 0.0 copy-start
  4.7 0.0 collective-permute-start.1
  4.7 6.7 %rims.1 = (f32[256,128]{1,0:T(8,128)S(1)}, f32[256,128]{1,0:T(8,128)S(1)}, f32[104,128]{1,0:T(8,128)S(1)}, f32[104,128]{1,0:T(8,128)S(1)}, f32[3,256,128]{2,1,0:T(8,128)S(1)}) custom-call(f32[256,128]{1,0:T(8,128)} %refs_3_.3, f32[30,256,128]{2,1,0:T(8,128)} %refs_9_.3, f32[30,256,128]{2,1,0:T(8,128)} %refs_10_.3, f32[30,256,128]{2,1,0:T(8,128)} %refs_11_.1), custom_call_target="tpu_custom_call" | custom-call | flops 6000000 | bytes 18000000 | tf_op jit(solution)/shard_map/rims/pallas_call | solution.py:177
  11.4 0.0 copy-start.5
  11.4 0.0 collective-permute-done.1.row_ref
  11.4 0.0 collective-permute-done.col_ref
  11.4 0.0 copy-done.3
  11.4 0.6 surface.1
  12.0 1.6 %collective-permute-start.3 = (f32[3,256,128]{2,1,0:T(8,128)S(1)}, f32[3,256,128]{2,1,0:T(8,128)S(1)}, u32[]{:S(2)}, u32[]{:S(2)}) collective-permute-start(f32[3,256,128]{2,1,0:T(8,128)S(1)} %get-tuple-element.46.refs_0_), channel_id=1, source_target_pairs={{0,2},{1,3},{2,0},{3,1},{4,6},{5,7},{6,4},{7,5},{8,10},{9,11},{10,... | collective-permute-start | bytes 1179656 | tf_op jit(solution)/shard_map/ppermute | solution.py:686
  13.5 0.2 collective-permute-start.2
  13.8 1.5 %collective-permute-start.4 = (f32[256,128]{1,0:T(8,128)S(1)}, f32[256,128]{1,0:T(8,128)S(1)}, u32[]{:S(2)}, u32[]{:S(2)}) collective-permute-start(f32[256,128]{1,0:T(8,128)S(1)} %get-tuple-element.47), channel_id=1, source_target_pairs={{0,4},{4,8},{8,12},{12,16},{16,20},{20,24},{24,28},{28,0},{1,5},{5... | collective-permute-start | bytes 393224 | tf_op jit(solution)/shard_map/ppermute | solution.py:680
  15.3 3.2 %collective-permute-start.5 = (f32[256,128]{1,0:T(8,128)S(1)}, f32[256,128]{1,0:T(8,128)S(1)}, u32[]{:S(2)}, u32[]{:S(2)}) collective-permute-start(f32[256,128]{1,0:T(8,128)S(1)} %get-tuple-element.48), channel_id=1, source_target_pairs={{4,0},{8,4},{12,8},{16,12},{20,16},{24,20},{28,24},{0,28},{5,1},{9... | collective-permute-start | bytes 393224 | tf_op jit(solution)/shard_map/ppermute | solution.py:681
  18.5 3.8 %collective-permute-done.4.west_ref.refs_4_ = f32[256,128]{1,0:T(8,128)S(1)} collective-permute-done((f32[256,128]{1,0:T(8,128)S(1)}, f32[256,128]{1,0:T(8,128)S(1)}, u32[]{:S(2)}, u32[]{:S(2)}) %collective-permute-start.4) | collective-permute-done | bytes 131104 | tf_op jit(solution)/shard_map/ppermute | solution.py:680
  22.3 1.2 %collective-permute-done.5.east_ref.refs_5_ = f32[256,128]{1,0:T(8,128)S(1)} collective-permute-done((f32[256,128]{1,0:T(8,128)S(1)}, f32[256,128]{1,0:T(8,128)S(1)}, u32[]{:S(2)}, u32[]{:S(2)}) %collective-permute-start.5) | collective-permute-done | bytes 131104 | tf_op jit(solution)/shard_map/ppermute | solution.py:681
  23.5 0.1 collective-permute-done.3.refs_2_
  23.6 0.0 collective-permute-done.2.refs_1_
  23.6 0.2 collective-permute-start.6
  23.9 0.3 collective-permute-start.7
  24.2 1.5 %collective-permute-start.8 = (f32[104,128]{1,0:T(8,128)S(1)}, f32[104,128]{1,0:T(8,128)}, u32[]{:S(2)}, u32[]{:S(2)}) collective-permute-start(f32[104,128]{1,0:T(8,128)S(1)} %get-tuple-element.56), channel_id=1, source_target_pairs={{1,0},{2,1},{3,2},{0,3},{5,4},{6,5},{7,6},{4,7},{9,8},{10,9},{11,1... | collective-permute-start | bytes 159752 | tf_op jit(solution)/shard_map/ppermute | solution.py:700
  25.7 0.0 copy-done.4
  25.7 0.1 copy.16.pattern_ref
  25.8 0.0 collective-permute-done.6.refs_3_
  25.8 0.0 copy-done
  25.8 2.5 %meridional.1.refs_11_ = f32[8,96,128]{2,1,0:T(8,128)} custom-call(s32[8,3]{1,0:T(8,128)S(1)} %copy.16.pattern_ref, f32[8,3,128,128]{3,2,1,0:T(8,128)S(1)} %copy-done, f32[3,256,128]{2,1,0:T(8,128)S(1)} %get-tuple-element.46.refs_0_, f32[3,256,128]{2,1,0:T(8,128)S(1)} %collective-permute-done.2.refs_1_, f32[3,256,128]{2,1,0:T(8,128)S(1)} %collective-permute-done.3.refs_2_, ...), custom_call_target="tpu_custom_call" | custom-call | flops 2000000 | bytes 6000000 | tf_op jit(solution)/shard_map/meridional/pallas_call | solution.py:627
  28.3 0.0 collective-permute-done.7.refs_7_
  28.3 0.0 collective-permute-done.8.refs_6_
  28.3 6.4 %all-to-all-start = ((f32[8,96,128]{2,1,0:T(8,128)}), f32[8,96,128]{2,1,0:T(8,128)S(1)}, u32[]{:S(2)}, u32[]{:S(2)}) async-start(f32[8,96,128]{2,1,0:T(8,128)} %meridional.1.refs_11_), calls=%async_computation | async-start | bytes 786432 | tf_op jit(solution)/shard_map/all_to_all | solution.py:703
  34.6 0.0 copy-done.5
  34.6 0.1 copy.17.pattern_ref
  34.7 0.0 copy-start.1
  34.7 9.6 %adjoint.2 = (f32[30,256,128]{2,1,0:T(8,128)}, f32[30,256,128]{2,1,0:T(8,128)}, f32[30,256,128]{2,1,0:T(8,128)}, f32[4,256,128]{2,1,0:T(8,128)S(1)}) custom-call(f32[256,128]{1,0:T(8,128)S(1)} %get-tuple-element.43.refs_0_, f32[256,128]{1,0:T(8,128)S(1)} %get-tuple-element.44.refs_1_, f32[256,128]{1,0:T(8,128)S(1)} %get-tuple-element.45.refs_2_, ...), custom_call_target="tpu_custom_call" | custom-call | flops 9000000 | bytes 27000000 | tf_op jit(solution)/shard_map/adjoint/pallas_call | solution.py:522
  44.3 1.3 %all-to-all-done.field_ref = f32[8,96,128]{2,1,0:T(8,128)S(1)} async-done(((f32[8,96,128]{2,1,0:T(8,128)}), f32[8,96,128]{2,1,0:T(8,128)S(1)}, u32[]{:S(2)}, u32[]{:S(2)}) %all-to-all-start) | async-done | bytes 393248 | tf_op jit(solution)/shard_map/all_to_all | solution.py:703
  45.6 0.0 copy-done.1
  45.6 2.2 %zonal.1.refs_12_ = f32[8,96,128]{2,1,0:T(8,128)} custom-call(s32[8,3]{1,0:T(8,128)S(1)} %copy.17.pattern_ref, f32[8,3,128,128]{3,2,1,0:T(8,128)S(1)} %copy-done.1, f32[8,96,128]{2,1,0:T(8,128)S(1)} %all-to-all-done.field_ref, f32[4,256,128]{2,1,0:T(8,128)S(1)} %get-tuple-element.60.after_ref.refs_8_), custom_call_target="tpu_custom_call" | custom-call | flops 2000000 | bytes 6000000 | tf_op jit(solution)/shard_map/zonal/pallas_call | solution.py:578
  47.9 4.2 %all-to-all-start.1 = ((f32[8,96,128]{2,1,0:T(8,128)}), f32[8,96,128]{2,1,0:T(8,128)S(1)}, u32[]{:S(2)}, u32[]{:S(2)}) async-start(f32[8,96,128]{2,1,0:T(8,128)} %zonal.1.refs_12_), calls=%async_computation.1 | async-start | bytes 786432 | tf_op jit(solution)/shard_map/all_to_all | solution.py:711
  52.1 8.9 %adjoint.3 = (f32[30,256,128]{2,1,0:T(8,128)}, f32[30,256,128]{2,1,0:T(8,128)}, f32[30,256,128]{2,1,0:T(8,128)}, f32[4,256,128]{2,1,0:T(8,128)S(1)}) custom-call(f32[256,128]{1,0:T(8,128)S(1)} %get-tuple-element.43.refs_0_, f32[256,128]{1,0:T(8,128)S(1)} %get-tuple-element.44.refs_1_, ...), custom_call_target="tpu_custom_call", output_to_operand_aliasing={{0}: (13, {}), {1}: (14, {}), {2}: (15, {})} | custom-call | flops 9000000 | bytes 27000000 | tf_op jit(solution)/shard_map/adjoint/pallas_call | solution.py:522
  61.0 1.2 %all-to-all-done.1.field_ref = f32[8,96,128]{2,1,0:T(8,128)S(1)} async-done(((f32[8,96,128]{2,1,0:T(8,128)}), f32[8,96,128]{2,1,0:T(8,128)S(1)}, u32[]{:S(2)}, u32[]{:S(2)}) %all-to-all-start.1) | async-done | bytes 393248 | tf_op jit(solution)/shard_map/all_to_all | solution.py:711
  62.2 0.8 %finish.1 = f32[3,256,128]{2,1,0:T(8,128)} custom-call(f32[8,96,128]{2,1,0:T(8,128)S(1)} %all-to-all-done.1.field_ref, f32[4,256,128]{2,1,0:T(8,128)S(1)} %get-tuple-element.67.after_ref), custom_call_target="tpu_custom_call" | custom-call | flops 700000 | bytes 2100000 | tf_op jit(solution)/shard_map/finish/pallas_call | solution.py:651
  (1 shorter events, 0.0 us)
Async XLA Ops:
  0.6 0.9 %copy-start.2 = (s32[256,128]{1,0:T(8,128)S(1)}, s32[256,128]{1,0:T(8,128)}, u32[]{:S(2)}) copy-start(s32[256,128]{1,0:T(8,128)} %levels_ref.3) | copy-start | bytes 393220
  1.6 9.8 %collective-permute-start = (f32[8,256]{1,0:T(8,128)S(1)}, f32[8,256]{1,0:T(8,128)S(1)}, u32[]{:S(2)}, u32[]{:S(2)}) collective-permute-start(f32[8,256]{1,0:T(8,128)S(1)} %get-tuple-element.36), channel_id=1, source_target_pairs={{0,4},{4,8},{8,12},{12,16},{16,20},{20,24},{24,28},{28,0},{1,5},{5... | collective-permute-start | bytes 24584 | tf_op jit(solution)/shard_map/ppermute | solution.py:674
  4.7 6.8 %copy-start.3 = (s32[256,128]{1,0:T(8,128)S(1)}, s32[256,128]{1,0:T(8,128)}, u32[]{:S(2)}) copy-start(s32[256,128]{1,0:T(8,128)} %levels_ref.3) | copy-start | bytes 393220
  4.7 21.0 %copy-start.4 = (s32[8,3]{0,1:T(4,128)S(1)}, s32[8,3]{0,1:T(4,128)}, u32[]{:S(2)}) copy-start(s32[8,3]{0,1:T(4,128)} %param.16) | copy-start | bytes 292
  4.7 21.1 %copy-start = (f32[8,3,128,128]{3,2,1,0:T(8,128)S(1)}, f32[8,3,128,128]{3,2,1,0:T(8,128)}, u32[]{:S(2)}) copy-start(f32[8,3,128,128]{3,2,1,0:T(8,128)} %blocks_ref.2) | copy-start | bytes 4718596
  4.7 6.7 %collective-permute-start.1 = (f32[8,128]{1,0:T(8,128)S(1)}, f32[8,128]{1,0:T(8,128)S(1)}, u32[]{:S(2)}, u32[]{:S(2)}) collective-permute-start(f32[8,128]{1,0:T(8,128)S(1)} %get-tuple-element.37), channel_id=1, source_target_pairs={{0,1},{1,2},{2,3},{3,0},{4,5},{5,6},{6,7},{7,4},{8,9},{9,10},{10,1... | collective-permute-start | bytes 12296 | tf_op jit(solution)/shard_map/ppermute | solution.py:675
  11.4 23.3 %copy-start.5 = (s32[8,3]{0,1:T(4,128)S(1)}, s32[8,3]{0,1:T(4,128)}, u32[]{:S(2)}) copy-start(s32[8,3]{0,1:T(4,128)} %param.14) | copy-start | bytes 292
  12.0 11.6 %collective-permute-start.3 = (f32[3,256,128]{2,1,0:T(8,128)S(1)}, f32[3,256,128]{2,1,0:T(8,128)S(1)}, u32[]{:S(2)}, u32[]{:S(2)}) collective-permute-start(f32[3,256,128]{2,1,0:T(8,128)S(1)} %get-tuple-element.46.refs_0_), channel_id=1, source_target_pairs={{0,2},{1,3},{2,0},{3,1},{4,6},{5,7},{6,4},{7,5},{8,10},{9,11},{10,... | collective-permute-start | bytes 1179656 | tf_op jit(solution)/shard_map/ppermute | solution.py:686
  13.5 10.1 %collective-permute-start.2 = (f32[3,256,128]{2,1,0:T(8,128)S(1)}, f32[3,256,128]{2,1,0:T(8,128)S(1)}, u32[]{:S(2)}, u32[]{:S(2)}) collective-permute-start(f32[3,256,128]{2,1,0:T(8,128)S(1)} %get-tuple-element.46.refs_0_), channel_id=1, source_target_pairs={{0,1},{1,0},{2,3},{3,2},{4,5},{5,4},{6,7},{7,6},{8,9},{9,8},{10,11... | collective-permute-start | bytes 1179656 | tf_op jit(solution)/shard_map/ppermute | solution.py:686
  13.8 8.5 %collective-permute-start.4 = (f32[256,128]{1,0:T(8,128)S(1)}, f32[256,128]{1,0:T(8,128)S(1)}, u32[]{:S(2)}, u32[]{:S(2)}) collective-permute-start(f32[256,128]{1,0:T(8,128)S(1)} %get-tuple-element.47), channel_id=1, source_target_pairs={{0,4},{4,8},{8,12},{12,16},{16,20},{20,24},{24,28},{28,0},{1,5},{5... | collective-permute-start | bytes 393224 | tf_op jit(solution)/shard_map/ppermute | solution.py:680
  15.3 8.2 %collective-permute-start.5 = (f32[256,128]{1,0:T(8,128)S(1)}, f32[256,128]{1,0:T(8,128)S(1)}, u32[]{:S(2)}, u32[]{:S(2)}) collective-permute-start(f32[256,128]{1,0:T(8,128)S(1)} %get-tuple-element.48), channel_id=1, source_target_pairs={{4,0},{8,4},{12,8},{16,12},{20,16},{24,20},{28,24},{0,28},{5,1},{9... | collective-permute-start | bytes 393224 | tf_op jit(solution)/shard_map/ppermute | solution.py:681
  23.6 2.1 %collective-permute-start.6 = (f32[3,256,128]{2,1,0:T(8,128)S(1)}, f32[3,256,128]{2,1,0:T(8,128)}, u32[]{:S(2)}, u32[]{:S(2)}) collective-permute-start(f32[3,256,128]{2,1,0:T(8,128)S(1)} %collective-permute-done.3.refs_2_), channel_id=1, source_target_pairs={{0,1},{1,0},{2,3},{3,2},{4,5},{5,4},{6,7},{7,6},{8,9},{9,8},{10,11... | collective-permute-start | bytes 1179656 | tf_op jit(solution)/shard_map/ppermute | solution.py:696
  23.9 4.4 %collective-permute-start.7 = (f32[104,128]{1,0:T(8,128)S(1)}, f32[104,128]{1,0:T(8,128)}, u32[]{:S(2)}, u32[]{:S(2)}) collective-permute-start(f32[104,128]{1,0:T(8,128)S(1)} %get-tuple-element.55), channel_id=1, source_target_pairs={{0,1},{1,2},{2,3},{3,0},{4,5},{5,6},{6,7},{7,4},{8,9},{9,10},{10,1... | collective-permute-start | bytes 159752 | tf_op jit(solution)/shard_map/ppermute | solution.py:699
  24.2 4.1 %collective-permute-start.8 = (f32[104,128]{1,0:T(8,128)S(1)}, f32[104,128]{1,0:T(8,128)}, u32[]{:S(2)}, u32[]{:S(2)}) collective-permute-start(f32[104,128]{1,0:T(8,128)S(1)} %get-tuple-element.56), channel_id=1, source_target_pairs={{1,0},{2,1},{3,2},{0,3},{5,4},{6,5},{7,6},{4,7},{9,8},{10,9},{11,1... | collective-permute-start | bytes 159752 | tf_op jit(solution)/shard_map/ppermute | solution.py:700
  28.3 17.4 %all-to-all-start = ((f32[8,96,128]{2,1,0:T(8,128)}), f32[8,96,128]{2,1,0:T(8,128)S(1)}, u32[]{:S(2)}, u32[]{:S(2)}) async-start(f32[8,96,128]{2,1,0:T(8,128)} %meridional.1.refs_11_), calls=%async_computation | async-start | bytes 786432 | tf_op jit(solution)/shard_map/all_to_all | solution.py:703
  34.7 10.9 %copy-start.1 = (f32[8,3,128,128]{3,2,1,0:T(8,128)S(1)}, f32[8,3,128,128]{3,2,1,0:T(8,128)}, u32[]{:S(2)}) copy-start(f32[8,3,128,128]{3,2,1,0:T(8,128)} %blocks_ref.3) | copy-start | bytes 4718596
  47.9 14.3 %all-to-all-start.1 = ((f32[8,96,128]{2,1,0:T(8,128)}), f32[8,96,128]{2,1,0:T(8,128)S(1)}, u32[]{:S(2)}, u32[]{:S(2)}) async-start(f32[8,96,128]{2,1,0:T(8,128)} %zonal.1.refs_12_), calls=%async_computation.1 | async-start | bytes 786432 | tf_op jit(solution)/shard_map/all_to_all | solution.py:711
